TPU v7x, 512 devices: a whole 4x8x8 slice. The times are simulated.
512 devices in a mesh: dir: 16 (over y, z_hi), box: 32 (over x, z_lo, core).
Axes of the slice: x: 4, y: 8, z: 8 (z_hi: 2, z_lo: 4; z = z_hi * 4 + z_lo), core: 2. Of those that a mesh axis runs over, the one named last changes fastest.
Arguments:
- child_fields: bfloat16 [4096, 8, 2, 512], P(('box', 'dir')), may hold values from -6 to 6
- interp_matrix: bfloat16 [512, 2048], replicated, may hold values from -0.25 to 0.25
- phase_angle: float32 [8, 2048], replicated, may hold values from -3.140625 to 3.140625
- patch_order: int32 [32, 128], P('box'), may hold values from 0 to 127, each once within a row
- offset_code: int32 [256, 16, 40], P('box'), may hold values from 0 to 48
- operator_index: int32 [256, 16, 40], P('box'), may hold values from 0 to 127
- operators: bfloat16 [128, 2, 2048], P(None, None, 'dir'), may hold values from -1 to 1
Outputs:
- local_fields: bfloat16 [4096, 8, 2, 512], P(('box', 'dir'))
Inputs may be any that keep to these rules, and one draw needn't show every extreme that they name: `patch_order`: each row holds every number of 0 to 127 once. `offset_code`: entry a names the box offset (a // 7 - 3, a % 7 - 3) on the surface grid, whose two dimensions wrap around.
All inputs are finite; a program needn't handle non-finite values.
Results may differ from a plain program's by a relative error of at most 0.0064.
Values may be sent and summed in bfloat16 or wider, within the bound.
No kernel may reach another device: no remote copies, remote signals or barrier semaphores. Data moves between devices by JAX's collectives and lax.ppermute only.
A program may use at most 64 MiB of HBM per device.

v0:
```python
import jax
import jax.numpy as jnp
from jax import lax
from jax.sharding import Mesh
from jax.sharding import PartitionSpec as P

DC = 512
DP = 2048
CHILDREN = 8
DIR = ("dir_0", "dir_1")
BOX_DIR = ("box", "dir_0", "dir_1")


def split_up(shard, dim, size):
    before, after = (shard.shape[:dim], shard.shape[dim + 1 :])
    return jnp.moveaxis(shard.reshape(*before, size, -1, *after), dim, 0)


def in_order(pieces, dim):
    shape = list(pieces.shape[1:])
    shape[dim] *= pieces.shape[0]
    return jnp.moveaxis(pieces, 0, dim).reshape(shape)


def turned_blocks(pieces, axes, order):
    inside = pieces.shape[1:]
    result = pieces.reshape(*(lax.axis_size(a) for a in axes), *inside)
    for k in order:
        result = lax.all_to_all(result, axes[k], k, k, tiled=True)
    return result.reshape(-1, *inside)


def one_axis_at_a_time(shard, axes, order, split_dim, concat_dim):
    pieces = split_up(shard, split_dim, lax.axis_size(axes))
    return in_order(turned_blocks(pieces, axes, order), concat_dim)


def padded_2(shard, sides, width):
    for axis, dim in sides:
        size, length = (lax.axis_size(axis), shard.shape[dim])
        up = [(i, (i + 1) % size) for i in range(size)]
        down = [(j, i) for i, j in up]
        last = lax.slice_in_dim(shard, length - width, length, axis=dim)
        initial = lax.slice_in_dim(shard, 0, width, axis=dim)
        before = lax.ppermute(last, axis, up)
        after = lax.ppermute(initial, axis, down)
        shard = jnp.concatenate([before, shard, after], axis=dim)
    return shard


def aggregate_rows(fields, interp_columns, cosine_part, sine_part):
    box_count = fields.shape[0]
    band_width = interp_columns.shape[1]
    flat_rows = fields.reshape(box_count * CHILDREN * 2, DC)
    product = jnp.dot(flat_rows, interp_columns, preferred_element_type=jnp.float32).reshape(
        box_count, CHILDREN, 2, band_width
    )
    real_part = jnp.sum(cosine_part * product[:, :, 0] - sine_part * product[:, :, 1], axis=1)
    imaginary_component = jnp.sum(
        cosine_part * product[:, :, 1] + sine_part * product[:, :, 0], axis=1
    )
    return jnp.stack([real_part, imaginary_component], axis=1).astype(jnp.bfloat16)


def wrap_columns(cells):
    return jnp.concatenate([cells[:, -3:], cells, cells[:, :3]], axis=1)


def translate_rows(padded, codes, which_onehot, flattened_operators):
    row_count = codes.shape[0]
    column_total = codes.shape[1]
    band_width = padded.shape[3]
    wrapped = wrap_columns(padded)
    codes_flat = codes.reshape(row_count * column_total, codes.shape[2])
    flattened_selector = which_onehot.reshape(
        row_count * column_total, codes.shape[2], which_onehot.shape[3]
    )
    col_offsets = jnp.arange(7, dtype=jnp.int32)
    real_total = jnp.zeros((row_count, column_total, band_width), jnp.float32)
    imag_total = jnp.zeros((row_count, column_total, band_width), jnp.float32)
    for row_shift in range(7):
        match_flags = (codes_flat[:, :, None] == row_shift * 7 + col_offsets).astype(jnp.bfloat16)
        counts = jnp.einsum(
            "pjf,pje->pfe", match_flags, flattened_selector, preferred_element_type=jnp.float32
        ).astype(jnp.bfloat16)
        real_sum = real_total
        imag_sum = imag_total
        for col_shift in range(7):
            weight_now = jnp.dot(
                counts[:, col_shift], flattened_operators, preferred_element_type=jnp.float32
            )
            weight_now = weight_now.reshape(row_count, column_total, 2, band_width)
            source = wrapped[
                row_shift : row_shift + row_count, col_shift : col_shift + column_total
            ].astype(jnp.float32)
            real_sum = (
                real_sum
                + weight_now[:, :, 0] * source[:, :, 0]
                - weight_now[:, :, 1] * source[:, :, 1]
            )
            imag_sum = (
                imag_sum
                + weight_now[:, :, 0] * source[:, :, 1]
                + weight_now[:, :, 1] * source[:, :, 0]
            )
        real_total = real_sum
        imag_total = imag_sum
    return jnp.stack([real_total, imag_total], axis=2).astype(jnp.bfloat16)


def per_device(
    child_fields, interp_matrix, phase_angle, patch_order, offset_code, operator_index, operators
):
    band_width = operators.shape[2]
    cosine_part = jnp.cos(phase_angle)
    sine_part = jnp.sin(phase_angle)
    parent = aggregate_rows(child_fields, interp_matrix, cosine_part, sine_part)
    listed = one_axis_at_a_time(parent, DIR, (0, 1), 2, 0)
    cell_order = patch_order[0]
    row_count = offset_code.shape[0]
    column_total = offset_code.shape[1]
    patch_cells = listed[cell_order].reshape(row_count, column_total, 2, band_width)
    which_onehot = (
        operator_index[:, :, :, None] == jnp.arange(operators.shape[0], dtype=jnp.int32)
    ).astype(jnp.bfloat16)
    flattened_operators = operators.reshape(operators.shape[0], 2 * band_width)
    padded = padded_2(patch_cells, (("box", 0),), 3)
    translated = translate_rows(padded, offset_code, which_onehot, flattened_operators)
    flat_cells = translated.reshape(row_count * column_total, 2, band_width)
    inverse_permutation = jnp.argsort(cell_order)
    listed_back = flat_cells[inverse_permutation]
    box_count = child_fields.shape[0]
    group_total = 4
    dir_count = lax.axis_size(DIR)
    sectioned = listed_back.reshape(dir_count, group_total, box_count // group_total, 2, band_width)
    ratio = interp_matrix.shape[0] / interp_matrix.shape[1]
    received = lax.all_to_all(sectioned, DIR, split_axis=0, concat_axis=4, tiled=True)
    group_count = received.shape[1]
    group_members = received.shape[2]
    values = received.reshape(group_count * group_members, 2, received.shape[4]).astype(jnp.float32)
    shifted_real = cosine_part * values[:, None, 0] + sine_part * values[:, None, 1]
    shifted_imag = cosine_part * values[:, None, 1] - sine_part * values[:, None, 0]
    shifted = jnp.stack([shifted_real, shifted_imag], axis=2).astype(jnp.bfloat16)
    flat_rows = shifted.reshape(group_count * group_members * CHILDREN * 2, DP)
    result = lax.dot_general(
        flat_rows, interp_matrix, (((1,), (1,)), ((), ())), preferred_element_type=jnp.float32
    )
    gathered = (
        (result * ratio).astype(jnp.bfloat16).reshape(group_count, group_members, CHILDREN, 2, DC)
    )
    return gathered.reshape(box_count, CHILDREN, 2, DC)


def solution(mesh):
    split = Mesh(mesh.devices.reshape(8, 2, mesh.shape["box"]), ("dir_0", "dir_1", "box"))
    placed = (
        P(BOX_DIR, None, None, None),
        P(),
        P(),
        P("box", None),
        P("box", None, None),
        P("box", None, None),
        P(None, None, DIR),
    )
    return jax.shard_map(
        per_device,
        mesh=split,
        in_specs=placed,
        out_specs=P(BOX_DIR, None, None, None),
        check_vma=False,
    )
```

profile of v0, /device:TPU:1, one launch (start us, length us, event | category | flops | bytes accessed | tf_op | source)
XLA Modules:
  0.0 122.7 jit_solution(17544864361483164053)
XLA Ops:
  0.0 1.2 fusion.136
  1.6 1.4 %fusion.7 = f32[8,8,2,2048]{3,1,2,0:T(8,128)S(1)} fusion(bf16[512,2048]{1,0:T(8,128)(2,1)S(1)} %copy-done, bf16[8,8,2,512]{3,2,1,0:T(2,128)(2,1)} %param.7), kind=kOutput, calls=%fused_computation.10 | convolution fusion | flops 268435456 | bytes 3276800 | tf_op jit(solution)/shard_map/dot_general | solution.py:55
  4.2 7.7 %all-to-all-start = ((bf16[8,2,8,2,128]{4,3,2,1,0:T(2,128)(2,1)}), bf16[8,2,8,2,128]{4,3,2,1,0:T(2,128)(2,1)}, u32[]{:S(2)}, u32[]{:S(2)}) async-start(bf16[8,2,8,2,128]{4,3,2,1,0:T(2,128)(2,1)} %copy.62), calls=%async_computation | async-start | bytes 131072 | tf_op jit(solution)/shard_map/all_to_all | solution.py:29
  13.1 1.4 %fusion.16 = bf16[128,7,128]{2,1,0:T(8,128)(2,1)S(1)} fusion(s32[128,40]{1,0:T(8,128)S(1)} %bitcast.430, s32[128,40]{1,0:T(8,128)S(1)} %bitcast.437), kind=kOutput, calls=%fused_computation.19 | convolution fusion | flops 9980928 | bytes 270336 | tf_op jit(solution)/shard_map/pjf,pje->pfe/dot_general | solution.py:83
  14.6 1.4 %fusion.17 = bf16[128,7,128]{2,1,0:T(8,128)(2,1)S(1)} fusion(s32[128,40]{1,0:T(8,128)S(1)} %bitcast.431, s32[128,40]{1,0:T(8,128)S(1)} %bitcast.438, s32[7]{0:T(128)S(1)} %iota_add_fusion.5), kind=kOutput, calls=%fused_computation.20 | convolution fusion | flops 9980928 | bytes 270364 | tf_op jit(solution)/shard_map/pjf,pje->pfe/dot_general | solution.py:83
  17.6 1.4 %fusion.18 = bf16[128,7,128]{2,1,0:T(8,128)(2,1)S(1)} fusion(s32[128,40]{1,0:T(8,128)S(1)} %bitcast.432, s32[128,40]{1,0:T(8,128)S(1)} %bitcast.439, s32[7]{0:T(128)S(1)} %iota_add_fusion.4), kind=kOutput, calls=%fused_computation.21 | convolution fusion | flops 9980928 | bytes 270364 | tf_op jit(solution)/shard_map/pjf,pje->pfe/dot_general | solution.py:83
  23.3 1.4 %fusion.19 = bf16[128,7,128]{2,1,0:T(8,128)(2,1)S(1)} fusion(s32[128,40]{1,0:T(8,128)S(1)} %bitcast.433, s32[128,40]{1,0:T(8,128)S(1)} %bitcast.440, s32[7]{0:T(128)S(1)} %copy-done.49), kind=kOutput, calls=%fused_computation.22 | convolution fusion | flops 9980928 | bytes 270364 | tf_op jit(solution)/shard_map/pjf,pje->pfe/dot_general | solution.py:83
  30.9 1.4 %fusion.20 = bf16[128,7,128]{2,1,0:T(8,128)(2,1)S(1)} fusion(s32[128,40]{1,0:T(8,128)S(1)} %bitcast.434, s32[128,40]{1,0:T(8,128)S(1)} %bitcast.441, s32[7]{0:T(128)S(1)} %copy-done.48), kind=kOutput, calls=%fused_computation.23 | convolution fusion | flops 9980928 | bytes 270364 | tf_op jit(solution)/shard_map/pjf,pje->pfe/dot_general | solution.py:83
  38.5 1.4 %fusion.21 = bf16[128,7,128]{2,1,0:T(8,128)(2,1)S(1)} fusion(s32[128,40]{1,0:T(8,128)S(1)} %bitcast.435, s32[128,40]{1,0:T(8,128)S(1)} %bitcast.442, s32[7]{0:T(128)S(1)} %iota_add_fusion.1), kind=kOutput, calls=%fused_computation.24 | convolution fusion | flops 9980928 | bytes 270364 | tf_op jit(solution)/shard_map/pjf,pje->pfe/dot_general | solution.py:83
  46.1 1.4 %fusion.22 = bf16[128,7,128]{2,1,0:T(8,128)(2,1)S(1)} fusion(s32[128,40]{1,0:T(8,128)S(1)} %bitcast.436, s32[128,40]{1,0:T(8,128)S(1)} %bitcast.443, s32[7]{0:T(128)S(1)} %iota_add_fusion), kind=kOutput, calls=%fused_computation.25 | convolution fusion | flops 9980928 | bytes 270364 | tf_op jit(solution)/shard_map/pjf,pje->pfe/dot_general | solution.py:83
  54.0 0.8 fusion.137
  59.0 0.8 fusion.143
  59.8 2.6 %sort.17 = (s32[128]{0:T(128)}, s32[128]{0:T(128)S(1)}) sort(s32[128]{0:T(128)S(1)} %bitcast.444, s32[128]{0:T(128)S(1)} %iota.42), dimensions={0}, to_apply=%region_2.0 | sort | flops 896 | bytes 2048 | tf_op jit(solution)/shard_map/jit(argsort)/sort | solution.py:130
  62.5 1.5 %copy.63 = bf16[8,2,8,2,128]{4,3,2,0,1:T(2,128)(2,1)} copy(bf16[8,2,8,2,128]{4,3,2,1,0:T(2,128)(2,1)} %all-to-all-done) | data formatting | bytes 131072 | tf_op jit(solution)/shard_map/all_to_all | solution.py:29
  64.0 10.0 %all-to-all-start.1 = ((bf16[8,2,8,2,128]{4,3,2,0,1:T(2,128)(2,1)}), bf16[8,2,8,2,128]{4,3,2,0,1:T(2,128)(2,1)S(1)}, u32[]{:S(2)}, u32[]{:S(2)}) async-start(bf16[8,2,8,2,128]{4,3,2,0,1:T(2,128)(2,1)} %copy.63), calls=%async_computation.1 | async-start | bytes 131072 | tf_op jit(solution)/shard_map/all_to_all | solution.py:29
  74.0 7.2 %all-to-all-done.1 = bf16[8,2,8,2,128]{4,3,2,0,1:T(2,128)(2,1)S(1)} async-done(((bf16[8,2,8,2,128]{4,3,2,0,1:T(2,128)(2,1)}), bf16[8,2,8,2,128]{4,3,2,0,1:T(2,128)(2,1)S(1)}, u32[]{:S(2)}, u32[]{:S(2)}) %all-to-all-start.1) | async-done | bytes 65568 | tf_op jit(solution)/shard_map/all_to_all | solution.py:29
  81.8 1.6 %gather_fusion = bf16[128,2,128]{2,1,0:T(2,128)(2,1)S(1)} fusion(bf16[128,2,128]{2,1,0:T(2,128)(2,1)} %bitcast.370, s32[1024]{0:T(1024)S(1)} %pad_clamp_fusion.1), kind=kCustom, calls=%fused_computation | custom fusion | bytes 131584 | tf_op jit(solution)/shard_map/gather | solution.py:122
  83.5 5.4 %collective-permute-start = (bf16[3,16,2,128]{3,1,2,0:T(8,128)(2,1)S(1)}, bf16[3,16,2,128]{3,1,2,0:T(8,128)(2,1)S(1)}, u32[]{:S(2)}, u32[]{:S(2)}) collective-permute-start(bf16[3,16,2,128]{3,1,2,0:T(8,128)(2,1)S(1)} %copy.66), channel_id=1, source_target_pairs={{0,1},{1,2},{2,3},{3,4},{4,5},{5,6},{6,7},{7,8},{8,9},{9,10},{10,1... | collective-permute-start | bytes 73736 | tf_op jit(solution)/shard_map/ppermute | solution.py:45
  88.9 2.1 %collective-permute-start.1 = (bf16[3,16,2,128]{3,1,2,0:T(8,128)(2,1)S(1)}, bf16[3,16,2,128]{3,1,2,0:T(8,128)(2,1)S(1)}, u32[]{:S(2)}, u32[]{:S(2)}) collective-permute-start(bf16[3,16,2,128]{3,1,2,0:T(8,128)(2,1)S(1)} %copy.69), channel_id=1, source_target_pairs={{1,0},{2,1},{3,2},{4,3},{5,4},{6,5},{7,6},{8,7},{9,8},{10,9},{11,1... | collective-permute-start | bytes 73736 | tf_op jit(solution)/shard_map/ppermute | solution.py:46
  91.1 3.2 %collective-permute-done.1 = bf16[3,16,2,128]{3,1,2,0:T(8,128)(2,1)S(1)} collective-permute-done((bf16[3,16,2,128]{3,1,2,0:T(8,128)(2,1)S(1)}, bf16[3,16,2,128]{3,1,2,0:T(8,128)(2,1)S(1)}, u32[]{:S(2)}, u32[]{:S(2)}) %collective-permute-start.1) | collective-permute-done | bytes 24608 | tf_op jit(solution)/shard_map/ppermute | solution.py:46
  98.1 0.9 add_convert_fusion.1
  100.0 18.5 %all_to_all.19 = bf16[16,4,2,2,128]{4,2,1,3,0:T(2,128)(2,1)S(1)} all-to-all(bf16[16,4,2,2,128]{4,2,1,3,0:T(2,128)(2,1)S(1)} %copy.76), channel_id=1, replica_groups=mesh['dir_0'=8,'dir_1'=2,'box'=32] {'dir_0','dir_1'}, dimensions={0} | all-to-all | bytes 131072 | tf_op jit(solution)/shard_map/all_to_all | solution.py:137
  118.7 1.1 add_convert_fusion
  119.8 1.2 pad_maximum_fusion
  (251 shorter events, 44.4 us)
Async XLA Ops:
  1.6 11.3 %copy-start.47 = (s32[1,128]{1,0:T(1,128)S(1)}, s32[1,128]{1,0:T(1,128)}, u32[]{:S(2)}) copy-start(s32[1,128]{1,0:T(1,128)} %param.10) | copy-start | bytes 1540
  1.6 11.3 %copy-start.42 = (bf16[128,2,128]{2,1,0:T(2,128)(2,1)S(1)}, bf16[128,2,128]{2,1,0:T(2,128)(2,1)}, u32[]{:S(2)}) copy-start(bf16[128,2,128]{2,1,0:T(2,128)(2,1)} %param.13) | copy-start | bytes 196612
  1.6 11.5 %copy-start.43 = (s32[8,16,40]{2,1,0:T(8,128)S(1)}, s32[8,16,40]{2,1,0:T(8,128)}, u32[]{:S(2)}) copy-start(s32[8,16,40]{2,1,0:T(8,128)} %param.12) | copy-start | bytes 61444
  1.6 11.5 %copy-start.45 = (s32[8,16,40]{2,1,0:T(8,128)S(1)}, s32[8,16,40]{2,1,0:T(8,128)}, u32[]{:S(2)}) copy-start(s32[8,16,40]{2,1,0:T(8,128)} %param.11) | copy-start | bytes 61444
  4.2 58.3 %all-to-all-start = ((bf16[8,2,8,2,128]{4,3,2,1,0:T(2,128)(2,1)}), bf16[8,2,8,2,128]{4,3,2,1,0:T(2,128)(2,1)}, u32[]{:S(2)}, u32[]{:S(2)}) async-start(bf16[8,2,8,2,128]{4,3,2,1,0:T(2,128)(2,1)} %copy.62), calls=%async_computation | async-start | bytes 131072 | tf_op jit(solution)/shard_map/all_to_all | solution.py:29
  17.6 5.7 %copy-start.44 = (s32[8,16,40]{2,1,0:T(8,128)S(1)}, s32[8,16,40]{2,1,0:T(8,128)}, u32[]{:S(2)}) copy-start(s32[8,16,40]{2,1,0:T(8,128)} %param.12) | copy-start | bytes 61444
  17.6 5.7 %copy-start.46 = (s32[8,16,40]{2,1,0:T(8,128)S(1)}, s32[8,16,40]{2,1,0:T(8,128)}, u32[]{:S(2)}) copy-start(s32[8,16,40]{2,1,0:T(8,128)} %param.11) | copy-start | bytes 61444
  17.6 5.7 %copy-start.49 = (s32[7]{0:T(128)S(1)}, s32[7]{0:T(128)}, u32[]{:S(2)}) copy-start(s32[7]{0:T(128)} %iota_add_fusion.3) | copy-start | bytes 88
  23.3 7.6 %copy-start.48 = (s32[7]{0:T(128)S(1)}, s32[7]{0:T(128)}, u32[]{:S(2)}) copy-start(s32[7]{0:T(128)} %iota_add_fusion.2) | copy-start | bytes 88
  64.0 17.2 %all-to-all-start.1 = ((bf16[8,2,8,2,128]{4,3,2,0,1:T(2,128)(2,1)}), bf16[8,2,8,2,128]{4,3,2,0,1:T(2,128)(2,1)S(1)}, u32[]{:S(2)}, u32[]{:S(2)}) async-start(bf16[8,2,8,2,128]{4,3,2,0,1:T(2,128)(2,1)} %copy.63), calls=%async_computation.1 | async-start | bytes 131072 | tf_op jit(solution)/shard_map/all_to_all | solution.py:29
  83.5 7.6 %collective-permute-start = (bf16[3,16,2,128]{3,1,2,0:T(8,128)(2,1)S(1)}, bf16[3,16,2,128]{3,1,2,0:T(8,128)(2,1)S(1)}, u32[]{:S(2)}, u32[]{:S(2)}) collective-permute-start(bf16[3,16,2,128]{3,1,2,0:T(8,128)(2,1)S(1)} %copy.66), channel_id=1, source_target_pairs={{0,1},{1,2},{2,3},{3,4},{4,5},{5,6},{6,7},{7,8},{8,9},{9,10},{10,1... | collective-permute-start | bytes 73736 | tf_op jit(solution)/shard_map/ppermute | solution.py:45
  88.9 5.4 %collective-permute-start.1 = (bf16[3,16,2,128]{3,1,2,0:T(8,128)(2,1)S(1)}, bf16[3,16,2,128]{3,1,2,0:T(8,128)(2,1)S(1)}, u32[]{:S(2)}, u32[]{:S(2)}) collective-permute-start(bf16[3,16,2,128]{3,1,2,0:T(8,128)(2,1)S(1)} %copy.69), channel_id=1, source_target_pairs={{1,0},{2,1},{3,2},{4,3},{5,4},{6,5},{7,6},{8,7},{9,8},{10,9},{11,1... | collective-permute-start | bytes 73736 | tf_op jit(solution)/shard_map/ppermute | solution.py:46
  95.2 1.7 %copy-start.17 = (f32[8,16,2,128]{3,1,2,0:T(8,128)S(1)}, f32[8,16,2,128]{3,1,2,0:T(8,128)}, u32[]{:S(2)}) copy-start(f32[8,16,2,128]{3,1,2,0:T(8,128)} %fusion.170) | copy-start | bytes 393220
  95.2 1.7 %copy-start.18 = (f32[8,16,2,128]{3,1,2,0:T(8,128)S(1)}, f32[8,16,2,128]{3,1,2,0:T(8,128)}, u32[]{:S(2)}) copy-start(f32[8,16,2,128]{3,1,2,0:T(8,128)} %fusion.171) | copy-start | bytes 393220
  95.2 1.7 %copy-start.19 = (f32[8,16,2,128]{3,1,2,0:T(8,128)S(1)}, f32[8,16,2,128]{3,1,2,0:T(8,128)}, u32[]{:S(2)}) copy-start(f32[8,16,2,128]{3,1,2,0:T(8,128)} %fusion.172) | copy-start | bytes 393220
  95.2 1.8 %copy-start.20 = (f32[8,16,2,128]{3,1,2,0:T(8,128)S(1)}, f32[8,16,2,128]{3,1,2,0:T(8,128)}, u32[]{:S(2)}) copy-start(f32[8,16,2,128]{3,1,2,0:T(8,128)} %fusion.173) | copy-start | bytes 393220
  95.2 1.8 %copy-start.21 = (f32[8,16,2,128]{3,1,2,0:T(8,128)S(1)}, f32[8,16,2,128]{3,1,2,0:T(8,128)}, u32[]{:S(2)}) copy-start(f32[8,16,2,128]{3,1,2,0:T(8,128)} %fusion.174) | copy-start | bytes 393220
  95.2 1.8 %copy-start.22 = (f32[8,16,2,128]{3,1,2,0:T(8,128)S(1)}, f32[8,16,2,128]{3,1,2,0:T(8,128)}, u32[]{:S(2)}) copy-start(f32[8,16,2,128]{3,1,2,0:T(8,128)} %fusion.175) | copy-start | bytes 393220
  95.2 1.9 %copy-start.23 = (f32[8,16,2,128]{3,1,2,0:T(8,128)S(1)}, f32[8,16,2,128]{3,1,2,0:T(8,128)}, u32[]{:S(2)}) copy-start(f32[8,16,2,128]{3,1,2,0:T(8,128)} %fusion.176) | copy-start | bytes 393220
  95.2 1.9 %copy-start.24 = (f32[8,16,2,128]{3,1,2,0:T(8,128)S(1)}, f32[8,16,2,128]{3,1,2,0:T(8,128)}, u32[]{:S(2)}) copy-start(f32[8,16,2,128]{3,1,2,0:T(8,128)} %fusion.177) | copy-start | bytes 393220
  95.2 1.9 %copy-start.25 = (f32[8,16,2,128]{3,1,2,0:T(8,128)S(1)}, f32[8,16,2,128]{3,1,2,0:T(8,128)}, u32[]{:S(2)}) copy-start(f32[8,16,2,128]{3,1,2,0:T(8,128)} %fusion.178) | copy-start | bytes 393220
  95.3 2.0 %copy-start.26 = (f32[8,16,2,128]{3,1,2,0:T(8,128)S(1)}, f32[8,16,2,128]{3,1,2,0:T(8,128)}, u32[]{:S(2)}) copy-start(f32[8,16,2,128]{3,1,2,0:T(8,128)} %fusion.179) | copy-start | bytes 393220
  95.3 2.0 %copy-start.27 = (f32[8,16,2,128]{3,1,2,0:T(8,128)S(1)}, f32[8,16,2,128]{3,1,2,0:T(8,128)}, u32[]{:S(2)}) copy-start(f32[8,16,2,128]{3,1,2,0:T(8,128)} %fusion.180) | copy-start | bytes 393220
  98.1 20.6 %copy-start.41 = (f32[8,2048]{1,0:T(8,128)S(1)}, f32[8,2048]{1,0:T(8,128)}, u32[]{:S(2)}) copy-start(f32[8,2048]{1,0:T(8,128)} %copy-done.40) | copy-start | bytes 196612
  (30 other events, 38.9 us)
where the time goes:
time: 125 us; the launch traced here: 123 us
  matrix products  45.8 us (37%)
  starting transfers between devices  25.1 us (20%)
  blocking collectives  18.5 us (15%)
  local copies, waits for them, and re-layouts  12.7 us (10%)
  waiting for transfers between devices  10.5 us (8%)
  other arithmetic  9.13 us (7%)
    dot_general x49, matrix products, translate_rows(): jnp.dot(counts[:, col_shift], flattened_operators, preferred_element_type...  33.6 us
    all_to_all x1, blocking collectives, per_device(): lax.all_to_all(sectioned, DIR, split_axis=0, concat_axis=4, tiled=True)  18.5 us
    all_to_all x2, starting transfers between devices, turned_blocks(): result = lax.all_to_all(result, axes[k], k, k, tiled=True)  17.6 us
    dot_general x7, matrix products, translate_rows(): jnp.einsum('pjf,pje->pfe', match_flags, flattened_selector, preferred_ele...  10 us
    all_to_all x2, waiting for transfers between devices, turned_blocks(): result = lax.all_to_all(result, axes[k], k, k, tiled=True)  7.21 us
    ppermute x1, starting transfers between devices, padded_2(): before = lax.ppermute(last, axis, up)  5.39 us
    ppermute x1, waiting for transfers between devices, padded_2(): after = lax.ppermute(initial, axis, down)  3.25 us
    another operation x3, other arithmetic  2.81 us
  transfers between devices with their start and end apart: 4, of which 2 were waited for; matrix products, arithmetic and copies ran while one was open for 41% of the time, Pallas kernels for 0%

commit v1 on v0

v1 whole, which is shorter than its diff:
```python
import jax
import jax.numpy as jnp
from jax import lax
from jax.experimental import pallas as pl
from jax.experimental.pallas import tpu as pltpu
from jax.sharding import Mesh
from jax.sharding import PartitionSpec as P

DC = 512
DP = 2048
CHILDREN = 8
BAND = 128
CELLS = 128
COLS = 16
ENTRIES = 40
HALO = 48
DIR = ("dir_0", "dir_1")
BOX_DIR = ("box", "dir_0", "dir_1")
F32 = jnp.float32
BF16 = jnp.bfloat16
VMEM_LIMIT = 48 * 1024 * 1024


def params():
    return pltpu.CompilerParams(vmem_limit_bytes=VMEM_LIMIT)


def cos_sin(angle):
    half = angle * 0.5
    sq = half * half
    s = F32(1.0 / 6227020800.0)
    for c in (-1.0 / 39916800.0, 1.0 / 362880.0, -1.0 / 5040.0, 1.0 / 120.0, -1.0 / 6.0, 1.0):
        s = s * sq + F32(c)
    s = s * half
    c_ = F32(1.0 / 479001600.0)
    for c in (-1.0 / 3628800.0, 1.0 / 40320.0, -1.0 / 720.0, 1.0 / 24.0, -0.5, 1.0):
        c_ = c_ * sq + F32(c)
    return 1.0 - 2.0 * s * s, 2.0 * s * c_


def aggregate_kernel(child_ref, interp_ref, phase_ref, out_ref):
    c, s = cos_sin(phase_ref[...])
    prod = jnp.dot(child_ref[...], interp_ref[...], preferred_element_type=F32)
    re = jnp.zeros((8, prod.shape[1]), F32)
    im = re
    for k in range(CHILDREN):
        pr, pi = prod[8 * k : 8 * k + 8], prod[64 + 8 * k : 72 + 8 * k]
        ck, sk = c[k : k + 1], s[k : k + 1]
        re = re + (ck * pr - sk * pi)
        im = im + (ck * pi + sk * pr)
    blocks = []
    for d in range(prod.shape[1] // BAND):
        at = slice(d * BAND, (d + 1) * BAND)
        blocks.append(jnp.concatenate([re[:, at], im[:, at]], axis=1))
    out_ref[...] = jnp.concatenate(blocks, axis=0).astype(BF16)


def aggregate(child_rows, interp, phase):
    tile = 512
    return pl.pallas_call(
        aggregate_kernel,
        grid=(DP // tile,),
        in_specs=[
            pl.BlockSpec((128, DC), lambda i: (0, 0)),
            pl.BlockSpec((DC, tile), lambda i: (0, i)),
            pl.BlockSpec((CHILDREN, tile), lambda i: (0, i)),
        ],
        out_specs=pl.BlockSpec((8 * tile // BAND, 2 * BAND), lambda i: (i, 0)),
        out_shape=jax.ShapeDtypeStruct((8 * DP // BAND, 2 * BAND), BF16),
        compiler_params=params(),
        cost_estimate=pl.CostEstimate(flops=2 * 128 * DC * DP, bytes_accessed=DC * DP * 2, transcendentals=0),
    )(child_rows, interp, phase)


def placement(order_row):
    rows = lax.broadcasted_iota(jnp.int32, (CELLS, CELLS), 0)
    return jnp.where(rows == order_row, 1.0, 0.0)


def cells_kernel(listed_ref, order_ref, cells_ref, low_ref, high_ref):
    onehot = placement(order_ref[...]).T.astype(BF16)
    cells = jnp.dot(onehot, listed_ref[...], preferred_element_type=F32).astype(BF16)
    cells_ref[...] = cells
    low_ref[...] = cells[:HALO]
    high_ref[...] = cells[CELLS - HALO :]


def to_cells(listed, order):
    edge = jax.ShapeDtypeStruct((HALO, 2 * BAND), BF16)
    return pl.pallas_call(
        cells_kernel,
        out_shape=(jax.ShapeDtypeStruct((CELLS, 2 * BAND), BF16), edge, edge),
        compiler_params=params(),
    )(listed, order)


def operators_kernel(index_ref, ops_ref, out_ref):
    index = index_ref[...]
    lanes = lax.broadcasted_iota(jnp.int32, (CELLS, BAND), 1)
    ops = ops_ref[...]
    step = 8
    for j0 in range(0, ENTRIES, step):
        picks = [
            jnp.where(index[:, j : j + 1] == lanes, 1.0, 0.0).astype(BF16)
            for j in range(j0, j0 + step)
        ]
        chosen = jnp.dot(jnp.concatenate(picks, axis=0), ops, preferred_element_type=F32)
        out_ref[j0 * CELLS : (j0 + step) * CELLS] = chosen.astype(BF16)


def chosen_operators(index, ops):
    return pl.pallas_call(
        operators_kernel,
        out_shape=jax.ShapeDtypeStruct((ENTRIES * CELLS, 2 * BAND), BF16),
        compiler_params=params(),
        cost_estimate=pl.CostEstimate(
            flops=2 * ENTRIES * CELLS * 128 * 256, bytes_accessed=ENTRIES * CELLS * 512, transcendentals=0
        ),
    )(index, ops)


def translate_kernel(cells_ref, before_ref, after_ref, code_ref, chosen_ref, order_ref, out_ref):
    grid_rows = jnp.concatenate([before_ref[...], cells_ref[...], after_ref[...]], axis=0)
    code = code_ref[...]
    cell = lax.broadcasted_iota(jnp.int32, code.shape, 0)
    up = (code * 37) >> 8
    source = ((cell >> 4) + up) * COLS + (((cell & 15) + code - 7 * up + (COLS - 3)) & 15)
    total_rows = CELLS + 2 * HALO
    lanes = lax.broadcasted_iota(jnp.int32, (CELLS, total_rows), 1)
    re = jnp.zeros((CELLS, BAND), F32)
    im = re
    step = 8
    for j0 in range(0, ENTRIES, step):
        picks = [
            jnp.where(source[:, j : j + 1] == lanes, 1.0, 0.0).astype(BF16)
            for j in range(j0, j0 + step)
        ]
        got = jnp.dot(jnp.concatenate(picks, axis=0), grid_rows, preferred_element_type=F32)
        for k in range(step):
            op = chosen_ref[(j0 + k) * CELLS : (j0 + k + 1) * CELLS].astype(F32)
            g = got[k * CELLS : (k + 1) * CELLS]
            gr, gi, wr, wi = g[:, :BAND], g[:, BAND:], op[:, :BAND], op[:, BAND:]
            re = re + (wr * gr - wi * gi)
            im = im + (wr * gi + wi * gr)
    translated = jnp.concatenate([re, im], axis=1).astype(BF16)
    onehot = placement(order_ref[...]).astype(BF16)
    out_ref[...] = jnp.dot(onehot, translated, preferred_element_type=F32).astype(BF16)


def translate(cells, before, after, code, chosen, order):
    return pl.pallas_call(
        translate_kernel,
        out_shape=jax.ShapeDtypeStruct((CELLS, 2 * BAND), BF16),
        compiler_params=params(),
    )(cells, before, after, code, chosen, order)


def anterpolate_kernel(recv_ref, interp_ref, phase_ref, out_ref, total_ref):
    step = pl.program_id(0)
    c, s = cos_sin(phase_ref[...])
    values = recv_ref[...].astype(F32)
    blocks = values.shape[0] // 8
    re = jnp.concatenate([values[8 * d : 8 * d + 8, :BAND] for d in range(blocks)], axis=1)
    im = jnp.concatenate([values[8 * d : 8 * d + 8, BAND:] for d in range(blocks)], axis=1)
    real, imag = [], []
    for k in range(CHILDREN):
        ck, sk = c[k : k + 1], s[k : k + 1]
        real.append(ck * re + sk * im)
        imag.append(ck * im - sk * re)
    shifted = jnp.concatenate(real + imag, axis=0).astype(BF16)
    part = lax.dot_general(shifted, interp_ref[...], (((1,), (1,)), ((), ())), preferred_element_type=F32)

    @pl.when(step == 0)
    def _():
        total_ref[...] = part

    @pl.when(step > 0)
    def _():
        total_ref[...] += part

    @pl.when(step == pl.num_programs(0) - 1)
    def _():
        out_ref[...] = (total_ref[...] * (DC / DP)).astype(BF16)


def anterpolate(received, interp, phase):
    tile = 512
    return pl.pallas_call(
        anterpolate_kernel,
        grid=(DP // tile,),
        in_specs=[
            pl.BlockSpec((8 * tile // BAND, 2 * BAND), lambda i: (i, 0)),
            pl.BlockSpec((DC, tile), lambda i: (0, i)),
            pl.BlockSpec((CHILDREN, tile), lambda i: (0, i)),
        ],
        out_specs=pl.BlockSpec((128, DC), lambda i: (0, 0)),
        out_shape=jax.ShapeDtypeStruct((128, DC), BF16),
        scratch_shapes=[pltpu.VMEM((128, DC), F32)],
        compiler_params=params(),
    )(received, interp, phase)


def exchange(rows):
    return lax.all_to_all(rows.reshape(16, 8, 2 * BAND), DIR, 0, 0, tiled=True).reshape(CELLS, 2 * BAND)


def per_device(child_fields, interp_matrix, phase_angle, patch_order, offset_code, operator_index, operators):
    child_rows = child_fields.transpose(2, 1, 0, 3).reshape(128, DC)
    parent = aggregate(child_rows, interp_matrix, phase_angle)
    listed = exchange(parent)
    chosen = chosen_operators(operator_index.reshape(CELLS, ENTRIES), operators.reshape(128, 2 * BAND))
    cells, low, high = to_cells(listed, patch_order)
    size = lax.axis_size("box")
    up = [(i, (i + 1) % size) for i in range(size)]
    down = [(j, i) for i, j in up]
    before = lax.ppermute(high, "box", up)
    after = lax.ppermute(low, "box", down)
    returned = translate(cells, before, after, offset_code.reshape(CELLS, ENTRIES), chosen, patch_order)
    received = exchange(returned)
    fields = anterpolate(received, interp_matrix, phase_angle)
    return fields.reshape(2, CHILDREN, 8, DC).transpose(2, 1, 0, 3)


def solution(mesh):
    split = Mesh(mesh.devices.reshape(8, 2, mesh.shape["box"]), ("dir_0", "dir_1", "box"))
    placed = (
        P(BOX_DIR, None, None, None),
        P(),
        P(),
        P("box", None),
        P("box", None, None),
        P("box", None, None),
        P(None, None, DIR),
    )
    return jax.shard_map(
        per_device,
        mesh=split,
        in_specs=placed,
        out_specs=P(BOX_DIR, None, None, None),
        check_vma=False,
    )
```

time: 125 us -> 64.3 us (0.51)
  the two profiles are of different devices: /device:TPU:1 before, /device:TPU:8 now
where the time goes in v1:
time: 64.3 us; the launch traced here: 64 us
  starting transfers between devices  25.5 us (40%)
  blocking collectives  15.6 us (24%)
  waiting for transfers between devices  12 us (19%)
  Pallas kernels  6.58 us (10%)
  local copies, waits for them, and re-layouts  4.27 us (7%)
    all_to_all x1, starting transfers between devices, exchange(): lax.all_to_all(rows.reshape(16, 8, 2 * BAND), DIR, 0, 0, tiled=True)  16 us
    all_to_all x1, blocking collectives, exchange(): lax.all_to_all(rows.reshape(16, 8, 2 * BAND), DIR, 0, 0, tiled=True)  15.6 us
    all_to_all x1, waiting for transfers between devices, exchange(): lax.all_to_all(rows.reshape(16, 8, 2 * BAND), DIR, 0, 0, tiled=True)  11.5 us
    ppermute x1, starting transfers between devices, per_device(): after = lax.ppermute(low, 'box', down)  7.55 us
    unnamed x17, local copies, waits for them, and re-layouts  2.46 us
    pallas_call x1, Pallas kernels, aggregate(): pl.pallas_call(aggregate_kernel, grid=(DP // tile,), in_specs=[pl.BlockSp...  2.13 us
    ppermute x1, starting transfers between devices, per_device(): before = lax.ppermute(high, 'box', up)  1.92 us
    pallas_call x1, Pallas kernels, translate(): pl.pallas_call(translate_kernel, out_shape=jax.ShapeDtypeStruct((CELLS, 2...  1.65 us
  transfers between devices with their start and end apart: 3, of which 2 were waited for; matrix products, arithmetic and copies ran while one was open for 0% of the time, Pallas kernels for 2%

profile of v1, /device:TPU:8, one launch (start us, length us, event | category | flops | bytes accessed | tf_op | source)
XLA Modules:
  0.0 64.0 jit_solution(8648585416083141589)
XLA Ops:
  0.0 1.0 %copy.8 = bf16[2,8,8,512]{3,2,1,0:T(8,128)(2,1)S(1)} copy(bf16[2,8,8,512]{3,0,1,2:T(2,128)(2,1)} %bitcast.24) | data formatting | bytes 262144 | tf_op jit(solution)/shard_map/transpose | solution.py:208
  1.0 0.0 copy-start
  1.0 1.6 %copy-done = bf16[512,2048]{1,0:T(8,128)(2,1)S(1)} copy-done((bf16[512,2048]{1,0:T(8,128)(2,1)S(1)}, bf16[512,2048]{1,0:T(8,128)(2,1)}, u32[]{:S(2)}) %copy-start) | copy-done | bytes 2097176
  2.6 0.8 %copy-done.2 = f32[8,2048]{1,0:T(8,128)S(1)} copy-done((f32[8,2048]{1,0:T(8,128)S(1)}, f32[8,2048]{1,0:T(8,128)}, u32[]{:S(2)}) %copy-start.2) | copy-done | bytes 65560
  3.5 2.1 %shard_map.73 = bf16[128,256]{1,0:T(8,128)(2,1)} custom-call(bf16[128,512]{1,0:T(8,128)(2,1)S(1)} %bitcast.17, bf16[512,2048]{1,0:T(8,128)(2,1)S(1)} %copy-done, f32[8,2048]{1,0:T(8,128)S(1)} %copy-done.2), custom_call_target="tpu_custom_call" | custom-call | flops 268435456 | bytes 2097152 | tf_op jit(solution)/shard_map/pallas_call | solution.py:60
  5.6 16.0 %all-to-all-start = ((bf16[16,8,256]{2,1,0:T(8,128)(2,1)}), bf16[16,8,256]{2,1,0:T(8,128)(2,1)S(1)}, u32[]{:S(2)}, u32[]{:S(2)}) async-start(bf16[16,8,256]{2,1,0:T(8,128)(2,1)} %bitcast.2), calls=%async_computation | async-start | bytes 131072 | tf_op jit(solution)/shard_map/all_to_all | solution.py:204
  21.6 0.0 copy-done.7
  21.6 11.5 %all-to-all-done = bf16[16,8,256]{2,1,0:T(8,128)(2,1)S(1)} async-done(((bf16[16,8,256]{2,1,0:T(8,128)(2,1)}), bf16[16,8,256]{2,1,0:T(8,128)(2,1)S(1)}, u32[]{:S(2)}, u32[]{:S(2)}) %all-to-all-start) | async-done | bytes 65568 | tf_op jit(solution)/shard_map/all_to_all | solution.py:204
  33.2 0.0 copy-done.6
  33.2 0.2 shard_map.74
  33.4 1.9 %collective-permute-start = (bf16[48,256]{1,0:T(8,128)(2,1)S(1)}, bf16[48,256]{1,0:T(8,128)(2,1)S(1)}, u32[]{:S(2)}, u32[]{:S(2)}) collective-permute-start(bf16[48,256]{1,0:T(8,128)(2,1)S(1)} %get-tuple-element.9), channel_id=1, source_target_pairs={{0,1},{1,2},{2,3},{3,4},{4,5},{5,6},{6,7},{7,8},{8,9},{9,10},{10,1... | collective-permute-start | bytes 73736 | tf_op jit(solution)/shard_map/ppermute | solution.py:216
  35.3 7.5 %collective-permute-start.1 = (bf16[48,256]{1,0:T(8,128)(2,1)S(1)}, bf16[48,256]{1,0:T(8,128)(2,1)S(1)}, u32[]{:S(2)}, u32[]{:S(2)}) collective-permute-start(bf16[48,256]{1,0:T(8,128)(2,1)S(1)} %get-tuple-element.10), channel_id=1, source_target_pairs={{1,0},{2,1},{3,2},{4,3},{5,4},{6,5},{7,6},{8,7},{9,8},{10,9},{11,1... | collective-permute-start | bytes 73736 | tf_op jit(solution)/shard_map/ppermute | solution.py:217
  42.9 0.0 copy-done.4
  42.9 0.0 copy-start.1
  42.9 0.0 copy-start.3
  42.9 1.0 %shard_map.75.chosen_ref = bf16[5120,256]{1,0:T(8,128)(2,1)S(1)} custom-call(s32[128,40]{1,0:T(8,128)S(1)} %bitcast.22, bf16[128,256]{1,0:T(8,128)(2,1)S(1)} %bitcast.18), custom_call_target="tpu_custom_call" | custom-call | flops 335544320 | bytes 2621440 | tf_op jit(solution)/shard_map/pallas_call | solution.py:112
  44.0 0.0 collective-permute-done.before_ref
  44.0 0.4 collective-permute-done.1.after_ref
  44.4 0.0 copy-done.5
  44.4 1.7 %shard_map.76 = bf16[128,256]{1,0:T(8,128)(2,1)S(1)} custom-call(bf16[128,256]{1,0:T(8,128)(2,1)S(1)} %get-tuple-element.8.cells_ref, bf16[48,256]{1,0:T(8,128)(2,1)S(1)} %collective-permute-done.before_ref, bf16[48,256]{1,0:T(8,128)(2,1)S(1)} %collective-permute-done.1.after_ref, s32[128,40]{1,0:T(8,128)S(1)} %bitcast.23, ...), custom_call_target="tpu_custom_call" | custom-call | tf_op jit(solution)/shard_map/pallas_call | solution.py:151
  46.0 15.6 %all_to_all.10 = bf16[16,8,256]{2,1,0:T(8,128)(2,1)S(1)} all-to-all(bf16[16,8,256]{2,1,0:T(8,128)(2,1)S(1)} %bitcast.19), channel_id=1, replica_groups=mesh['dir_0'=8,'dir_1'=2,'box'=32] {'dir_0','dir_1'}, dimensions={0} | all-to-all | bytes 131072 | tf_op jit(solution)/shard_map/all_to_all | solution.py:204
  61.6 0.0 copy-done.1
  61.6 1.5 %shard_map.77 = bf16[128,512]{1,0:T(8,128)(2,1)S(1)} custom-call(bf16[128,256]{1,0:T(8,128)(2,1)S(1)} %bitcast.20, bf16[512,2048]{1,0:T(8,128)(2,1)S(1)} %copy-done.1, f32[8,2048]{1,0:T(8,128)S(1)} %copy-done.3), custom_call_target="tpu_custom_call" | custom-call | tf_op jit(solution)/shard_map/pallas_call | solution.py:188
  63.2 0.8 %copy.13 = bf16[2,8,8,512]{3,0,1,2:T(2,128)(2,1)} copy(bf16[2,8,8,512]{3,2,1,0:T(8,128)(2,1)S(1)} %bitcast.16) | data formatting | bytes 262144 | tf_op jit(solution)/shard_map/reshape | solution.py:221
  (7 shorter events, 0.0 us)
Async XLA Ops:
  0.0 21.6 %copy-start.7 = (bf16[128,2,128]{2,1,0:T(2,128)(2,1)S(1)}, bf16[128,2,128]{2,1,0:T(2,128)(2,1)}, u32[]{:S(2)}) copy-start(bf16[128,2,128]{2,1,0:T(2,128)(2,1)} %param.13) | copy-start | bytes 196612
  0.0 33.2 %copy-start.6 = (s32[1,128]{1,0:T(1,128)S(1)}, s32[1,128]{1,0:T(1,128)}, u32[]{:S(2)}) copy-start(s32[1,128]{1,0:T(1,128)} %order_ref.3) | copy-start | bytes 1540
  0.0 42.9 %copy-start.4 = (s32[8,16,40]{2,1,0:T(8,128)S(1)}, s32[8,16,40]{2,1,0:T(8,128)}, u32[]{:S(2)}) copy-start(s32[8,16,40]{2,1,0:T(8,128)} %param.12) | copy-start | bytes 61444
  1.0 1.6 %copy-start = (bf16[512,2048]{1,0:T(8,128)(2,1)S(1)}, bf16[512,2048]{1,0:T(8,128)(2,1)}, u32[]{:S(2)}) copy-start(bf16[512,2048]{1,0:T(8,128)(2,1)} %interp_ref.3) | copy-start | bytes 6291460
  2.6 0.8 %copy-start.2 = (f32[8,2048]{1,0:T(8,128)S(1)}, f32[8,2048]{1,0:T(8,128)}, u32[]{:S(2)}) copy-start(f32[8,2048]{1,0:T(8,128)} %phase_ref.3) | copy-start | bytes 196612
  3.5 40.9 %copy-start.5 = (s32[8,16,40]{2,1,0:T(8,128)S(1)}, s32[8,16,40]{2,1,0:T(8,128)}, u32[]{:S(2)}) copy-start(s32[8,16,40]{2,1,0:T(8,128)} %param.11) | copy-start | bytes 61444
  5.6 27.6 %all-to-all-start = ((bf16[16,8,256]{2,1,0:T(8,128)(2,1)}), bf16[16,8,256]{2,1,0:T(8,128)(2,1)S(1)}, u32[]{:S(2)}, u32[]{:S(2)}) async-start(bf16[16,8,256]{2,1,0:T(8,128)(2,1)} %bitcast.2), calls=%async_computation | async-start | bytes 131072 | tf_op jit(solution)/shard_map/all_to_all | solution.py:204
  33.4 10.6 %collective-permute-start = (bf16[48,256]{1,0:T(8,128)(2,1)S(1)}, bf16[48,256]{1,0:T(8,128)(2,1)S(1)}, u32[]{:S(2)}, u32[]{:S(2)}) collective-permute-start(bf16[48,256]{1,0:T(8,128)(2,1)S(1)} %get-tuple-element.9), channel_id=1, source_target_pairs={{0,1},{1,2},{2,3},{3,4},{4,5},{5,6},{6,7},{7,8},{8,9},{9,10},{10,1... | collective-permute-start | bytes 73736 | tf_op jit(solution)/shard_map/ppermute | solution.py:216
  35.3 9.1 %collective-permute-start.1 = (bf16[48,256]{1,0:T(8,128)(2,1)S(1)}, bf16[48,256]{1,0:T(8,128)(2,1)S(1)}, u32[]{:S(2)}, u32[]{:S(2)}) collective-permute-start(bf16[48,256]{1,0:T(8,128)(2,1)S(1)} %get-tuple-element.10), channel_id=1, source_target_pairs={{1,0},{2,1},{3,2},{4,3},{5,4},{6,5},{7,6},{8,7},{9,8},{10,9},{11,1... | collective-permute-start | bytes 73736 | tf_op jit(solution)/shard_map/ppermute | solution.py:217
  42.9 18.7 %copy-start.1 = (bf16[512,2048]{1,0:T(8,128)(2,1)S(1)}, bf16[512,2048]{1,0:T(8,128)(2,1)}, u32[]{:S(2)}) copy-start(bf16[512,2048]{1,0:T(8,128)(2,1)} %interp_ref.3) | copy-start | bytes 6291460
  42.9 18.7 %copy-start.3 = (f32[8,2048]{1,0:T(8,128)S(1)}, f32[8,2048]{1,0:T(8,128)}, u32[]{:S(2)}) copy-start(f32[8,2048]{1,0:T(8,128)} %phase_ref.3) | copy-start | bytes 196612

commit v2 on v1

v2 whole, which is shorter than its diff:
```python
import jax
import jax.numpy as jnp
from jax import lax
from jax.experimental import pallas as pl
from jax.experimental.pallas import tpu as pltpu
from jax.sharding import Mesh
from jax.sharding import PartitionSpec as P

DC = 512
DP = 2048
CHILDREN = 8
BAND = 128
CELLS = 128
COLS = 16
ENTRIES = 40
DBLOCKS = 16
RUN = 4
DIR = ("dir_0", "dir_1")
F32 = jnp.float32
BF16 = jnp.bfloat16
VMEM_LIMIT = 24 * 1024 * 1024


def params():
    return pltpu.CompilerParams(vmem_limit_bytes=VMEM_LIMIT)


def cos_sin(angle):
    half = angle * 0.5
    sq = half * half
    s = F32(1.0 / 6227020800.0)
    for c in (-1.0 / 39916800.0, 1.0 / 362880.0, -1.0 / 5040.0, 1.0 / 120.0, -1.0 / 6.0, 1.0):
        s = s * sq + F32(c)
    s = s * half
    c_ = F32(1.0 / 479001600.0)
    for c in (-1.0 / 3628800.0, 1.0 / 40320.0, -1.0 / 720.0, 1.0 / 24.0, -0.5, 1.0):
        c_ = c_ * sq + F32(c)
    return 1.0 - 2.0 * s * s, 2.0 * s * c_


def parents(child, interp_ref, phase_ref):
    blocks = []
    tile = 512
    for t in range(DP // tile):
        at = slice(t * tile, (t + 1) * tile)
        c, s = cos_sin(phase_ref[:, at])
        prod = jnp.dot(child, interp_ref[:, at], preferred_element_type=F32)
        re = jnp.zeros((8, tile), F32)
        im = re
        for k in range(CHILDREN):
            pr, pi = prod[8 * k : 8 * k + 8], prod[64 + 8 * k : 72 + 8 * k]
            ck, sk = c[k : k + 1], s[k : k + 1]
            re = re + (ck * pr - sk * pi)
            im = im + (ck * pi + sk * pr)
        for d in range(tile // BAND):
            own = slice(d * BAND, (d + 1) * BAND)
            blocks.append(jnp.concatenate([re[:, own], im[:, own]], axis=1))
    return blocks


def own_kernel(packed_ref, interp_ref, phase_ref, out_ref):
    blocks = parents(packed_ref[:128], interp_ref, phase_ref)
    for d in range(0, DBLOCKS, 2):
        out_ref[8 * d : 8 * d + 16] = jnp.concatenate(blocks[d : d + 2], axis=0).astype(BF16)


def send_kernel(packed_ref, own_ref, order_ref, interp_ref, phase_ref, out_ref):
    core = lax.axis_index("core")
    blocks = parents(packed_ref[:128], interp_ref, phase_ref)
    order = order_ref[...].astype(F32)
    order = jnp.broadcast_to(jnp.concatenate([order, order], axis=1), (8, 2 * BAND))
    own = own_ref[...].astype(F32)
    for d in range(DBLOCKS):
        first = own[8 * d : 8 * d + 8]
        for c in range(2):
            second = jnp.where(core == c, blocks[d], order)
            out_ref[d, c] = jnp.concatenate([first, second], axis=0).astype(BF16)


def whole():
    return pl.BlockSpec(memory_space=pltpu.VMEM)


def own_parents(packed, interp, phase):
    return pl.pallas_call(
        own_kernel,
        in_specs=[whole()] * 3,
        out_specs=whole(),
        out_shape=jax.ShapeDtypeStruct((8 * DBLOCKS, 2 * BAND), BF16),
        compiler_params=params(),
        cost_estimate=pl.CostEstimate(flops=2 * 128 * DC * DP, bytes_accessed=DC * DP * 2, transcendentals=0),
    )(packed, interp, phase)


def to_send(packed, own, order, interp, phase):
    return pl.pallas_call(
        send_kernel,
        in_specs=[whole()] * 5,
        out_specs=whole(),
        out_shape=jax.ShapeDtypeStruct((DBLOCKS, 2, 16, 2 * BAND), BF16),
        compiler_params=params(),
        cost_estimate=pl.CostEstimate(flops=2 * 128 * DC * DP, bytes_accessed=DC * DP * 2, transcendentals=0),
    )(packed, own, order, interp, phase)


def operators_kernel(index_ref, ops_ref, out_ref):
    index = index_ref[...]
    lanes = lax.broadcasted_iota(jnp.int32, (CELLS, BAND), 1)
    ops = ops_ref[...]
    step = 8
    for j0 in range(0, ENTRIES, step):
        picks = [
            jnp.where(index[:, j : j + 1] == lanes, 1.0, 0.0).astype(BF16)
            for j in range(j0, j0 + step)
        ]
        chosen = jnp.dot(jnp.concatenate(picks, axis=0), ops, preferred_element_type=F32)
        out_ref[j0 * CELLS : (j0 + step) * CELLS] = chosen.astype(BF16)


def chosen_operators(index, ops):
    return pl.pallas_call(
        operators_kernel,
        in_specs=[whole()] * 2,
        out_specs=whole(),
        out_shape=jax.ShapeDtypeStruct((ENTRIES * CELLS, 2 * BAND), BF16),
        compiler_params=params(),
        cost_estimate=pl.CostEstimate(
            flops=2 * ENTRIES * CELLS * 128 * 256, bytes_accessed=ENTRIES * CELLS * 512, transcendentals=0
        ),
    )(index, ops)


def translate_kernel(recv_ref, packed_ref, code_ref, chosen_ref, order_ref, out_ref):
    core, chip = lax.axis_index("core"), lax.axis_index("chip")
    flip = jnp.where(core == 0, jnp.where(chip % RUN == 0, 8, 0), jnp.where(chip % RUN == RUN - 1, 8, 0))
    own = order_ref[...]
    mates = [recv_ref[0, c].astype(F32)[8:9, :BAND] for c in range(2)]
    mate = jnp.where(core == 0, mates[1], mates[0]).astype(jnp.int32)
    outside = packed_ref[128:144].astype(F32)[0:1, :BAND].astype(jnp.int32)

    def row_of(position, c, half):
        return (position >> 3) * 32 + c * 16 + half * 8 + (position & 7)

    inside_row = row_of(own, core, 0)
    mate_row = row_of(mate, 1 - core, 0)
    outside_row = row_of(outside ^ flip, core, 1)
    lane = lax.broadcasted_iota(jnp.int32, (1, BAND), 1)
    edge_row = jnp.where((lane < 64) == (core == 0), mate_row, outside_row)
    onehots = []
    for rows in (inside_row, edge_row):
        column = jnp.broadcast_to(rows.astype(F32), (BAND, BAND)).T.astype(jnp.int32)
        parts = [
            jnp.where(column == lax.broadcasted_iota(jnp.int32, (BAND, BAND), 1) + k * BAND, 1.0, 0.0).astype(BF16)
            for k in range(4)
        ]
        onehots.append(jnp.concatenate(parts, axis=1))
    listed = recv_ref[...].reshape(32 * DBLOCKS, 2 * BAND)
    sources = jnp.dot(jnp.concatenate(onehots, axis=0), listed, preferred_element_type=F32).astype(BF16)

    code = code_ref[...]
    cell = lax.broadcasted_iota(jnp.int32, code.shape, 0)
    up = (code * 37) >> 8
    u = (cell >> 4) + up - 3
    v = ((cell & 15) + code - 7 * up + (COLS - 3)) & 15
    source = (u & 7) * COLS + v + jnp.where((u < 0) | (u > 7), CELLS, 0)
    lanes = lax.broadcasted_iota(jnp.int32, (CELLS, 2 * CELLS), 1)
    re = jnp.zeros((CELLS, BAND), F32)
    im = re
    step = 8
    for j0 in range(0, ENTRIES, step):
        picks = [
            jnp.where(source[:, j : j + 1] == lanes, 1.0, 0.0).astype(BF16)
            for j in range(j0, j0 + step)
        ]
        got = jnp.dot(jnp.concatenate(picks, axis=0), sources, preferred_element_type=F32)
        for k in range(step):
            op = chosen_ref[(j0 + k) * CELLS : (j0 + k + 1) * CELLS].astype(F32)
            g = got[k * CELLS : (k + 1) * CELLS]
            gr, gi, wr, wi = g[:, :BAND], g[:, BAND:], op[:, :BAND], op[:, BAND:]
            re = re + (wr * gr - wi * gi)
            im = im + (wr * gi + wi * gr)
    translated = jnp.concatenate([re, im], axis=1).astype(BF16)
    rows = lax.broadcasted_iota(jnp.int32, (CELLS, CELLS), 0)
    onehot = jnp.where(rows == own, 1.0, 0.0).astype(BF16)
    out_ref[...] = jnp.dot(onehot, translated, preferred_element_type=F32).astype(BF16)


def translate(received, packed, code, chosen, order):
    return pl.pallas_call(
        translate_kernel,
        in_specs=[whole()] * 5,
        out_specs=whole(),
        out_shape=jax.ShapeDtypeStruct((CELLS, 2 * BAND), BF16),
        compiler_params=params(),
    )(received, packed, code, chosen, order)


def anterpolate_kernel(recv_ref, interp_ref, phase_ref, out_ref):
    tile = 512
    total = jnp.zeros((128, DC), F32)
    for t in range(DP // tile):
        at = slice(t * tile, (t + 1) * tile)
        c, s = cos_sin(phase_ref[:, at])
        values = recv_ref[8 * tile // BAND * t : 8 * tile // BAND * (t + 1)].astype(F32)
        blocks = values.shape[0] // 8
        re = jnp.concatenate([values[8 * d : 8 * d + 8, :BAND] for d in range(blocks)], axis=1)
        im = jnp.concatenate([values[8 * d : 8 * d + 8, BAND:] for d in range(blocks)], axis=1)
        real, imag = [], []
        for k in range(CHILDREN):
            ck, sk = c[k : k + 1], s[k : k + 1]
            real.append(ck * re + sk * im)
            imag.append(ck * im - sk * re)
        shifted = jnp.concatenate(real + imag, axis=0).astype(BF16)
        total += lax.dot_general(
            shifted, interp_ref[:, at], (((1,), (1,)), ((), ())), preferred_element_type=F32
        )
    out_ref[...] = (total * (DC / DP)).astype(BF16)


def anterpolate(received, interp, phase):
    return pl.pallas_call(
        anterpolate_kernel,
        in_specs=[whole()] * 3,
        out_specs=whole(),
        out_shape=jax.ShapeDtypeStruct((128, DC), BF16),
        compiler_params=params(),
    )(received, interp, phase)


def outside_pairs(halves, chips):
    pairs = []
    for half in range(halves):
        for chip in range(chips):
            there = half ^ 1 if chip % RUN == RUN - 1 else half
            i = (half * chips + chip) * 2 + 1
            j = (there * chips + (chip + 1) % chips) * 2
            pairs += [(i, j), (j, i)]
    return pairs


def per_device(child_fields, interp_matrix, phase_angle, patch_order, offset_code, operator_index, operators):
    child_rows = child_fields.transpose(2, 1, 0, 3).reshape(128, DC)
    order_rows = jnp.pad(patch_order.astype(BF16), ((0, 15), (0, DC - CELLS)))
    packed = jnp.concatenate([child_rows, order_rows], axis=0)
    outside = lax.ppermute(packed, ("dir_1", "chip", "core"), outside_pairs(2, lax.axis_size("chip")))
    own = own_parents(packed, interp_matrix, phase_angle)
    chosen = chosen_operators(operator_index.reshape(CELLS, ENTRIES), operators.reshape(128, 2 * BAND))
    send = to_send(outside, own, patch_order, interp_matrix, phase_angle)
    send, chosen = lax.optimization_barrier((send, chosen))
    listed = lax.all_to_all(send.reshape(2 * DBLOCKS, 16, 2 * BAND), DIR + ("core",), 0, 0, tiled=True)
    returned = translate(
        listed.reshape(DBLOCKS, 2, 16, 2 * BAND), outside, offset_code.reshape(CELLS, ENTRIES), chosen, patch_order
    )
    received = lax.all_to_all(returned.reshape(DBLOCKS, 8, 2 * BAND), DIR, 0, 0, tiled=True)
    fields = anterpolate(received.reshape(8 * DBLOCKS, 2 * BAND), interp_matrix, phase_angle)
    return fields.reshape(2, CHILDREN, 8, DC).transpose(2, 1, 0, 3)


def solution(mesh):
    split = Mesh(mesh.devices.reshape(8, 2, mesh.shape["box"] // 2, 2), ("dir_0", "dir_1", "chip", "core"))
    box = ("chip", "core")
    placed = (
        P(box + DIR, None, None, None),
        P(),
        P(),
        P(box, None),
        P(box, None, None),
        P(box, None, None),
        P(None, None, DIR),
    )
    return jax.shard_map(
        per_device,
        mesh=split,
        in_specs=placed,
        out_specs=P(box + DIR, None, None, None),
        check_vma=False,
    )
```

time: 64.3 us -> 63.2 us (0.983)
  the two profiles are of different devices: /device:TPU:8 before, /device:TPU:1 now
where the time goes in v2:
time: 63.2 us; the launch traced here: 62.8 us
  blocking collectives  46.7 us (74%)
  starting transfers between devices  5.39 us (9%)
  local copies, waits for them, and re-layouts  5.11 us (8%)
  Pallas kernels  4.8 us (8%)
  other arithmetic  0.7 us (1%)
    all_to_all x1, blocking collectives, per_device(): lax.all_to_all(send.reshape(2 * DBLOCKS, 16, 2 * BAND), DIR + ('core',),...  31.7 us
    all_to_all x1, blocking collectives, per_device(): lax.all_to_all(returned.reshape(DBLOCKS, 8, 2 * BAND), DIR, 0, 0, tiled=T...  14.9 us
    ppermute x1, starting transfers between devices, per_device(): lax.ppermute(packed, ('dir_1', 'chip', 'core'), outside_pairs(2, lax.axis...  5.39 us
    unnamed x15, local copies, waits for them, and re-layouts  3.33 us
    pallas_call x1, Pallas kernels, translate(): pl.pallas_call(translate_kernel, in_specs=[whole()] * 5, out_specs=whole(...  1.83 us
  transfers between devices with their start and end apart: 1, of which 0 were waited for; matrix products, arithmetic and copies ran while one was open for 1% of the time, Pallas kernels for 3%

profile of v2, /device:TPU:1, one launch (start us, length us, event | category | flops | bytes accessed | tf_op | source)
XLA Modules:
  0.0 62.8 jit_solution(1967176597970249935)
XLA Ops:
  0.0 0.7 %convert_element_type.5 = bf16[1,128]{1,0:T(2,128)(2,1)S(1)} convert(s32[1,128]{1,0:T(1,128)} %order_ref.3) | non-fusion elementwise | flops 128 | bytes 768 | tf_op jit(solution)/shard_map/convert_element_type | solution.py:243
  0.7 1.0 %copy.8 = bf16[2,8,8,512]{3,2,1,0:T(8,128)(2,1)S(1)} copy(bf16[2,8,8,512]{3,0,1,2:T(2,128)(2,1)} %bitcast.25) | data formatting | bytes 262144 | tf_op jit(solution)/shard_map/transpose | solution.py:242
  1.7 5.4 %collective-permute-start = (bf16[144,512]{1,0:T(8,128)(2,1)S(1)}, bf16[144,512]{1,0:T(8,128)(2,1)S(1)}, u32[]{:S(2)}, u32[]{:S(2)}) collective-permute-start(bf16[144,512]{1,0:T(8,128)(2,1)S(1)} %fusion.1.packed_ref), channel_id=1, source_target_pairs={{1,2},{2,1},{3,4},{4,3},{5,6},{6,5},{7,40},{40,7},{9,10},{10,9},{1... | collective-permute-start | bytes 442376 | tf_op jit(solution)/shard_map/ppermute | solution.py:245
  7.1 0.0 copy-start.3
  7.1 0.0 copy-start.6
  7.1 0.9 %copy.14 = bf16[16,8,2,128]{3,1,2,0:T(8,128)(2,1)S(1)} copy(bf16[16,8,2,128]{3,2,1,0:T(2,128)(2,1)} %bitcast.26) | data formatting | bytes 131072
  8.0 0.0 copy-start
  8.0 1.6 %copy-done = bf16[512,2048]{1,0:T(8,128)(2,1)S(1)} copy-done((bf16[512,2048]{1,0:T(8,128)(2,1)S(1)}, bf16[512,2048]{1,0:T(8,128)(2,1)}, u32[]{:S(2)}) %copy-start) | copy-done | bytes 2097176
  9.6 0.8 %copy-done.2 = f32[8,2048]{1,0:T(8,128)S(1)} copy-done((f32[8,2048]{1,0:T(8,128)S(1)}, f32[8,2048]{1,0:T(8,128)}, u32[]{:S(2)}) %copy-start.2) | copy-done | bytes 65560
  10.4 0.5 shard_map.73.own_ref
  11.0 0.0 copy-done.4
  11.0 0.0 copy-start.5
  11.0 1.0 %shard_map.75.chosen_ref = bf16[5120,256]{1,0:T(8,128)(2,1)S(1)} custom-call(s32[128,40]{1,0:T(8,128)S(1)} %bitcast.22, bf16[128,256]{1,0:T(8,128)(2,1)S(1)} %bitcast.19), custom_call_target="tpu_custom_call" | custom-call | flops 335544320 | bytes 2621440 | tf_op jit(solution)/shard_map/pallas_call | solution.py:121
  12.0 0.0 collective-permute-done.packed_ref
  12.1 0.0 copy-done.3
  12.1 0.0 copy-done.6
  12.1 0.0 copy-done.1
  12.1 0.6 shard_map.74
  12.7 31.7 %all_to_all.10 = bf16[32,16,256]{2,1,0:T(8,128)(2,1)S(1)} all-to-all(bf16[32,16,256]{2,1,0:T(8,128)(2,1)S(1)} %bitcast.16), channel_id=1, replica_groups=mesh['dir_0'=8,'dir_1'=2,'chip'=16,'core'=2] {'dir_0','dir_1','core'}, dimensions={0} | all-to-all | bytes 524288 | tf_op jit(solution)/shard_map/all_to_all | solution.py:250
  44.4 0.0 copy-done.5
  44.4 1.8 %shard_map.76 = bf16[128,256]{1,0:T(8,128)(2,1)S(1)} custom-call(bf16[16,2,16,256]{3,2,1,0:T(8,128)(2,1)S(1)} %bitcast.17, bf16[144,512]{1,0:T(8,128)(2,1)S(1)} %collective-permute-done.packed_ref, s32[128,40]{1,0:T(8,128)S(1)} %bitcast.23, bf16[5120,256]{1,0:T(8,128)(2,1)S(1)} %shard_map.75.chosen_ref, s32[1,128]{1,0:T(1,128)S(1)} %copy-done.6), custom_call_target="tpu_custom_call" | custom-call | tf_op jit(solution)/shard_map/pallas_call | solution.py:189
  46.2 14.9 %all_to_all.11 = bf16[16,8,256]{2,1,0:T(8,128)(2,1)S(1)} all-to-all(bf16[16,8,256]{2,1,0:T(8,128)(2,1)S(1)} %bitcast.21), channel_id=1, replica_groups=mesh['dir_0'=8,'dir_1'=2,'chip'=16,'core'=2] {'dir_0','dir_1'}, dimensions={0} | all-to-all | bytes 131072 | tf_op jit(solution)/shard_map/all_to_all | solution.py:254
  61.2 0.8 %shard_map.77 = bf16[128,512]{1,0:T(8,128)(2,1)S(1)} custom-call(bf16[128,256]{1,0:T(8,128)(2,1)S(1)} %bitcast.20, bf16[512,2048]{1,0:T(8,128)(2,1)S(1)} %copy-done.1, f32[8,2048]{1,0:T(8,128)S(1)} %copy-done.3), custom_call_target="tpu_custom_call" | custom-call | tf_op jit(solution)/shard_map/pallas_call | solution.py:221
  62.0 0.8 %copy.13 = bf16[2,8,8,512]{3,0,1,2:T(2,128)(2,1)} copy(bf16[2,8,8,512]{3,2,1,0:T(8,128)(2,1)S(1)} %bitcast.18) | data formatting | bytes 262144 | tf_op jit(solution)/shard_map/reshape | solution.py:256
  (4 shorter events, 0.0 us)
Async XLA Ops:
  0.0 11.0 %copy-start.4 = (s32[8,16,40]{2,1,0:T(8,128)S(1)}, s32[8,16,40]{2,1,0:T(8,128)}, u32[]{:S(2)}) copy-start(s32[8,16,40]{2,1,0:T(8,128)} %param.12) | copy-start | bytes 61444
  1.7 10.4 %collective-permute-start = (bf16[144,512]{1,0:T(8,128)(2,1)S(1)}, bf16[144,512]{1,0:T(8,128)(2,1)S(1)}, u32[]{:S(2)}, u32[]{:S(2)}) collective-permute-start(bf16[144,512]{1,0:T(8,128)(2,1)S(1)} %fusion.1.packed_ref), channel_id=1, source_target_pairs={{1,2},{2,1},{3,4},{4,3},{5,6},{6,5},{7,40},{40,7},{9,10},{10,9},{1... | collective-permute-start | bytes 442376 | tf_op jit(solution)/shard_map/ppermute | solution.py:245
  7.1 5.0 %copy-start.3 = (f32[8,2048]{1,0:T(8,128)S(1)}, f32[8,2048]{1,0:T(8,128)}, u32[]{:S(2)}) copy-start(f32[8,2048]{1,0:T(8,128)} %phase_ref.5) | copy-start | bytes 196612
  7.1 5.0 %copy-start.6 = (s32[1,128]{1,0:T(1,128)S(1)}, s32[1,128]{1,0:T(1,128)}, u32[]{:S(2)}) copy-start(s32[1,128]{1,0:T(1,128)} %order_ref.3) | copy-start | bytes 1540
  8.0 1.6 %copy-start = (bf16[512,2048]{1,0:T(8,128)(2,1)S(1)}, bf16[512,2048]{1,0:T(8,128)(2,1)}, u32[]{:S(2)}) copy-start(bf16[512,2048]{1,0:T(8,128)(2,1)} %interp_ref.5) | copy-start | bytes 6291460
  9.6 0.8 %copy-start.2 = (f32[8,2048]{1,0:T(8,128)S(1)}, f32[8,2048]{1,0:T(8,128)}, u32[]{:S(2)}) copy-start(f32[8,2048]{1,0:T(8,128)} %phase_ref.5) | copy-start | bytes 196612
  10.4 1.6 %copy-start.1 = (bf16[512,2048]{1,0:T(8,128)(2,1)S(1)}, bf16[512,2048]{1,0:T(8,128)(2,1)}, u32[]{:S(2)}) copy-start(bf16[512,2048]{1,0:T(8,128)(2,1)} %interp_ref.5) | copy-start | bytes 6291460
  11.0 33.4 %copy-start.5 = (s32[8,16,40]{2,1,0:T(8,128)S(1)}, s32[8,16,40]{2,1,0:T(8,128)}, u32[]{:S(2)}) copy-start(s32[8,16,40]{2,1,0:T(8,128)} %param.11) | copy-start | bytes 61444

commit v3 on v2

--- a/solution.py
+++ b/solution.py
@@ -15,6 +15,8 @@
 ENTRIES = 40
 DBLOCKS = 16
 RUN = 4
+TILE = 512
+TILES = DP // TILE
 DIR = ("dir_0", "dir_1")
 F32 = jnp.float32
 BF16 = jnp.bfloat16
@@ -38,72 +40,68 @@
     return 1.0 - 2.0 * s * s, 2.0 * s * c_
 
 
-def parents(child, interp_ref, phase_ref):
-    blocks = []
-    tile = 512
-    for t in range(DP // tile):
-        at = slice(t * tile, (t + 1) * tile)
-        c, s = cos_sin(phase_ref[:, at])
-        prod = jnp.dot(child, interp_ref[:, at], preferred_element_type=F32)
-        re = jnp.zeros((8, tile), F32)
-        im = re
-        for k in range(CHILDREN):
-            pr, pi = prod[8 * k : 8 * k + 8], prod[64 + 8 * k : 72 + 8 * k]
-            ck, sk = c[k : k + 1], s[k : k + 1]
-            re = re + (ck * pr - sk * pi)
-            im = im + (ck * pi + sk * pr)
-        for d in range(tile // BAND):
-            own = slice(d * BAND, (d + 1) * BAND)
-            blocks.append(jnp.concatenate([re[:, own], im[:, own]], axis=1))
-    return blocks
-
-
-def own_kernel(packed_ref, interp_ref, phase_ref, out_ref):
-    blocks = parents(packed_ref[:128], interp_ref, phase_ref)
-    for d in range(0, DBLOCKS, 2):
-        out_ref[8 * d : 8 * d + 16] = jnp.concatenate(blocks[d : d + 2], axis=0).astype(BF16)
-
-
-def send_kernel(packed_ref, own_ref, order_ref, interp_ref, phase_ref, out_ref):
-    core = lax.axis_index("core")
-    blocks = parents(packed_ref[:128], interp_ref, phase_ref)
-    order = order_ref[...].astype(F32)
-    order = jnp.broadcast_to(jnp.concatenate([order, order], axis=1), (8, 2 * BAND))
-    own = own_ref[...].astype(F32)
-    for d in range(DBLOCKS):
-        first = own[8 * d : 8 * d + 8]
-        for c in range(2):
-            second = jnp.where(core == c, blocks[d], order)
-            out_ref[d, c] = jnp.concatenate([first, second], axis=0).astype(BF16)
+def block_fields(child, interp, c, s):
+    prod = jnp.dot(child, interp, preferred_element_type=F32)
+    re = jnp.zeros((8, prod.shape[1]), F32)
+    im = re
+    for k in range(CHILDREN):
+        pr, pi = prod[8 * k : 8 * k + 8], prod[64 + 8 * k : 72 + 8 * k]
+        ck, sk = c[k : k + 1], s[k : k + 1]
+        re = re + (ck * pr - sk * pi)
+        im = im + (ck * pi + sk * pr)
+    columns = [slice(d * BAND, (d + 1) * BAND) for d in range(prod.shape[1] // BAND)]
+    return [jnp.concatenate([re[:, at], im[:, at]], axis=1) for at in columns]
 
 
 def whole():
     return pl.BlockSpec(memory_space=pltpu.VMEM)
 
 
-def own_parents(packed, interp, phase):
-    return pl.pallas_call(
-        own_kernel,
-        in_specs=[whole()] * 3,
+def outer():
+    return pl.BlockSpec(memory_space=pltpu.HBM)
+
+
+def pack_kernel(rows_ref, order_ref, out_ref):
+    out_ref[:128] = rows_ref[...]
+    order = jnp.broadcast_to(order_ref[...].astype(F32), (16, CELLS)).astype(BF16)
+    out_ref[128:144] = jnp.concatenate([order] * (DC // CELLS), axis=1)
+
+
+def pack(rows, order):
+    return pl.pallas_call(
+        pack_kernel,
+        in_specs=[whole()] * 2,
         out_specs=whole(),
-        out_shape=jax.ShapeDtypeStruct((8 * DBLOCKS, 2 * BAND), BF16),
-        compiler_params=params(),
-        cost_estimate=pl.CostEstimate(flops=2 * 128 * DC * DP, bytes_accessed=DC * DP * 2, transcendentals=0),
-    )(packed, interp, phase)
-
-
-def to_send(packed, own, order, interp, phase):
-    return pl.pallas_call(
-        send_kernel,
-        in_specs=[whole()] * 5,
-        out_specs=whole(),
-        out_shape=jax.ShapeDtypeStruct((DBLOCKS, 2, 16, 2 * BAND), BF16),
-        compiler_params=params(),
-        cost_estimate=pl.CostEstimate(flops=2 * 128 * DC * DP, bytes_accessed=DC * DP * 2, transcendentals=0),
-    )(packed, own, order, interp, phase)
-
-
-def operators_kernel(index_ref, ops_ref, out_ref):
+        out_shape=jax.ShapeDtypeStruct((144, DC), BF16),
+        compiler_params=params(),
+    )(rows, order)
+
+
+def front_kernel(
+    packed_ref,
+    ops_ref,
+    index_hbm,
+    interp_hbm,
+    phase_hbm,
+    own_ref,
+    chosen_ref,
+    interp_ref,
+    cos_ref,
+    sin_ref,
+    index_ref,
+    phase_ref,
+    sems,
+):
+    load_index = pltpu.make_async_copy(index_hbm, index_ref, sems.at[TILES + 1])
+    load_index.start()
+    load_phase = pltpu.make_async_copy(phase_hbm, phase_ref, sems.at[TILES])
+    load_phase.start()
+    loads = []
+    for t in range(TILES):
+        at = pl.ds(t * TILE, TILE)
+        loads.append(pltpu.make_async_copy(interp_hbm.at[:, at], interp_ref.at[:, at], sems.at[t]))
+        loads[t].start()
+    load_index.wait()
     index = index_ref[...]
     lanes = lax.broadcasted_iota(jnp.int32, (CELLS, BAND), 1)
     ops = ops_ref[...]
@@ -114,20 +112,70 @@
             for j in range(j0, j0 + step)
         ]
         chosen = jnp.dot(jnp.concatenate(picks, axis=0), ops, preferred_element_type=F32)
-        out_ref[j0 * CELLS : (j0 + step) * CELLS] = chosen.astype(BF16)
-
-
-def chosen_operators(index, ops):
-    return pl.pallas_call(
-        operators_kernel,
-        in_specs=[whole()] * 2,
+        chosen_ref[j0 * CELLS : (j0 + step) * CELLS] = chosen.astype(BF16)
+    load_phase.wait()
+    c, s = cos_sin(phase_ref[...])
+    cos_ref[...] = c
+    sin_ref[...] = s
+    child = packed_ref[:128]
+    for t in range(TILES):
+        at = slice(t * TILE, (t + 1) * TILE)
+        loads[t].wait()
+        blocks = block_fields(child, interp_ref[:, at], c[:, at], s[:, at])
+        rows = 8 * len(blocks)
+        own_ref[t * rows : (t + 1) * rows] = jnp.concatenate(blocks, axis=0).astype(BF16)
+
+
+def front(packed, ops, *outside):
+    outside = [pltpu.with_memory_space_constraint(x, pltpu.HBM) for x in outside]
+    wave = jax.ShapeDtypeStruct((CHILDREN, DP), F32)
+    return pl.pallas_call(
+        front_kernel,
+        in_specs=[whole()] * 2 + [outer()] * 3,
+        out_specs=[whole()] * 5,
+        out_shape=(
+            jax.ShapeDtypeStruct((8 * DBLOCKS, 2 * BAND), BF16),
+            jax.ShapeDtypeStruct((ENTRIES * CELLS, 2 * BAND), BF16),
+            jax.ShapeDtypeStruct((DC, DP), BF16),
+            wave,
+            wave,
+        ),
+        scratch_shapes=[
+            pltpu.VMEM((CELLS, ENTRIES), jnp.int32),
+            pltpu.VMEM((CHILDREN, DP), F32),
+            pltpu.SemaphoreType.DMA((TILES + 2,)),
+        ],
+        compiler_params=params(),
+        cost_estimate=pl.CostEstimate(flops=4 * 128 * DC * DP, bytes_accessed=DC * DP * 2, transcendentals=0),
+    )(packed, ops, *outside)
+
+
+def send_kernel(packed_ref, own_ref, order_ref, interp_ref, cos_ref, sin_ref, out_ref):
+    core = lax.axis_index("core")
+    order = order_ref[...].astype(F32)
+    order = jnp.broadcast_to(jnp.concatenate([order, order], axis=1), (8, 2 * BAND))
+    own = own_ref[...].astype(F32)
+    child = packed_ref[:128]
+    for t in range(TILES):
+        at = slice(t * TILE, (t + 1) * TILE)
+        blocks = block_fields(child, interp_ref[:, at], cos_ref[:, at], sin_ref[:, at])
+        for k, block in enumerate(blocks):
+            d = t * len(blocks) + k
+            first = own[8 * d : 8 * d + 8]
+            for c in range(2):
+                second = jnp.where(core == c, block, order)
+                out_ref[d, c] = jnp.concatenate([first, second], axis=0).astype(BF16)
+
+
+def to_send(packed, own, order, interp, c, s):
+    return pl.pallas_call(
+        send_kernel,
+        in_specs=[whole()] * 6,
         out_specs=whole(),
-        out_shape=jax.ShapeDtypeStruct((ENTRIES * CELLS, 2 * BAND), BF16),
-        compiler_params=params(),
-        cost_estimate=pl.CostEstimate(
-            flops=2 * ENTRIES * CELLS * 128 * 256, bytes_accessed=ENTRIES * CELLS * 512, transcendentals=0
-        ),
-    )(index, ops)
+        out_shape=jax.ShapeDtypeStruct((DBLOCKS, 2, 16, 2 * BAND), BF16),
+        compiler_params=params(),
+        cost_estimate=pl.CostEstimate(flops=2 * 128 * DC * DP, bytes_accessed=DC * DP * 2, transcendentals=0),
+    )(packed, own, order, interp, c, s)
 
 
 def translate_kernel(recv_ref, packed_ref, code_ref, chosen_ref, order_ref, out_ref):
@@ -195,14 +243,14 @@
     )(received, packed, code, chosen, order)
 
 
-def anterpolate_kernel(recv_ref, interp_ref, phase_ref, out_ref):
-    tile = 512
+def anterpolate_kernel(recv_ref, interp_ref, cos_ref, sin_ref, out_ref):
     total = jnp.zeros((128, DC), F32)
-    for t in range(DP // tile):
-        at = slice(t * tile, (t + 1) * tile)
-        c, s = cos_sin(phase_ref[:, at])
-        values = recv_ref[8 * tile // BAND * t : 8 * tile // BAND * (t + 1)].astype(F32)
-        blocks = values.shape[0] // 8
+    rows = 8 * TILE // BAND
+    for t in range(TILES):
+        at = slice(t * TILE, (t + 1) * TILE)
+        c, s = cos_ref[:, at], sin_ref[:, at]
+        values = recv_ref[rows * t : rows * (t + 1)].astype(F32)
+        blocks = rows // 8
         re = jnp.concatenate([values[8 * d : 8 * d + 8, :BAND] for d in range(blocks)], axis=1)
         im = jnp.concatenate([values[8 * d : 8 * d + 8, BAND:] for d in range(blocks)], axis=1)
         real, imag = [], []
@@ -217,14 +265,14 @@
     out_ref[...] = (total * (DC / DP)).astype(BF16)
 
 
-def anterpolate(received, interp, phase):
+def anterpolate(received, interp, c, s):
     return pl.pallas_call(
         anterpolate_kernel,
-        in_specs=[whole()] * 3,
+        in_specs=[whole()] * 4,
         out_specs=whole(),
         out_shape=jax.ShapeDtypeStruct((128, DC), BF16),
         compiler_params=params(),
-    )(received, interp, phase)
+    )(received, interp, c, s)
 
 
 def outside_pairs(halves, chips):
@@ -240,19 +288,22 @@
 
 def per_device(child_fields, interp_matrix, phase_angle, patch_order, offset_code, operator_index, operators):
     child_rows = child_fields.transpose(2, 1, 0, 3).reshape(128, DC)
-    order_rows = jnp.pad(patch_order.astype(BF16), ((0, 15), (0, DC - CELLS)))
-    packed = jnp.concatenate([child_rows, order_rows], axis=0)
+    packed = pack(child_rows, patch_order)
     outside = lax.ppermute(packed, ("dir_1", "chip", "core"), outside_pairs(2, lax.axis_size("chip")))
-    own = own_parents(packed, interp_matrix, phase_angle)
-    chosen = chosen_operators(operator_index.reshape(CELLS, ENTRIES), operators.reshape(128, 2 * BAND))
-    send = to_send(outside, own, patch_order, interp_matrix, phase_angle)
-    send, chosen = lax.optimization_barrier((send, chosen))
+    own, chosen, interp, c, s = front(
+        packed,
+        operators.reshape(128, 2 * BAND),
+        operator_index.reshape(CELLS, ENTRIES),
+        interp_matrix,
+        phase_angle,
+    )
+    send = to_send(outside, own, patch_order, interp, c, s)
     listed = lax.all_to_all(send.reshape(2 * DBLOCKS, 16, 2 * BAND), DIR + ("core",), 0, 0, tiled=True)
     returned = translate(
         listed.reshape(DBLOCKS, 2, 16, 2 * BAND), outside, offset_code.reshape(CELLS, ENTRIES), chosen, patch_order
     )
     received = lax.all_to_all(returned.reshape(DBLOCKS, 8, 2 * BAND), DIR, 0, 0, tiled=True)
-    fields = anterpolate(received.reshape(8 * DBLOCKS, 2 * BAND), interp_matrix, phase_angle)
+    fields = anterpolate(received.reshape(8 * DBLOCKS, 2 * BAND), interp, c, s)
     return fields.reshape(2, CHILDREN, 8, DC).transpose(2, 1, 0, 3)
 
 

time: 63.2 us -> 63 us (level)
  local copies, waits for them, and re-layouts: 5.11 us -> 3.3 us
  Pallas kernels: 4.8 us -> 6.31 us
  blocking collectives: 46.7 us -> 47.6 us
  other arithmetic: 0.7 us -> 0 us
    unnamed x15 -> x7, local copies, waits for them, and re-layouts: 3.33 us -> 1.51 us
    pallas_call x4, Pallas kernels: 2.97 us -> 4.55 us  [the longest x1 3.14 us: front(): pl.pallas_call(front_kernel, in_specs=[whole()] * 2 + [outer()] * 3, out_...]
    all_to_all x1, blocking collectives: 31.7 us -> 32.7 us  [per_device(): lax.all_to_all(send.reshape(2 * DBLOCKS, 16, 2 * BAND), DIR + ('core',),...]
    convert_element_type x1 -> x0, other arithmetic: 0.69 us -> none  [per_device(): order_rows = jnp.pad(patch_order.astype(BF16), ((0, 15), (0, DC - CELLS)))]
  transfers between devices with their start and end apart: 1 -> 1, of which waited for: 0 -> 0; matrix products, arithmetic and copies ran while one was open for 1% -> 1% of each run, Pallas kernels for 3% -> 5%
where the time goes in v3:
time: 63 us; the launch traced here: 62.7 us
  blocking collectives  47.6 us (76%)
  Pallas kernels  6.31 us (10%)
  starting transfers between devices  5.39 us (9%)
  local copies, waits for them, and re-layouts  3.3 us (5%)
    all_to_all x1, blocking collectives, per_device(): lax.all_to_all(send.reshape(2 * DBLOCKS, 16, 2 * BAND), DIR + ('core',),...  32.7 us
    all_to_all x1, blocking collectives, per_device(): lax.all_to_all(returned.reshape(DBLOCKS, 8, 2 * BAND), DIR, 0, 0, tiled=T...  14.9 us
    ppermute x1, starting transfers between devices, per_device(): lax.ppermute(packed, ('dir_1', 'chip', 'core'), outside_pairs(2, lax.axis...  5.39 us
    pallas_call x1, Pallas kernels, front(): pl.pallas_call(front_kernel, in_specs=[whole()] * 2 + [outer()] * 3, out_...  3.14 us
    pallas_call x1, Pallas kernels, translate(): pl.pallas_call(translate_kernel, in_specs=[whole()] * 5, out_specs=whole(...  1.77 us
    unnamed x7, local copies, waits for them, and re-layouts  1.51 us
  transfers between devices with their start and end apart: 1, of which 0 were waited for; matrix products, arithmetic and copies ran while one was open for 1% of the time, Pallas kernels for 5%

profile of v3, /device:TPU:1, one launch (start us, length us, event | category | flops | bytes accessed | tf_op | source)
XLA Modules:
  0.0 62.7 jit_solution(13798782179096789022)
XLA Ops:
  0.0 0.0 copy-start.2
  0.0 1.0 %copy.8 = bf16[2,8,8,512]{3,2,1,0:T(8,128)(2,1)S(1)} copy(bf16[2,8,8,512]{3,0,1,2:T(2,128)(2,1)} %bitcast.24) | data formatting | bytes 262144 | tf_op jit(solution)/shard_map/transpose | solution.py:290
  1.0 0.0 copy-start.1
  1.0 0.6 %copy-done.1 = s32[1,128]{1,0:T(1,128)S(1)} copy-done((s32[1,128]{1,0:T(1,128)S(1)}, s32[1,128]{1,0:T(1,128)}, u32[]{:S(2)}) %copy-start.1) | copy-done | bytes 536
  1.7 5.4 %collective-permute-start = (bf16[144,512]{1,0:T(8,128)(2,1)S(1)}, bf16[144,512]{1,0:T(8,128)(2,1)S(1)}, u32[]{:S(2)}, u32[]{:S(2)}) collective-permute-start(bf16[144,512]{1,0:T(8,128)(2,1)S(1)} %shard_map.73.packed_ref), channel_id=1, source_target_pairs={{1,2},{2,1},{3,4},{4,3},{5,6},{6,5},{7,40},{40,7},{9,10},{10,9},{1... | collective-permute-start | bytes 442376 | tf_op jit(solution)/shard_map/ppermute | solution.py:292
  7.1 0.9 %copy.14 = bf16[16,8,2,128]{3,1,2,0:T(8,128)(2,1)S(1)} copy(bf16[16,8,2,128]{3,2,1,0:T(2,128)(2,1)} %bitcast.26) | data formatting | bytes 131072
  7.9 3.1 %shard_map.74 = (bf16[128,256]{1,0:T(8,128)(2,1)S(1)}, bf16[5120,256]{1,0:T(8,128)(2,1)S(1)}, bf16[512,2048]{1,0:T(8,128)(2,1)S(1)}, f32[8,2048]{1,0:T(8,128)S(1)}, f32[8,2048]{1,0:T(8,128)S(1)}) custom-call(bf16[144,512]{1,0:T(8,128)(2,1)S(1)} %shard_map.73.packed_ref, bf16[128,256]{1,0:T(8,128)(2,1)S(1)} %bitcast.20, s32[128,40]{1,0:T(8,128)} %bitcast.25, ...), custom_call_target="tpu_custom_call" | custom-call | flops 536870912 | bytes 2097152 | tf_op jit(solution)/shard_map/pallas_call | solution.py:132
  11.1 0.0 copy-start
  11.1 0.0 collective-permute-done.packed_ref
  11.1 0.0 copy-done.2
  11.1 0.6 shard_map.75
  11.7 32.7 %all_to_all.10 = bf16[32,16,256]{2,1,0:T(8,128)(2,1)S(1)} all-to-all(bf16[32,16,256]{2,1,0:T(8,128)(2,1)S(1)} %bitcast.16), channel_id=1, replica_groups=mesh['dir_0'=8,'dir_1'=2,'chip'=16,'core'=2] {'dir_0','dir_1','core'}, dimensions={0} | all-to-all | bytes 524288 | tf_op jit(solution)/shard_map/all_to_all | solution.py:301
  44.4 0.0 copy-done
  44.4 1.8 %shard_map.76 = bf16[128,256]{1,0:T(8,128)(2,1)S(1)} custom-call(bf16[16,2,16,256]{3,2,1,0:T(8,128)(2,1)S(1)} %bitcast.17, bf16[144,512]{1,0:T(8,128)(2,1)S(1)} %collective-permute-done.packed_ref, s32[128,40]{1,0:T(8,128)S(1)} %bitcast.23, bf16[5120,256]{1,0:T(8,128)(2,1)S(1)} %get-tuple-element.14.chosen_ref, s32[1,128]{1,0:T(1,128)S(1)} %copy-done.2), custom_call_target="tpu_custom_call" | custom-call | tf_op jit(solution)/shard_map/pallas_call | solution.py:237
  46.1 14.9 %all_to_all.11 = bf16[16,8,256]{2,1,0:T(8,128)(2,1)S(1)} all-to-all(bf16[16,8,256]{2,1,0:T(8,128)(2,1)S(1)} %bitcast.22), channel_id=1, replica_groups=mesh['dir_0'=8,'dir_1'=2,'chip'=16,'core'=2] {'dir_0','dir_1'}, dimensions={0} | all-to-all | bytes 131072 | tf_op jit(solution)/shard_map/all_to_all | solution.py:305
  61.1 0.8 %shard_map.77 = bf16[128,512]{1,0:T(8,128)(2,1)S(1)} custom-call(bf16[128,256]{1,0:T(8,128)(2,1)S(1)} %bitcast.21, bf16[512,2048]{1,0:T(8,128)(2,1)S(1)} %get-tuple-element.11.interp_ref, f32[8,2048]{1,0:T(8,128)S(1)} %get-tuple-element.12.cos_ref, f32[8,2048]{1,0:T(8,128)S(1)} %get-tuple-element.13.sin_ref), custom_call_target="tpu_custom_call" | custom-call | tf_op jit(solution)/shard_map/pallas_call | solution.py:269
  61.9 0.8 %copy.13 = bf16[2,8,8,512]{3,0,1,2:T(2,128)(2,1)} copy(bf16[2,8,8,512]{3,2,1,0:T(8,128)(2,1)S(1)} %bitcast.18) | data formatting | bytes 262144 | tf_op jit(solution)/shard_map/reshape | solution.py:307
  (1 shorter events, 0.0 us)
Async XLA Ops:
  0.0 11.1 %copy-start.2 = (s32[1,128]{1,0:T(1,128)S(1)}, s32[1,128]{1,0:T(1,128)}, u32[]{:S(2)}) copy-start(s32[1,128]{1,0:T(1,128)} %order_ref.5) | copy-start | bytes 1540
  1.0 0.7 %copy-start.1 = (s32[1,128]{1,0:T(1,128)S(1)}, s32[1,128]{1,0:T(1,128)}, u32[]{:S(2)}) copy-start(s32[1,128]{1,0:T(1,128)} %order_ref.5) | copy-start | bytes 1540
  1.7 9.4 %collective-permute-start = (bf16[144,512]{1,0:T(8,128)(2,1)S(1)}, bf16[144,512]{1,0:T(8,128)(2,1)S(1)}, u32[]{:S(2)}, u32[]{:S(2)}) collective-permute-start(bf16[144,512]{1,0:T(8,128)(2,1)S(1)} %shard_map.73.packed_ref), channel_id=1, source_target_pairs={{1,2},{2,1},{3,4},{4,3},{5,6},{6,5},{7,40},{40,7},{9,10},{10,9},{1... | collective-permute-start | bytes 442376 | tf_op jit(solution)/shard_map/ppermute | solution.py:292
  11.1 33.3 %copy-start = (s32[8,16,40]{2,1,0:T(8,128)S(1)}, s32[8,16,40]{2,1,0:T(8,128)}, u32[]{:S(2)}) copy-start(s32[8,16,40]{2,1,0:T(8,128)} %param.11) | copy-start | bytes 61444

commit v4 on v3

--- a/solution.py
+++ b/solution.py
@@ -53,6 +53,22 @@
     return [jnp.concatenate([re[:, at], im[:, at]], axis=1) for at in columns]
 
 
+def by_part(rows):
+    there = lax.broadcasted_iota(jnp.int32, (128, 128), 0)
+    here = lax.broadcasted_iota(jnp.int32, (128, 128), 1)
+    wanted = (there & 7) * 16 + ((there >> 3) & 7) * 2 + (there >> 6)
+    pick = jnp.where(here == wanted, 1.0, 0.0).astype(BF16)
+    return jnp.dot(pick, rows, preferred_element_type=F32).astype(BF16)
+
+
+def by_box(rows):
+    there = lax.broadcasted_iota(jnp.int32, (128, 128), 0)
+    here = lax.broadcasted_iota(jnp.int32, (128, 128), 1)
+    wanted = (there & 1) * 64 + ((there >> 1) & 7) * 8 + (there >> 4)
+    pick = jnp.where(here == wanted, 1.0, 0.0).astype(BF16)
+    return jnp.dot(pick, rows, preferred_element_type=F32).astype(BF16)
+
+
 def whole():
     return pl.BlockSpec(memory_space=pltpu.VMEM)
 
@@ -61,50 +77,69 @@
     return pl.BlockSpec(memory_space=pltpu.HBM)
 
 
-def pack_kernel(rows_ref, order_ref, out_ref):
-    out_ref[:128] = rows_ref[...]
+def pack_kernel(child_hbm, order_hbm, packed_ref, child_ref, order_ref, sems):
+    loads = [
+        pltpu.make_async_copy(child_hbm, child_ref, sems.at[0]),
+        pltpu.make_async_copy(order_hbm, order_ref, sems.at[1]),
+    ]
+    for load in loads:
+        load.start()
+    loads[1].wait()
     order = jnp.broadcast_to(order_ref[...].astype(F32), (16, CELLS)).astype(BF16)
-    out_ref[128:144] = jnp.concatenate([order] * (DC // CELLS), axis=1)
-
-
-def pack(rows, order):
+    packed_ref[128:144] = jnp.concatenate([order] * (DC // CELLS), axis=1)
+    loads[0].wait()
+    packed_ref[:128] = child_ref[...].reshape(128, DC)
+
+
+def in_hbm(*args):
+    return [pltpu.with_memory_space_constraint(x, pltpu.HBM) for x in args]
+
+
+def pack(child, order):
     return pl.pallas_call(
         pack_kernel,
-        in_specs=[whole()] * 2,
+        in_specs=[outer()] * 2,
         out_specs=whole(),
         out_shape=jax.ShapeDtypeStruct((144, DC), BF16),
-        compiler_params=params(),
-    )(rows, order)
+        scratch_shapes=[
+            pltpu.VMEM((64, 2, DC), BF16),
+            pltpu.VMEM((1, CELLS), jnp.int32),
+            pltpu.SemaphoreType.DMA((2,)),
+        ],
+        compiler_params=params(),
+    )(*in_hbm(child, order))
 
 
 def front_kernel(
     packed_ref,
-    ops_ref,
+    ops_hbm,
     index_hbm,
+    phase_hbm,
     interp_hbm,
-    phase_hbm,
     own_ref,
     chosen_ref,
     interp_ref,
     cos_ref,
     sin_ref,
+    ops_ref,
     index_ref,
     phase_ref,
     sems,
 ):
-    load_index = pltpu.make_async_copy(index_hbm, index_ref, sems.at[TILES + 1])
-    load_index.start()
-    load_phase = pltpu.make_async_copy(phase_hbm, phase_ref, sems.at[TILES])
-    load_phase.start()
-    loads = []
+    small = [(ops_hbm, ops_ref), (index_hbm, index_ref), (phase_hbm, phase_ref)]
+    loads = [pltpu.make_async_copy(there, here, sems.at[k]) for k, (there, here) in enumerate(small)]
     for t in range(TILES):
         at = pl.ds(t * TILE, TILE)
-        loads.append(pltpu.make_async_copy(interp_hbm.at[:, at], interp_ref.at[:, at], sems.at[t]))
-        loads[t].start()
-    load_index.wait()
+        loads.append(pltpu.make_async_copy(interp_hbm.at[:, at], interp_ref.at[:, at], sems.at[len(small) + t]))
+    for load in loads:
+        load.start()
+    child = by_part(packed_ref[:128])
+    loads[0].wait()
+    ops = ops_ref[...].astype(F32)
+    ops = jnp.concatenate([ops[:, 0], ops[:, 1]], axis=1).astype(BF16)
+    loads[1].wait()
     index = index_ref[...]
     lanes = lax.broadcasted_iota(jnp.int32, (CELLS, BAND), 1)
-    ops = ops_ref[...]
     step = 8
     for j0 in range(0, ENTRIES, step):
         picks = [
@@ -113,25 +148,23 @@
         ]
         chosen = jnp.dot(jnp.concatenate(picks, axis=0), ops, preferred_element_type=F32)
         chosen_ref[j0 * CELLS : (j0 + step) * CELLS] = chosen.astype(BF16)
-    load_phase.wait()
+    loads[2].wait()
     c, s = cos_sin(phase_ref[...])
     cos_ref[...] = c
     sin_ref[...] = s
-    child = packed_ref[:128]
     for t in range(TILES):
         at = slice(t * TILE, (t + 1) * TILE)
-        loads[t].wait()
+        loads[len(small) + t].wait()
         blocks = block_fields(child, interp_ref[:, at], c[:, at], s[:, at])
-        rows = 8 * len(blocks)
-        own_ref[t * rows : (t + 1) * rows] = jnp.concatenate(blocks, axis=0).astype(BF16)
-
-
-def front(packed, ops, *outside):
-    outside = [pltpu.with_memory_space_constraint(x, pltpu.HBM) for x in outside]
+        count = 8 * len(blocks)
+        own_ref[t * count : (t + 1) * count] = jnp.concatenate(blocks, axis=0).astype(BF16)
+
+
+def front(packed, *args):
     wave = jax.ShapeDtypeStruct((CHILDREN, DP), F32)
     return pl.pallas_call(
         front_kernel,
-        in_specs=[whole()] * 2 + [outer()] * 3,
+        in_specs=[whole()] + [outer()] * 4,
         out_specs=[whole()] * 5,
         out_shape=(
             jax.ShapeDtypeStruct((8 * DBLOCKS, 2 * BAND), BF16),
@@ -141,13 +174,14 @@
             wave,
         ),
         scratch_shapes=[
+            pltpu.VMEM((128, 2, BAND), BF16),
             pltpu.VMEM((CELLS, ENTRIES), jnp.int32),
             pltpu.VMEM((CHILDREN, DP), F32),
-            pltpu.SemaphoreType.DMA((TILES + 2,)),
+            pltpu.SemaphoreType.DMA((TILES + 3,)),
         ],
         compiler_params=params(),
         cost_estimate=pl.CostEstimate(flops=4 * 128 * DC * DP, bytes_accessed=DC * DP * 2, transcendentals=0),
-    )(packed, ops, *outside)
+    )(packed, *in_hbm(*args))
 
 
 def send_kernel(packed_ref, own_ref, order_ref, interp_ref, cos_ref, sin_ref, out_ref):
@@ -155,7 +189,7 @@
     order = order_ref[...].astype(F32)
     order = jnp.broadcast_to(jnp.concatenate([order, order], axis=1), (8, 2 * BAND))
     own = own_ref[...].astype(F32)
-    child = packed_ref[:128]
+    child = by_part(packed_ref[:128])
     for t in range(TILES):
         at = slice(t * TILE, (t + 1) * TILE)
         blocks = block_fields(child, interp_ref[:, at], cos_ref[:, at], sin_ref[:, at])
@@ -262,7 +296,8 @@
         total += lax.dot_general(
             shifted, interp_ref[:, at], (((1,), (1,)), ((), ())), preferred_element_type=F32
         )
-    out_ref[...] = (total * (DC / DP)).astype(BF16)
+    rows = by_box((total * (DC / DP)).astype(BF16))
+    out_ref[...] = rows.reshape(64, 2, DC)
 
 
 def anterpolate(received, interp, c, s):
@@ -270,7 +305,7 @@
         anterpolate_kernel,
         in_specs=[whole()] * 4,
         out_specs=whole(),
-        out_shape=jax.ShapeDtypeStruct((128, DC), BF16),
+        out_shape=jax.ShapeDtypeStruct((64, 2, DC), BF16),
         compiler_params=params(),
     )(received, interp, c, s)
 
@@ -287,15 +322,10 @@
 
 
 def per_device(child_fields, interp_matrix, phase_angle, patch_order, offset_code, operator_index, operators):
-    child_rows = child_fields.transpose(2, 1, 0, 3).reshape(128, DC)
-    packed = pack(child_rows, patch_order)
+    packed = pack(child_fields.reshape(64, 2, DC), patch_order)
     outside = lax.ppermute(packed, ("dir_1", "chip", "core"), outside_pairs(2, lax.axis_size("chip")))
     own, chosen, interp, c, s = front(
-        packed,
-        operators.reshape(128, 2 * BAND),
-        operator_index.reshape(CELLS, ENTRIES),
-        interp_matrix,
-        phase_angle,
+        packed, operators, operator_index.reshape(CELLS, ENTRIES), phase_angle, interp_matrix
     )
     send = to_send(outside, own, patch_order, interp, c, s)
     listed = lax.all_to_all(send.reshape(2 * DBLOCKS, 16, 2 * BAND), DIR + ("core",), 0, 0, tiled=True)
@@ -304,7 +334,7 @@
     )
     received = lax.all_to_all(returned.reshape(DBLOCKS, 8, 2 * BAND), DIR, 0, 0, tiled=True)
     fields = anterpolate(received.reshape(8 * DBLOCKS, 2 * BAND), interp, c, s)
-    return fields.reshape(2, CHILDREN, 8, DC).transpose(2, 1, 0, 3)
+    return fields.reshape(8, CHILDREN, 2, DC)
 
 
 def solution(mesh):

time: 63 us -> 62.3 us (0.989)
  local copies, waits for them, and re-layouts: 3.3 us -> 0.01 us
  Pallas kernels: 6.31 us -> 8.3 us
  blocking collectives: 47.6 us -> 48.3 us
    unnamed x7 -> x4, local copies, waits for them, and re-layouts: 1.51 us -> 0.01 us
    pallas_call x2, Pallas kernels: 3.15 us -> 4.24 us  [the longest x1 3.29 us: front(): pl.pallas_call(front_kernel, in_specs=[whole()] + [outer()] * 4, out_spec...]
    transpose x1 -> x0, local copies, waits for them, and re-layouts: 0.99 us -> none  [per_device(): child_rows = child_fields.transpose(2, 1, 0, 3).reshape(128, DC)]
    pallas_call x1, Pallas kernels: 0.84 us -> 1.66 us  [anterpolate(): pl.pallas_call(anterpolate_kernel, in_specs=[whole()] * 4, out_specs=whol...]
    reshape x1 -> x0, local copies, waits for them, and re-layouts: 0.79 us -> none  [per_device(): return fields.reshape(2, CHILDREN, 8, DC).transpose(2, 1, 0, 3)]
    all_to_all x1, blocking collectives: 32.7 us -> 33.4 us  [per_device(): lax.all_to_all(send.reshape(2 * DBLOCKS, 16, 2 * BAND), DIR + ('core',),...]
  transfers between devices with their start and end apart: 1 -> 1, of which waited for: 0 -> 0; matrix products, arithmetic and copies ran while one was open for 1% -> 0% of each run, Pallas kernels for 5% -> 5%
where the time goes in v4:
time: 62.3 us; the launch traced here: 62.1 us
  blocking collectives  48.3 us (78%)
  Pallas kernels  8.3 us (13%)
  starting transfers between devices  5.39 us (9%)
    all_to_all x1, blocking collectives, per_device(): lax.all_to_all(send.reshape(2 * DBLOCKS, 16, 2 * BAND), DIR + ('core',),...  33.4 us
    all_to_all x1, blocking collectives, per_device(): lax.all_to_all(returned.reshape(DBLOCKS, 8, 2 * BAND), DIR, 0, 0, tiled=T...  14.9 us
    ppermute x1, starting transfers between devices, per_device(): lax.ppermute(packed, ('dir_1', 'chip', 'core'), outside_pairs(2, lax.axis...  5.39 us
    pallas_call x1, Pallas kernels, front(): pl.pallas_call(front_kernel, in_specs=[whole()] + [outer()] * 4, out_spec...  3.29 us
    pallas_call x1, Pallas kernels, translate(): pl.pallas_call(translate_kernel, in_specs=[whole()] * 5, out_specs=whole(...  1.77 us
    pallas_call x1, Pallas kernels, anterpolate(): pl.pallas_call(anterpolate_kernel, in_specs=[whole()] * 4, out_specs=whol...  1.66 us
  transfers between devices with their start and end apart: 1, of which 0 were waited for; matrix products, arithmetic and copies ran while one was open for 0% of the time, Pallas kernels for 5%

profile of v4, /device:TPU:1, one launch (start us, length us, event | category | flops | bytes accessed | tf_op | source)
XLA Modules:
  0.0 62.1 jit_solution(6565187726068720436)
XLA Ops:
  0.0 0.0 copy-start.1
  0.0 0.9 %shard_map.73.packed_ref = bf16[144,512]{1,0:T(8,128)(2,1)S(1)} custom-call(bf16[64,2,512]{2,1,0:T(2,128)(2,1)} %bitcast.13, s32[1,128]{1,0:T(1,128)} %order_ref.3), custom_call_target="tpu_custom_call" | custom-call | tf_op jit(solution)/shard_map/pallas_call | solution.py:99
  1.0 5.4 %collective-permute-start = (bf16[144,512]{1,0:T(8,128)(2,1)S(1)}, bf16[144,512]{1,0:T(8,128)(2,1)S(1)}, u32[]{:S(2)}, u32[]{:S(2)}) collective-permute-start(bf16[144,512]{1,0:T(8,128)(2,1)S(1)} %shard_map.73.packed_ref), channel_id=1, source_target_pairs={{1,2},{2,1},{3,4},{4,3},{5,6},{6,5},{7,40},{40,7},{9,10},{10,9},{1... | collective-permute-start | bytes 442376 | tf_op jit(solution)/shard_map/ppermute | solution.py:326
  6.4 3.3 %shard_map.74 = (bf16[128,256]{1,0:T(8,128)(2,1)S(1)}, bf16[5120,256]{1,0:T(8,128)(2,1)S(1)}, bf16[512,2048]{1,0:T(8,128)(2,1)S(1)}, f32[8,2048]{1,0:T(8,128)S(1)}, f32[8,2048]{1,0:T(8,128)S(1)}) custom-call(bf16[144,512]{1,0:T(8,128)(2,1)S(1)} %shard_map.73.packed_ref, bf16[128,2,128]{2,1,0:T(2,128)(2,1)} %ops_hbm.1, s32[128,40]{1,0:T(8,128)} %bitcast.14, ...), custom_call_target="tpu_custom_call" | custom-call | flops 536870912 | bytes 2097152 | tf_op jit(solution)/shard_map/pallas_call | solution.py:165
  9.7 0.0 copy-start
  9.7 0.0 collective-permute-done.packed_ref
  9.7 0.0 copy-done.1
  9.7 0.6 %shard_map.75 = bf16[16,2,16,256]{3,2,1,0:T(8,128)(2,1)S(1)} custom-call(bf16[144,512]{1,0:T(8,128)(2,1)S(1)} %collective-permute-done.packed_ref, bf16[128,256]{1,0:T(8,128)(2,1)S(1)} %get-tuple-element.10.own_ref, s32[1,128]{1,0:T(1,128)S(1)} %copy-done.1, bf16[512,2048]{1,0:T(8,128)(2,1)S(1)} %get-tuple-element.11.interp_ref, ...), custom_call_target="tpu_custom_call" | custom-call | flops 268435456 | bytes 2097152 | tf_op jit(solution)/shard_map/pallas_call | solution.py:205
  10.3 33.4 %all_to_all.10 = bf16[32,16,256]{2,1,0:T(8,128)(2,1)S(1)} all-to-all(bf16[32,16,256]{2,1,0:T(8,128)(2,1)S(1)} %bitcast.8), channel_id=1, replica_groups=mesh['dir_0'=8,'dir_1'=2,'chip'=16,'core'=2] {'dir_0','dir_1','core'}, dimensions={0} | all-to-all | bytes 524288 | tf_op jit(solution)/shard_map/all_to_all | solution.py:331
  43.7 0.0 copy-done
  43.7 1.8 %shard_map.76 = bf16[128,256]{1,0:T(8,128)(2,1)S(1)} custom-call(bf16[16,2,16,256]{3,2,1,0:T(8,128)(2,1)S(1)} %bitcast.9, bf16[144,512]{1,0:T(8,128)(2,1)S(1)} %collective-permute-done.packed_ref, s32[128,40]{1,0:T(8,128)S(1)} %bitcast.12, bf16[5120,256]{1,0:T(8,128)(2,1)S(1)} %get-tuple-element.14.chosen_ref, s32[1,128]{1,0:T(1,128)S(1)} %copy-done.1), custom_call_target="tpu_custom_call" | custom-call | tf_op jit(solution)/shard_map/pallas_call | solution.py:271
  45.5 14.9 %all_to_all.11 = bf16[16,8,256]{2,1,0:T(8,128)(2,1)S(1)} all-to-all(bf16[16,8,256]{2,1,0:T(8,128)(2,1)S(1)} %bitcast.11), channel_id=1, replica_groups=mesh['dir_0'=8,'dir_1'=2,'chip'=16,'core'=2] {'dir_0','dir_1'}, dimensions={0} | all-to-all | bytes 131072 | tf_op jit(solution)/shard_map/all_to_all | solution.py:335
  60.4 1.7 %shard_map.77 = bf16[64,2,512]{2,1,0:T(2,128)(2,1)} custom-call(bf16[128,256]{1,0:T(8,128)(2,1)S(1)} %bitcast.10, bf16[512,2048]{1,0:T(8,128)(2,1)S(1)} %get-tuple-element.11.interp_ref, f32[8,2048]{1,0:T(8,128)S(1)} %get-tuple-element.12.cos_ref, f32[8,2048]{1,0:T(8,128)S(1)} %get-tuple-element.13.sin_ref), custom_call_target="tpu_custom_call" | custom-call | tf_op jit(solution)/shard_map/pallas_call | solution.py:304
Async XLA Ops:
  0.0 9.7 %copy-start.1 = (s32[1,128]{1,0:T(1,128)S(1)}, s32[1,128]{1,0:T(1,128)}, u32[]{:S(2)}) copy-start(s32[1,128]{1,0:T(1,128)} %order_ref.3) | copy-start | bytes 1540
  1.0 8.7 %collective-permute-start = (bf16[144,512]{1,0:T(8,128)(2,1)S(1)}, bf16[144,512]{1,0:T(8,128)(2,1)S(1)}, u32[]{:S(2)}, u32[]{:S(2)}) collective-permute-start(bf16[144,512]{1,0:T(8,128)(2,1)S(1)} %shard_map.73.packed_ref), channel_id=1, source_target_pairs={{1,2},{2,1},{3,4},{4,3},{5,6},{6,5},{7,40},{40,7},{9,10},{10,9},{1... | collective-permute-start | bytes 442376 | tf_op jit(solution)/shard_map/ppermute | solution.py:326
  9.7 34.1 %copy-start = (s32[8,16,40]{2,1,0:T(8,128)S(1)}, s32[8,16,40]{2,1,0:T(8,128)}, u32[]{:S(2)}) copy-start(s32[8,16,40]{2,1,0:T(8,128)} %param.11) | copy-start | bytes 61444

commit v5 on v4

v5 whole, which is shorter than its diff:
```python
import jax
import jax.numpy as jnp
from jax import lax
from jax.experimental import pallas as pl
from jax.experimental.pallas import tpu as pltpu
from jax.sharding import Mesh
from jax.sharding import PartitionSpec as P

DC = 512
DP = 2048
CHILDREN = 8
BAND = 128
CELLS = 128
COLS = 16
ENTRIES = 40
DBLOCKS = 16
HALO = 48
TILE = 512
TILES = DP // TILE
DIR = ("dir_0", "dir_1")
F32 = jnp.float32
BF16 = jnp.bfloat16
VMEM_LIMIT = 24 * 1024 * 1024


def params():
    return pltpu.CompilerParams(vmem_limit_bytes=VMEM_LIMIT)


def cos_sin(angle):
    half = angle * 0.5
    sq = half * half
    s = F32(1.0 / 6227020800.0)
    for c in (-1.0 / 39916800.0, 1.0 / 362880.0, -1.0 / 5040.0, 1.0 / 120.0, -1.0 / 6.0, 1.0):
        s = s * sq + F32(c)
    s = s * half
    c_ = F32(1.0 / 479001600.0)
    for c in (-1.0 / 3628800.0, 1.0 / 40320.0, -1.0 / 720.0, 1.0 / 24.0, -0.5, 1.0):
        c_ = c_ * sq + F32(c)
    return 1.0 - 2.0 * s * s, 2.0 * s * c_


def block_fields(child, interp, c, s):
    prod = jnp.dot(child, interp, preferred_element_type=F32)
    re = jnp.zeros((8, prod.shape[1]), F32)
    im = re
    for k in range(CHILDREN):
        pr, pi = prod[8 * k : 8 * k + 8], prod[64 + 8 * k : 72 + 8 * k]
        ck, sk = c[k : k + 1], s[k : k + 1]
        re = re + (ck * pr - sk * pi)
        im = im + (ck * pi + sk * pr)
    columns = [slice(d * BAND, (d + 1) * BAND) for d in range(prod.shape[1] // BAND)]
    return [jnp.concatenate([re[:, at], im[:, at]], axis=1) for at in columns]


def by_part(rows):
    there = lax.broadcasted_iota(jnp.int32, (128, 128), 0)
    here = lax.broadcasted_iota(jnp.int32, (128, 128), 1)
    wanted = (there & 7) * 16 + ((there >> 3) & 7) * 2 + (there >> 6)
    pick = jnp.where(here == wanted, 1.0, 0.0).astype(BF16)
    return jnp.dot(pick, rows, preferred_element_type=F32).astype(BF16)


def by_box(rows):
    there = lax.broadcasted_iota(jnp.int32, (128, 128), 0)
    here = lax.broadcasted_iota(jnp.int32, (128, 128), 1)
    wanted = (there & 1) * 64 + ((there >> 1) & 7) * 8 + (there >> 4)
    pick = jnp.where(here == wanted, 1.0, 0.0).astype(BF16)
    return jnp.dot(pick, rows, preferred_element_type=F32).astype(BF16)


def whole():
    return pl.BlockSpec(memory_space=pltpu.VMEM)


def outer():
    return pl.BlockSpec(memory_space=pltpu.HBM)


def in_hbm(*args):
    return [pltpu.with_memory_space_constraint(x, pltpu.HBM) for x in args]


def front_kernel(
    child_hbm, order_hbm, phase_hbm, interp_hbm, send_ref, interp_ref, cos_ref, sin_ref, child_ref, order_ref, phase_ref, sems
):
    small = [(child_hbm, child_ref), (order_hbm, order_ref), (phase_hbm, phase_ref)]
    loads = [pltpu.make_async_copy(there, here, sems.at[k]) for k, (there, here) in enumerate(small)]
    for t in range(TILES):
        at = pl.ds(t * TILE, TILE)
        loads.append(pltpu.make_async_copy(interp_hbm.at[:, at], interp_ref.at[:, at], sems.at[len(small) + t]))
    for load in loads:
        load.start()
    loads[0].wait()
    child = by_part(child_ref[...].reshape(128, DC))
    loads[1].wait()
    order = jnp.broadcast_to(order_ref[...].astype(F32), (8, CELLS))
    loads[2].wait()
    c, s = cos_sin(phase_ref[...])
    cos_ref[...] = c
    sin_ref[...] = s
    for t in range(TILES):
        at = slice(t * TILE, (t + 1) * TILE)
        loads[len(small) + t].wait()
        blocks = block_fields(child, interp_ref[:, at], c[:, at], s[:, at])
        for k, block in enumerate(blocks):
            d = t * len(blocks) + k
            out = jnp.concatenate([block, order], axis=1).astype(BF16)
            send_ref[2 * d] = out
            send_ref[2 * d + 1] = out


def front(*args):
    wave = jax.ShapeDtypeStruct((CHILDREN, DP), F32)
    return pl.pallas_call(
        front_kernel,
        in_specs=[outer()] * 4,
        out_specs=[whole()] * 4,
        out_shape=(
            jax.ShapeDtypeStruct((2 * DBLOCKS, 8, 3 * BAND), BF16),
            jax.ShapeDtypeStruct((DC, DP), BF16),
            wave,
            wave,
        ),
        scratch_shapes=[
            pltpu.VMEM((64, 2, DC), BF16),
            pltpu.VMEM((1, CELLS), jnp.int32),
            pltpu.VMEM((CHILDREN, DP), F32),
            pltpu.SemaphoreType.DMA((TILES + 3,)),
        ],
        compiler_params=params(),
        cost_estimate=pl.CostEstimate(flops=2 * 128 * DC * DP, bytes_accessed=DC * DP * 2, transcendentals=0),
    )(*in_hbm(*args))


def cells_kernel(recv_ref, order_ref, sources_ref, edge_ref):
    core = lax.axis_index("core")
    own = order_ref[...]
    ends = recv_ref[:16, 2 * BAND :].astype(F32)
    mate = jnp.where(core == 0, ends[0:1], ends[8:9]).astype(jnp.int32)
    onehots = []
    for position, side in ((own, 1 - core), (mate, core)):
        rows = (position >> 3) * 16 + side * 8 + (position & 7)
        column = jnp.broadcast_to(rows.astype(F32), (BAND, BAND)).T.astype(jnp.int32)
        parts = [
            jnp.where(column == lax.broadcasted_iota(jnp.int32, (BAND, BAND), 1) + k * BAND, 1.0, 0.0).astype(BF16)
            for k in range(2)
        ]
        onehots.append(jnp.concatenate(parts, axis=1))
    listed = recv_ref[:, : 2 * BAND]
    sources = jnp.dot(jnp.concatenate(onehots, axis=0), listed, preferred_element_type=F32)
    sources_ref[...] = sources.astype(BF16)
    edge_ref[...] = jnp.where(core == 0, sources[CELLS - HALO : CELLS], sources[:HALO]).astype(BF16)


def to_cells(received, order):
    return pl.pallas_call(
        cells_kernel,
        in_specs=[whole()] * 2,
        out_specs=[whole()] * 2,
        out_shape=(
            jax.ShapeDtypeStruct((2 * CELLS, 2 * BAND), BF16),
            jax.ShapeDtypeStruct((HALO, 2 * BAND), BF16),
        ),
        compiler_params=params(),
    )(received, order)


def operators_kernel(index_ref, ops_ref, out_ref):
    ops = ops_ref[...].astype(F32)
    ops = jnp.concatenate([ops[:, 0], ops[:, 1]], axis=1).astype(BF16)
    index = index_ref[...]
    lanes = lax.broadcasted_iota(jnp.int32, (CELLS, BAND), 1)
    step = 8
    for j0 in range(0, ENTRIES, step):
        picks = [
            jnp.where(index[:, j : j + 1] == lanes, 1.0, 0.0).astype(BF16)
            for j in range(j0, j0 + step)
        ]
        chosen = jnp.dot(jnp.concatenate(picks, axis=0), ops, preferred_element_type=F32)
        out_ref[j0 * CELLS : (j0 + step) * CELLS] = chosen.astype(BF16)


def chosen_operators(index, ops):
    return pl.pallas_call(
        operators_kernel,
        in_specs=[whole()] * 2,
        out_specs=whole(),
        out_shape=jax.ShapeDtypeStruct((ENTRIES * CELLS, 2 * BAND), BF16),
        compiler_params=params(),
        cost_estimate=pl.CostEstimate(
            flops=2 * ENTRIES * CELLS * 128 * 256, bytes_accessed=ENTRIES * CELLS * 512, transcendentals=0
        ),
    )(index, ops)


def translate_kernel(sources_ref, edge_ref, code_ref, chosen_ref, order_ref, out_ref):
    core = lax.axis_index("core")
    edge = edge_ref[...].astype(F32)
    outside = sources_ref[CELLS:].astype(F32)
    first = jnp.concatenate([edge, outside[HALO:]], axis=0)
    second = jnp.concatenate([outside[: CELLS - HALO], edge], axis=0)
    edges = jnp.where(core == 0, first, second).astype(BF16)
    sources = jnp.concatenate([sources_ref[:CELLS], edges], axis=0)

    code = code_ref[...]
    cell = lax.broadcasted_iota(jnp.int32, code.shape, 0)
    up = (code * 37) >> 8
    u = (cell >> 4) + up - 3
    v = ((cell & 15) + code - 7 * up + (COLS - 3)) & 15
    source = (u & 7) * COLS + v + jnp.where((u < 0) | (u > 7), CELLS, 0)
    lanes = lax.broadcasted_iota(jnp.int32, (CELLS, 2 * CELLS), 1)
    re = jnp.zeros((CELLS, BAND), F32)
    im = re
    step = 8
    for j0 in range(0, ENTRIES, step):
        picks = [
            jnp.where(source[:, j : j + 1] == lanes, 1.0, 0.0).astype(BF16)
            for j in range(j0, j0 + step)
        ]
        got = jnp.dot(jnp.concatenate(picks, axis=0), sources, preferred_element_type=F32)
        for k in range(step):
            op = chosen_ref[(j0 + k) * CELLS : (j0 + k + 1) * CELLS].astype(F32)
            g = got[k * CELLS : (k + 1) * CELLS]
            gr, gi, wr, wi = g[:, :BAND], g[:, BAND:], op[:, :BAND], op[:, BAND:]
            re = re + (wr * gr - wi * gi)
            im = im + (wr * gi + wi * gr)
    translated = jnp.concatenate([re, im], axis=1).astype(BF16)
    rows = lax.broadcasted_iota(jnp.int32, (CELLS, CELLS), 0)
    onehot = jnp.where(rows == order_ref[...], 1.0, 0.0).astype(BF16)
    out_ref[...] = jnp.dot(onehot, translated, preferred_element_type=F32).astype(BF16)


def translate(sources, edge, code, chosen, order):
    return pl.pallas_call(
        translate_kernel,
        in_specs=[whole()] * 5,
        out_specs=whole(),
        out_shape=jax.ShapeDtypeStruct((CELLS, 2 * BAND), BF16),
        compiler_params=params(),
    )(sources, edge, code, chosen, order)


def anterpolate_kernel(recv_ref, interp_ref, cos_ref, sin_ref, out_ref):
    total = jnp.zeros((128, DC), F32)
    rows = 8 * TILE // BAND
    for t in range(TILES):
        at = slice(t * TILE, (t + 1) * TILE)
        c, s = cos_ref[:, at], sin_ref[:, at]
        values = recv_ref[rows * t : rows * (t + 1)].astype(F32)
        blocks = rows // 8
        re = jnp.concatenate([values[8 * d : 8 * d + 8, :BAND] for d in range(blocks)], axis=1)
        im = jnp.concatenate([values[8 * d : 8 * d + 8, BAND:] for d in range(blocks)], axis=1)
        real, imag = [], []
        for k in range(CHILDREN):
            ck, sk = c[k : k + 1], s[k : k + 1]
            real.append(ck * re + sk * im)
            imag.append(ck * im - sk * re)
        shifted = jnp.concatenate(real + imag, axis=0).astype(BF16)
        total += lax.dot_general(
            shifted, interp_ref[:, at], (((1,), (1,)), ((), ())), preferred_element_type=F32
        )
    rows = by_box((total * (DC / DP)).astype(BF16))
    out_ref[...] = rows.reshape(64, 2, DC)


def anterpolate(received, interp, c, s):
    return pl.pallas_call(
        anterpolate_kernel,
        in_specs=[whole()] * 4,
        out_specs=whole(),
        out_shape=jax.ShapeDtypeStruct((64, 2, DC), BF16),
        compiler_params=params(),
    )(received, interp, c, s)


def neighbour_groups(chips):
    groups = []
    for chip in range(chips):
        sides = (2 * chip + 1, 2 * ((chip + 1) % chips))
        groups.append([d * 2 * chips + side for d in range(DBLOCKS) for side in sides])
    return groups


def per_device(child_fields, interp_matrix, phase_angle, patch_order, offset_code, operator_index, operators):
    send, interp, c, s = front(child_fields.reshape(64, 2, DC), patch_order, phase_angle, interp_matrix)
    received = lax.all_to_all(
        send, DIR + ("chip", "core"), 0, 0, axis_index_groups=neighbour_groups(lax.axis_size("chip")), tiled=True
    )
    sources, edge = to_cells(received.reshape(256, 3 * BAND), patch_order)
    index, edge = lax.optimization_barrier((operator_index.reshape(CELLS, ENTRIES), edge))
    chosen = chosen_operators(index, operators)
    edge = lax.ppermute(edge, "core", [(0, 1), (1, 0)])
    returned = translate(sources, edge, offset_code.reshape(CELLS, ENTRIES), chosen, patch_order)
    back = lax.all_to_all(returned.reshape(DBLOCKS, 8, 2 * BAND), DIR, 0, 0, tiled=True)
    fields = anterpolate(back.reshape(8 * DBLOCKS, 2 * BAND), interp, c, s)
    return fields.reshape(8, CHILDREN, 2, DC)


def solution(mesh):
    split = Mesh(mesh.devices.reshape(8, 2, mesh.shape["box"] // 2, 2), ("dir_0", "dir_1", "chip", "core"))
    box = ("chip", "core")
    placed = (
        P(box + DIR, None, None, None),
        P(),
        P(),
        P(box, None),
        P(box, None, None),
        P(box, None, None),
        P(None, None, DIR),
    )
    return jax.shard_map(
        per_device,
        mesh=split,
        in_specs=placed,
        out_specs=P(box + DIR, None, None, None),
        check_vma=False,
    )
```

time: 62.3 us -> 59.2 us (0.950)
  starting transfers between devices: 5.39 us -> 3.77 us
  Pallas kernels: 8.3 us -> 6.88 us
    all_to_all x1, blocking collectives: 33.4 us -> 30.8 us  [per_device(): lax.all_to_all(send, DIR + ('chip', 'core'), 0, 0, axis_index_groups=neig...]
    all_to_all x1, blocking collectives: 14.9 us -> 17.3 us  [per_device(): lax.all_to_all(returned.reshape(DBLOCKS, 8, 2 * BAND), DIR, 0, 0, tiled=T...]
    ppermute x1, starting transfers between devices: 5.39 us -> 3.77 us  [per_device(): edge = lax.ppermute(edge, 'core', [(0, 1), (1, 0)])]
    pallas_call x3, Pallas kernels: 4.87 us -> 3.64 us  [the longest x1 2.3 us: front(): pl.pallas_call(front_kernel, in_specs=[outer()] * 4, out_specs=[whole()]...]
  transfers between devices with their start and end apart: 1 -> 1, of which waited for: 0 -> 0; matrix products, arithmetic and copies ran while one was open for 0% -> 0% of each run, Pallas kernels for 5% -> 2%
where the time goes in v5:
time: 59.2 us; the launch traced here: 58.9 us
  blocking collectives  48.2 us (81%)
  Pallas kernels  6.88 us (12%)
  starting transfers between devices  3.77 us (6%)
    all_to_all x1, blocking collectives, per_device(): lax.all_to_all(send, DIR + ('chip', 'core'), 0, 0, axis_index_groups=neig...  30.8 us
    all_to_all x1, blocking collectives, per_device(): lax.all_to_all(returned.reshape(DBLOCKS, 8, 2 * BAND), DIR, 0, 0, tiled=T...  17.3 us
    ppermute x1, starting transfers between devices, per_device(): edge = lax.ppermute(edge, 'core', [(0, 1), (1, 0)])  3.77 us
    pallas_call x1, Pallas kernels, front(): pl.pallas_call(front_kernel, in_specs=[outer()] * 4, out_specs=[whole()]...  2.3 us
    pallas_call x1, Pallas kernels, anterpolate(): pl.pallas_call(anterpolate_kernel, in_specs=[whole()] * 4, out_specs=whol...  1.65 us
    pallas_call x1, Pallas kernels, translate(): pl.pallas_call(translate_kernel, in_specs=[whole()] * 5, out_specs=whole(...  1.59 us
  transfers between devices with their start and end apart: 1, of which 0 were waited for; matrix products, arithmetic and copies ran while one was open for 0% of the time, Pallas kernels for 2%

profile of v5, /device:TPU:1, one launch (start us, length us, event | category | flops | bytes accessed | tf_op | source)
XLA Modules:
  0.0 58.9 jit_solution(3970408010818180171)
XLA Ops:
  0.0 0.0 copy-start.3
  0.0 0.0 copy-start
  0.0 0.0 copy-start.1
  0.0 2.3 %shard_map.73 = (bf16[32,8,384]{2,1,0:T(8,128)(2,1)S(1)}, bf16[512,2048]{1,0:T(8,128)(2,1)S(1)}, f32[8,2048]{1,0:T(8,128)S(1)}, f32[8,2048]{1,0:T(8,128)S(1)}) custom-call(bf16[64,2,512]{2,1,0:T(2,128)(2,1)} %bitcast.12, s32[1,128]{1,0:T(1,128)} %order_ref.3, f32[8,2048]{1,0:T(8,128)} %phase_hbm.1, bf16[512,2048]{1,0:T(8,128)(2,1)} %interp_hbm.1), custom_call_target="tpu_custom_call" | custom-call | flops 268435456 | bytes 2097152 | tf_op jit(solution)/shard_map/pallas_call | solution.py:115
  2.3 0.0 copy-start.2
  2.3 30.8 %all_to_all.10 = bf16[32,8,384]{2,1,0:T(8,128)(2,1)S(1)} all-to-all(bf16[32,8,384]{2,1,0:T(8,128)(2,1)S(1)} %get-tuple-element.13), channel_id=1, replica_groups={{1,2,33,34,65,66,97,98,129,130,161,162,193,194,225,226,257,258,289,290,..., dimensions={0} | all-to-all | bytes 393216 | tf_op jit(solution)/shard_map/all_to_all | solution.py:287
  33.2 0.0 copy-done.3
  33.2 0.2 shard_map.74
  33.4 3.8 %collective-permute-start = (bf16[48,256]{1,0:T(8,128)(2,1)S(1)}, bf16[48,256]{1,0:T(8,128)(2,1)S(1)}, u32[]{:S(2)}, u32[]{:S(2)}) collective-permute-start(bf16[48,256]{1,0:T(8,128)(2,1)S(1)} %get-tuple-element.16), channel_id=1, source_target_pairs={{0,1},{1,0},{2,3},{3,2},{4,5},{5,4},{6,7},{7,6},{8,9},{9,8},{10,11... | collective-permute-start | bytes 73736 | tf_op jit(solution)/shard_map/ppermute | solution.py:293
  37.2 0.0 copy-done
  37.2 0.0 copy-done.1
  37.2 1.1 %shard_map.75.chosen_ref = bf16[5120,256]{1,0:T(8,128)(2,1)S(1)} custom-call(s32[128,40]{1,0:T(8,128)S(1)} %bitcast.10, bf16[128,2,128]{2,1,0:T(2,128)(2,1)S(1)} %copy-done.1), custom_call_target="tpu_custom_call" | custom-call | flops 335544320 | bytes 2621440 | tf_op jit(solution)/shard_map/pallas_call | solution.py:185
  38.3 0.0 collective-permute-done.edge_ref
  38.3 0.0 copy-done.2
  38.3 1.6 %shard_map.76 = bf16[128,256]{1,0:T(8,128)(2,1)S(1)} custom-call(bf16[256,256]{1,0:T(8,128)(2,1)S(1)} %get-tuple-element.14.sources_ref, bf16[48,256]{1,0:T(8,128)(2,1)S(1)} %collective-permute-done.edge_ref, s32[128,40]{1,0:T(8,128)S(1)} %bitcast.11, bf16[5120,256]{1,0:T(8,128)(2,1)S(1)} %shard_map.75.chosen_ref, s32[1,128]{1,0:T(1,128)S(1)} %copy-done.3), custom_call_target="tpu_custom_call" | custom-call | tf_op jit(solution)/shard_map/pallas_call | solution.py:235
  39.9 17.3 %all_to_all.11 = bf16[16,8,256]{2,1,0:T(8,128)(2,1)S(1)} all-to-all(bf16[16,8,256]{2,1,0:T(8,128)(2,1)S(1)} %bitcast.9), channel_id=1, replica_groups=mesh['dir_0'=8,'dir_1'=2,'chip'=16,'core'=2] {'dir_0','dir_1'}, dimensions={0} | all-to-all | bytes 131072 | tf_op jit(solution)/shard_map/all_to_all | solution.py:295
  57.3 1.7 %shard_map.77 = bf16[64,2,512]{2,1,0:T(2,128)(2,1)} custom-call(bf16[128,256]{1,0:T(8,128)(2,1)S(1)} %bitcast.8, bf16[512,2048]{1,0:T(8,128)(2,1)S(1)} %get-tuple-element.18.interp_ref, f32[8,2048]{1,0:T(8,128)S(1)} %get-tuple-element.19.cos_ref, f32[8,2048]{1,0:T(8,128)S(1)} %get-tuple-element.20.sin_ref), custom_call_target="tpu_custom_call" | custom-call | tf_op jit(solution)/shard_map/pallas_call | solution.py:268
Async XLA Ops:
  0.0 33.2 %copy-start.3 = (s32[1,128]{1,0:T(1,128)S(1)}, s32[1,128]{1,0:T(1,128)}, u32[]{:S(2)}) copy-start(s32[1,128]{1,0:T(1,128)} %order_ref.3) | copy-start | bytes 1540
  0.0 37.2 %copy-start = (s32[8,16,40]{2,1,0:T(8,128)S(1)}, s32[8,16,40]{2,1,0:T(8,128)}, u32[]{:S(2)}) copy-start(s32[8,16,40]{2,1,0:T(8,128)} %param.12) | copy-start | bytes 61444
  0.0 37.2 %copy-start.1 = (bf16[128,2,128]{2,1,0:T(2,128)(2,1)S(1)}, bf16[128,2,128]{2,1,0:T(2,128)(2,1)}, u32[]{:S(2)}) copy-start(bf16[128,2,128]{2,1,0:T(2,128)(2,1)} %ops_ref.1) | copy-start | bytes 196612
  2.3 36.0 %copy-start.2 = (s32[8,16,40]{2,1,0:T(8,128)S(1)}, s32[8,16,40]{2,1,0:T(8,128)}, u32[]{:S(2)}) copy-start(s32[8,16,40]{2,1,0:T(8,128)} %param.11) | copy-start | bytes 61444
  33.4 4.9 %collective-permute-start = (bf16[48,256]{1,0:T(8,128)(2,1)S(1)}, bf16[48,256]{1,0:T(8,128)(2,1)S(1)}, u32[]{:S(2)}, u32[]{:S(2)}) collective-permute-start(bf16[48,256]{1,0:T(8,128)(2,1)S(1)} %get-tuple-element.16), channel_id=1, source_target_pairs={{0,1},{1,0},{2,3},{3,2},{4,5},{5,4},{6,7},{7,6},{8,9},{9,8},{10,11... | collective-permute-start | bytes 73736 | tf_op jit(solution)/shard_map/ppermute | solution.py:293

commit v6 on v5

--- a/solution.py
+++ b/solution.py
@@ -15,6 +15,8 @@
 ENTRIES = 40
 DBLOCKS = 16
 HALO = 48
+WIDE = 4 * BAND
+RUN = 4
 TILE = 512
 TILES = DP // TILE
 DIR = ("dir_0", "dir_1")
@@ -82,7 +84,7 @@
 
 
 def front_kernel(
-    child_hbm, order_hbm, phase_hbm, interp_hbm, send_ref, interp_ref, cos_ref, sin_ref, child_ref, order_ref, phase_ref, sems
+    child_hbm, order_hbm, phase_hbm, interp_hbm, send_ref, cos_ref, sin_ref, child_ref, order_ref, phase_ref, interp_ref, sems
 ):
     small = [(child_hbm, child_ref), (order_hbm, order_ref), (phase_hbm, phase_ref)]
     loads = [pltpu.make_async_copy(there, here, sems.at[k]) for k, (there, here) in enumerate(small)]
@@ -103,11 +105,11 @@
         at = slice(t * TILE, (t + 1) * TILE)
         loads[len(small) + t].wait()
         blocks = block_fields(child, interp_ref[:, at], c[:, at], s[:, at])
-        for k, block in enumerate(blocks):
-            d = t * len(blocks) + k
-            out = jnp.concatenate([block, order], axis=1).astype(BF16)
-            send_ref[2 * d] = out
-            send_ref[2 * d + 1] = out
+        for k in range(0, len(blocks), 2):
+            at = t * len(blocks) + k
+            out = jnp.concatenate([blocks[k], blocks[k + 1], order], axis=1).astype(BF16)
+            send_ref[at] = out
+            send_ref[at + 1] = out
 
 
 def front(*args):
@@ -115,10 +117,9 @@
     return pl.pallas_call(
         front_kernel,
         in_specs=[outer()] * 4,
-        out_specs=[whole()] * 4,
+        out_specs=[whole()] * 3,
         out_shape=(
-            jax.ShapeDtypeStruct((2 * DBLOCKS, 8, 3 * BAND), BF16),
-            jax.ShapeDtypeStruct((DC, DP), BF16),
+            jax.ShapeDtypeStruct((DBLOCKS, 8, WIDE + BAND), BF16),
             wave,
             wave,
         ),
@@ -126,6 +127,7 @@
             pltpu.VMEM((64, 2, DC), BF16),
             pltpu.VMEM((1, CELLS), jnp.int32),
             pltpu.VMEM((CHILDREN, DP), F32),
+            pltpu.VMEM((DC, DP), BF16),
             pltpu.SemaphoreType.DMA((TILES + 3,)),
         ],
         compiler_params=params(),
@@ -133,43 +135,40 @@
     )(*in_hbm(*args))
 
 
-def cells_kernel(recv_ref, order_ref, sources_ref, edge_ref):
-    core = lax.axis_index("core")
+def cells_kernel(recv_ref, order_ref, done_ref, sources_ref, edge_ref):
+    core, half, chip = lax.axis_index("core"), lax.axis_index("dir_1"), lax.axis_index("chip")
+    turned = jnp.where(core == 0, chip % RUN == 0, chip % RUN == RUN - 1).astype(jnp.int32)
     own = order_ref[...]
-    ends = recv_ref[:16, 2 * BAND :].astype(F32)
+    ends = recv_ref[:16, WIDE:].astype(F32)
     mate = jnp.where(core == 0, ends[0:1], ends[8:9]).astype(jnp.int32)
     onehots = []
-    for position, side in ((own, 1 - core), (mate, core)):
-        rows = (position >> 3) * 16 + side * 8 + (position & 7)
+    for position, side, held in ((own, 1 - core, half), (mate, core, half ^ turned)):
+        rows = (position >> 4) * 16 + side * 8 + (position & 7)
+        rows = jnp.where(((position >> 3) & 1) == held, rows, -1)
         column = jnp.broadcast_to(rows.astype(F32), (BAND, BAND)).T.astype(jnp.int32)
-        parts = [
-            jnp.where(column == lax.broadcasted_iota(jnp.int32, (BAND, BAND), 1) + k * BAND, 1.0, 0.0).astype(BF16)
-            for k in range(2)
-        ]
-        onehots.append(jnp.concatenate(parts, axis=1))
-    listed = recv_ref[:, : 2 * BAND]
-    sources = jnp.dot(jnp.concatenate(onehots, axis=0), listed, preferred_element_type=F32)
+        lanes = lax.broadcasted_iota(jnp.int32, (BAND, BAND), 1)
+        onehots.append(jnp.where(column == lanes, 1.0, 0.0).astype(BF16))
+    sources = jnp.dot(jnp.concatenate(onehots, axis=0), recv_ref[:, :WIDE], preferred_element_type=F32)
     sources_ref[...] = sources.astype(BF16)
     edge_ref[...] = jnp.where(core == 0, sources[CELLS - HALO : CELLS], sources[:HALO]).astype(BF16)
 
 
-def to_cells(received, order):
+def to_cells(received, order, done):
     return pl.pallas_call(
         cells_kernel,
-        in_specs=[whole()] * 2,
+        in_specs=[whole()] * 3,
         out_specs=[whole()] * 2,
         out_shape=(
-            jax.ShapeDtypeStruct((2 * CELLS, 2 * BAND), BF16),
-            jax.ShapeDtypeStruct((HALO, 2 * BAND), BF16),
+            jax.ShapeDtypeStruct((2 * CELLS, WIDE), BF16),
+            jax.ShapeDtypeStruct((HALO, WIDE), BF16),
         ),
         compiler_params=params(),
-    )(received, order)
-
-
-def operators_kernel(index_ref, ops_ref, out_ref):
-    ops = ops_ref[...].astype(F32)
+    )(received, order, done)
+
+
+def choose(index, ops, out_ref):
+    ops = ops.astype(F32)
     ops = jnp.concatenate([ops[:, 0], ops[:, 1]], axis=1).astype(BF16)
-    index = index_ref[...]
     lanes = lax.broadcasted_iota(jnp.int32, (CELLS, BAND), 1)
     step = 8
     for j0 in range(0, ENTRIES, step):
@@ -181,27 +180,66 @@
         out_ref[j0 * CELLS : (j0 + step) * CELLS] = chosen.astype(BF16)
 
 
-def chosen_operators(index, ops):
-    return pl.pallas_call(
-        operators_kernel,
+def own_operators_kernel(index_hbm, ops_hbm, out_ref, done_ref, index_ref, ops_ref, sems):
+    loads = [
+        pltpu.make_async_copy(index_hbm, index_ref, sems.at[0]),
+        pltpu.make_async_copy(ops_hbm, ops_ref, sems.at[1]),
+    ]
+    for load in loads:
+        load.start()
+    for load in loads:
+        load.wait()
+    choose(index_ref[...], ops_ref[...], out_ref)
+    done_ref[...] = jnp.zeros_like(done_ref)
+
+
+def other_operators_kernel(index_ref, ops_ref, out_ref):
+    choose(index_ref[...], ops_ref[...], out_ref)
+
+
+CHOICE = pl.CostEstimate(flops=2 * ENTRIES * CELLS * 128 * 256, bytes_accessed=ENTRIES * CELLS * 512, transcendentals=0)
+
+
+def own_operators(index, ops):
+    return pl.pallas_call(
+        own_operators_kernel,
+        in_specs=[outer()] * 2,
+        out_specs=[whole()] * 2,
+        out_shape=(
+            jax.ShapeDtypeStruct((ENTRIES * CELLS, 2 * BAND), BF16),
+            jax.ShapeDtypeStruct((8, BAND), F32),
+        ),
+        scratch_shapes=[
+            pltpu.VMEM((CELLS, ENTRIES), jnp.int32),
+            pltpu.VMEM((128, 2, BAND), BF16),
+            pltpu.SemaphoreType.DMA((2,)),
+        ],
+        compiler_params=params(),
+        cost_estimate=CHOICE,
+    )(*in_hbm(index, ops))
+
+
+def other_operators(index, ops):
+    return pl.pallas_call(
+        other_operators_kernel,
         in_specs=[whole()] * 2,
         out_specs=whole(),
         out_shape=jax.ShapeDtypeStruct((ENTRIES * CELLS, 2 * BAND), BF16),
         compiler_params=params(),
-        cost_estimate=pl.CostEstimate(
-            flops=2 * ENTRIES * CELLS * 128 * 256, bytes_accessed=ENTRIES * CELLS * 512, transcendentals=0
-        ),
+        cost_estimate=CHOICE,
     )(index, ops)
 
 
-def translate_kernel(sources_ref, edge_ref, code_ref, chosen_ref, order_ref, out_ref):
-    core = lax.axis_index("core")
+def translate_kernel(sources_ref, edge_ref, code_ref, own_ref, other_ref, order_ref, out_ref):
+    core, half = lax.axis_index("core"), lax.axis_index("dir_1")
     edge = edge_ref[...].astype(F32)
     outside = sources_ref[CELLS:].astype(F32)
     first = jnp.concatenate([edge, outside[HALO:]], axis=0)
     second = jnp.concatenate([outside[: CELLS - HALO], edge], axis=0)
     edges = jnp.where(core == 0, first, second).astype(BF16)
     sources = jnp.concatenate([sources_ref[:CELLS], edges], axis=0)
+    low, high = sources[:, : 2 * BAND], sources[:, 2 * BAND :]
+    sides = ((jnp.where(half == 0, low, high), own_ref), (jnp.where(half == 0, high, low), other_ref))
 
     code = code_ref[...]
     cell = lax.broadcasted_iota(jnp.int32, code.shape, 0)
@@ -210,47 +248,54 @@
     v = ((cell & 15) + code - 7 * up + (COLS - 3)) & 15
     source = (u & 7) * COLS + v + jnp.where((u < 0) | (u > 7), CELLS, 0)
     lanes = lax.broadcasted_iota(jnp.int32, (CELLS, 2 * CELLS), 1)
-    re = jnp.zeros((CELLS, BAND), F32)
-    im = re
+    totals = [jnp.zeros((CELLS, BAND), F32)] * 4
     step = 8
     for j0 in range(0, ENTRIES, step):
         picks = [
             jnp.where(source[:, j : j + 1] == lanes, 1.0, 0.0).astype(BF16)
             for j in range(j0, j0 + step)
         ]
-        got = jnp.dot(jnp.concatenate(picks, axis=0), sources, preferred_element_type=F32)
-        for k in range(step):
-            op = chosen_ref[(j0 + k) * CELLS : (j0 + k + 1) * CELLS].astype(F32)
-            g = got[k * CELLS : (k + 1) * CELLS]
-            gr, gi, wr, wi = g[:, :BAND], g[:, BAND:], op[:, :BAND], op[:, BAND:]
-            re = re + (wr * gr - wi * gi)
-            im = im + (wr * gi + wi * gr)
-    translated = jnp.concatenate([re, im], axis=1).astype(BF16)
+        picks = jnp.concatenate(picks, axis=0)
+        for h, (fields, chosen_ref) in enumerate(sides):
+            got = jnp.dot(picks, fields, preferred_element_type=F32)
+            re, im = totals[2 * h : 2 * h + 2]
+            for k in range(step):
+                op = chosen_ref[(j0 + k) * CELLS : (j0 + k + 1) * CELLS].astype(F32)
+                g = got[k * CELLS : (k + 1) * CELLS]
+                gr, gi, wr, wi = g[:, :BAND], g[:, BAND:], op[:, :BAND], op[:, BAND:]
+                re = re + (wr * gr - wi * gi)
+                im = im + (wr * gi + wi * gr)
+            totals[2 * h : 2 * h + 2] = re, im
+    own, other = jnp.concatenate(totals[:2], axis=1), jnp.concatenate(totals[2:], axis=1)
+    translated = jnp.concatenate([jnp.where(half == 0, own, other), jnp.where(half == 0, other, own)], axis=1).astype(BF16)
     rows = lax.broadcasted_iota(jnp.int32, (CELLS, CELLS), 0)
     onehot = jnp.where(rows == order_ref[...], 1.0, 0.0).astype(BF16)
     out_ref[...] = jnp.dot(onehot, translated, preferred_element_type=F32).astype(BF16)
 
 
-def translate(sources, edge, code, chosen, order):
+def translate(*args):
     return pl.pallas_call(
         translate_kernel,
-        in_specs=[whole()] * 5,
+        in_specs=[whole()] * 6,
         out_specs=whole(),
-        out_shape=jax.ShapeDtypeStruct((CELLS, 2 * BAND), BF16),
-        compiler_params=params(),
-    )(sources, edge, code, chosen, order)
+        out_shape=jax.ShapeDtypeStruct((CELLS, WIDE), BF16),
+        compiler_params=params(),
+    )(*args)
 
 
 def anterpolate_kernel(recv_ref, interp_ref, cos_ref, sin_ref, out_ref):
     total = jnp.zeros((128, DC), F32)
-    rows = 8 * TILE // BAND
+    per_tile = TILE // (2 * BAND)
     for t in range(TILES):
         at = slice(t * TILE, (t + 1) * TILE)
         c, s = cos_ref[:, at], sin_ref[:, at]
-        values = recv_ref[rows * t : rows * (t + 1)].astype(F32)
-        blocks = rows // 8
-        re = jnp.concatenate([values[8 * d : 8 * d + 8, :BAND] for d in range(blocks)], axis=1)
-        im = jnp.concatenate([values[8 * d : 8 * d + 8, BAND:] for d in range(blocks)], axis=1)
+        values = recv_ref[16 * per_tile * t : 16 * per_tile * (t + 1)].astype(F32)
+        re, im = [], []
+        for y in range(per_tile):
+            both = values[16 * y : 16 * y + 8] + values[16 * y + 8 : 16 * y + 16]
+            re += [both[:, :BAND], both[:, 2 * BAND : 3 * BAND]]
+            im += [both[:, BAND : 2 * BAND], both[:, 3 * BAND :]]
+        re, im = jnp.concatenate(re, axis=1), jnp.concatenate(im, axis=1)
         real, imag = [], []
         for k in range(CHILDREN):
             ck, sk = c[k : k + 1], s[k : k + 1]
@@ -276,24 +321,41 @@
 
 def neighbour_groups(chips):
     groups = []
-    for chip in range(chips):
-        sides = (2 * chip + 1, 2 * ((chip + 1) % chips))
-        groups.append([d * 2 * chips + side for d in range(DBLOCKS) for side in sides])
+    for half in range(2):
+        for chip in range(chips):
+            there = half ^ 1 if chip % RUN == RUN - 1 else half
+            sides = ((half * chips + chip) * 2 + 1, (there * chips + (chip + 1) % chips) * 2)
+            groups.append([y * 4 * chips + side for y in range(DBLOCKS // 2) for side in sides])
     return groups
 
 
+def other_half(chips):
+    pairs = []
+    for half in range(2):
+        for chip in range(chips):
+            for core in range(2):
+                pairs.append(((half * chips + chip) * 2 + core, ((half ^ 1) * chips + (chip ^ 2)) * 2 + core))
+    return pairs
+
+
 def per_device(child_fields, interp_matrix, phase_angle, patch_order, offset_code, operator_index, operators):
-    send, interp, c, s = front(child_fields.reshape(64, 2, DC), patch_order, phase_angle, interp_matrix)
+    chips = lax.axis_size("chip")
+    other = lax.ppermute(operators, ("dir_1", "chip", "core"), other_half(chips))
+    send, c, s = front(child_fields.reshape(64, 2, DC), patch_order, phase_angle, interp_matrix)
     received = lax.all_to_all(
-        send, DIR + ("chip", "core"), 0, 0, axis_index_groups=neighbour_groups(lax.axis_size("chip")), tiled=True
+        send, DIR + ("chip", "core"), 0, 0, axis_index_groups=neighbour_groups(chips), tiled=True
     )
-    sources, edge = to_cells(received.reshape(256, 3 * BAND), patch_order)
-    index, edge = lax.optimization_barrier((operator_index.reshape(CELLS, ENTRIES), edge))
-    chosen = chosen_operators(index, operators)
+    index = operator_index.reshape(CELLS, ENTRIES)
+    chosen, done = own_operators(index, operators)
+    sources, edge = to_cells(received.reshape(CELLS, WIDE + BAND), patch_order, done)
+    edge, index = lax.optimization_barrier((edge, index))
+    chosen_other = other_operators(index, other)
     edge = lax.ppermute(edge, "core", [(0, 1), (1, 0)])
-    returned = translate(sources, edge, offset_code.reshape(CELLS, ENTRIES), chosen, patch_order)
-    back = lax.all_to_all(returned.reshape(DBLOCKS, 8, 2 * BAND), DIR, 0, 0, tiled=True)
-    fields = anterpolate(back.reshape(8 * DBLOCKS, 2 * BAND), interp, c, s)
+    returned = translate(
+        sources, edge, offset_code.reshape(CELLS, ENTRIES), chosen, chosen_other, patch_order
+    )
+    back = lax.all_to_all(returned.reshape(DBLOCKS, 8, WIDE), DIR, 0, 0, tiled=True)
+    fields = anterpolate(back.reshape(8 * DBLOCKS, WIDE), interp_matrix, c, s)
     return fields.reshape(8, CHILDREN, 2, DC)
 
 

time: 59.2 us -> 56.5 us (0.954); the launches traced: 58.9 us -> 55.4 us
  blocking collectives: 48.2 us -> 17 us
  starting transfers between devices: 3.77 us -> 27.3 us
  Pallas kernels: 6.88 us -> 10.9 us
    all_to_all x2 -> x1, blocking collectives: 48.2 us -> 17 us  [per_device(): lax.all_to_all(returned.reshape(DBLOCKS, 8, WIDE), DIR, 0, 0, tiled=True)]
    all_to_all x0 -> x1, starting transfers between devices: none -> 10.3 us  [per_device(): lax.all_to_all(send, DIR + ('chip', 'core'), 0, 0, axis_index_groups=neig...]
    ppermute x0 -> x1, starting transfers between devices: none -> 9.76 us  [per_device(): lax.ppermute(operators, ('dir_1', 'chip', 'core'), other_half(chips))]
    ppermute x1, starting transfers between devices: 3.77 us -> 7.3 us  [per_device(): edge = lax.ppermute(edge, 'core', [(0, 1), (1, 0)])]
    pallas_call x3 -> x4, Pallas kernels: 2.93 us -> 6.32 us  [the longest x1 2.97 us: translate(): pl.pallas_call(translate_kernel, in_specs=[whole()] * 6, out_specs=whole(...]
    pallas_call x1, Pallas kernels: 2.3 us -> 2.95 us  [front(): pl.pallas_call(front_kernel, in_specs=[outer()] * 4, out_specs=[whole()]...]
  transfers between devices with their start and end apart: 1 -> 3, of which waited for: 0 -> 0; matrix products, arithmetic and copies ran while one was open for 0% -> 0% of each run, Pallas kernels for 2% -> 6%
where the time goes in v6:
time: 56.5 us; the launch traced here: 55.4 us
  starting transfers between devices  27.3 us (48%)
  blocking collectives  17 us (30%)
  Pallas kernels  10.9 us (19%)
    all_to_all x1, blocking collectives, per_device(): lax.all_to_all(returned.reshape(DBLOCKS, 8, WIDE), DIR, 0, 0, tiled=True)  17 us
    all_to_all x1, starting transfers between devices, per_device(): lax.all_to_all(send, DIR + ('chip', 'core'), 0, 0, axis_index_groups=neig...  10.3 us
    ppermute x1, starting transfers between devices, per_device(): lax.ppermute(operators, ('dir_1', 'chip', 'core'), other_half(chips))  9.76 us
    ppermute x1, starting transfers between devices, per_device(): edge = lax.ppermute(edge, 'core', [(0, 1), (1, 0)])  7.3 us
    pallas_call x1, Pallas kernels, translate(): pl.pallas_call(translate_kernel, in_specs=[whole()] * 6, out_specs=whole(...  2.97 us
    pallas_call x1, Pallas kernels, front(): pl.pallas_call(front_kernel, in_specs=[outer()] * 4, out_specs=[whole()]...  2.95 us
    pallas_call x1, Pallas kernels, own_operators(): pl.pallas_call(own_operators_kernel, in_specs=[outer()] * 2, out_specs=[w...  1.98 us
    pallas_call x1, Pallas kernels, anterpolate(): pl.pallas_call(anterpolate_kernel, in_specs=[whole()] * 4, out_specs=whol...  1.66 us
  transfers between devices with their start and end apart: 3, of which 0 were waited for; matrix products, arithmetic and copies ran while one was open for 0% of the time, Pallas kernels for 6%

profile of v6, /device:TPU:1, one launch (start us, length us, event | category | flops | bytes accessed | tf_op | source)
XLA Modules:
  0.0 55.4 jit_solution(6271664670166746799)
XLA Ops:
  0.0 0.0 copy-start.3
  0.0 0.0 copy-start.4
  0.0 0.0 copy-start.2
  0.0 3.0 %shard_map.73 = (bf16[16,8,640]{2,1,0:T(8,128)(2,1)}, f32[8,2048]{1,0:T(8,128)S(1)}, f32[8,2048]{1,0:T(8,128)S(1)}) custom-call(bf16[64,2,512]{2,1,0:T(2,128)(2,1)} %bitcast.13, s32[1,128]{1,0:T(1,128)} %order_ref.3, f32[8,2048]{1,0:T(8,128)} %phase_hbm.1, bf16[512,2048]{1,0:T(8,128)(2,1)} %interp_ref.1), custom_call_target="tpu_custom_call" | custom-call | flops 268435456 | bytes 2097152 | tf_op jit(solution)/shard_map/pallas_call | solution.py:117
  3.0 0.0 copy-start.1
  3.0 10.3 %all-to-all-start = ((bf16[16,8,640]{2,1,0:T(8,128)(2,1)}), bf16[16,8,640]{2,1,0:T(8,128)(2,1)S(1)}, u32[]{:S(2)}, u32[]{:S(2)}) async-start(bf16[16,8,640]{2,1,0:T(8,128)(2,1)} %get-tuple-element.14), calls=%async_computation | async-start | bytes 327680 | tf_op jit(solution)/shard_map/all_to_all | solution.py:345
  13.3 0.0 copy-done.4
  13.3 9.8 %collective-permute-start.1 = (bf16[128,2,128]{2,1,0:T(2,128)(2,1)S(1)}, bf16[128,2,128]{2,1,0:T(2,128)(2,1)S(1)}, u32[]{:S(2)}, u32[]{:S(2)}) collective-permute-start(bf16[128,2,128]{2,1,0:T(2,128)(2,1)S(1)} %copy-done.4), channel_id=1, source_target_pairs={{0,36},{1,37},{2,38},{3,39},{4,32},{5,33},{6,34},{7,35},{8,44},{9,... | collective-permute-start | bytes 196616 | tf_op jit(solution)/shard_map/ppermute | solution.py:343
  23.0 2.0 %shard_map.74 = (bf16[5120,256]{1,0:T(8,128)(2,1)S(1)}, f32[8,128]{1,0:T(8,128)S(1)}) custom-call(s32[128,40]{1,0:T(8,128)} %bitcast.11, bf16[128,2,128]{2,1,0:T(2,128)(2,1)} %ops_hbm.1), custom_call_target="tpu_custom_call" | custom-call | flops 335544320 | bytes 2621440 | tf_op jit(solution)/shard_map/pallas_call | solution.py:204
  25.0 0.0 all-to-all-done
  25.0 0.0 copy-done.3
  25.0 0.3 shard_map.75
  25.3 7.3 %collective-permute-start = (bf16[48,512]{1,0:T(8,128)(2,1)S(1)}, bf16[48,512]{1,0:T(8,128)(2,1)S(1)}, u32[]{:S(2)}, u32[]{:S(2)}) collective-permute-start(bf16[48,512]{1,0:T(8,128)(2,1)S(1)} %get-tuple-element.18), channel_id=1, source_target_pairs={{0,1},{1,0},{2,3},{3,2},{4,5},{5,4},{6,7},{7,6},{8,9},{9,8},{10,11... | collective-permute-start | bytes 147464 | tf_op jit(solution)/shard_map/ppermute | solution.py:353
  32.6 0.0 collective-permute-done.1.ops_ref
  32.6 0.0 copy-done.2
  32.7 1.1 %shard_map.76.other_ref = bf16[5120,256]{1,0:T(8,128)(2,1)S(1)} custom-call(s32[128,40]{1,0:T(8,128)S(1)} %bitcast.12, bf16[128,2,128]{2,1,0:T(2,128)(2,1)S(1)} %collective-permute-done.1.ops_ref), custom_call_target="tpu_custom_call" | custom-call | flops 335544320 | bytes 2621440 | tf_op jit(solution)/shard_map/pallas_call | solution.py:223
  33.7 0.0 collective-permute-done.edge_ref
  33.8 0.0 copy-done.1
  33.8 0.0 copy-start
  33.8 3.0 %shard_map.77 = bf16[128,512]{1,0:T(8,128)(2,1)S(1)} custom-call(bf16[256,512]{1,0:T(8,128)(2,1)S(1)} %get-tuple-element.16.sources_ref, bf16[48,512]{1,0:T(8,128)(2,1)S(1)} %collective-permute-done.edge_ref, s32[128,40]{1,0:T(8,128)S(1)} %bitcast.10, bf16[5120,256]{1,0:T(8,128)(2,1)S(1)} %get-tuple-element.19.own_ref, ...), custom_call_target="tpu_custom_call" | custom-call | tf_op jit(solution)/shard_map/pallas_call | solution.py:277
  36.8 17.0 %all_to_all.10 = bf16[16,8,512]{2,1,0:T(8,128)(2,1)S(1)} all-to-all(bf16[16,8,512]{2,1,0:T(8,128)(2,1)S(1)} %bitcast.8), channel_id=1, replica_groups=mesh['dir_0'=8,'dir_1'=2,'chip'=16,'core'=2] {'dir_0','dir_1'}, dimensions={0} | all-to-all | bytes 262144 | tf_op jit(solution)/shard_map/all_to_all | solution.py:357
  53.7 0.0 copy-done
  53.7 1.7 %shard_map.78 = bf16[64,2,512]{2,1,0:T(2,128)(2,1)} custom-call(bf16[128,512]{1,0:T(8,128)(2,1)S(1)} %bitcast.9, bf16[512,2048]{1,0:T(8,128)(2,1)S(1)} %copy-done, f32[8,2048]{1,0:T(8,128)S(1)} %get-tuple-element.21.cos_ref, f32[8,2048]{1,0:T(8,128)S(1)} %get-tuple-element.22.sin_ref), custom_call_target="tpu_custom_call" | custom-call | tf_op jit(solution)/shard_map/pallas_call | solution.py:313
Async XLA Ops:
  0.0 25.0 %copy-start.3 = (s32[1,128]{1,0:T(1,128)S(1)}, s32[1,128]{1,0:T(1,128)}, u32[]{:S(2)}) copy-start(s32[1,128]{1,0:T(1,128)} %order_ref.3) | copy-start | bytes 1540
  0.0 13.3 %copy-start.4 = (bf16[128,2,128]{2,1,0:T(2,128)(2,1)S(1)}, bf16[128,2,128]{2,1,0:T(2,128)(2,1)}, u32[]{:S(2)}) copy-start(bf16[128,2,128]{2,1,0:T(2,128)(2,1)} %ops_hbm.1) | copy-start | bytes 196612
  0.0 32.6 %copy-start.2 = (s32[8,16,40]{2,1,0:T(8,128)S(1)}, s32[8,16,40]{2,1,0:T(8,128)}, u32[]{:S(2)}) copy-start(s32[8,16,40]{2,1,0:T(8,128)} %param.12) | copy-start | bytes 61444
  3.0 30.8 %copy-start.1 = (s32[8,16,40]{2,1,0:T(8,128)S(1)}, s32[8,16,40]{2,1,0:T(8,128)}, u32[]{:S(2)}) copy-start(s32[8,16,40]{2,1,0:T(8,128)} %param.11) | copy-start | bytes 61444
  3.0 22.0 %all-to-all-start = ((bf16[16,8,640]{2,1,0:T(8,128)(2,1)}), bf16[16,8,640]{2,1,0:T(8,128)(2,1)S(1)}, u32[]{:S(2)}, u32[]{:S(2)}) async-start(bf16[16,8,640]{2,1,0:T(8,128)(2,1)} %get-tuple-element.14), calls=%async_computation | async-start | bytes 327680 | tf_op jit(solution)/shard_map/all_to_all | solution.py:345
  13.3 19.4 %collective-permute-start.1 = (bf16[128,2,128]{2,1,0:T(2,128)(2,1)S(1)}, bf16[128,2,128]{2,1,0:T(2,128)(2,1)S(1)}, u32[]{:S(2)}, u32[]{:S(2)}) collective-permute-start(bf16[128,2,128]{2,1,0:T(2,128)(2,1)S(1)} %copy-done.4), channel_id=1, source_target_pairs={{0,36},{1,37},{2,38},{3,39},{4,32},{5,33},{6,34},{7,35},{8,44},{9,... | collective-permute-start | bytes 196616 | tf_op jit(solution)/shard_map/ppermute | solution.py:343
  25.3 8.4 %collective-permute-start = (bf16[48,512]{1,0:T(8,128)(2,1)S(1)}, bf16[48,512]{1,0:T(8,128)(2,1)S(1)}, u32[]{:S(2)}, u32[]{:S(2)}) collective-permute-start(bf16[48,512]{1,0:T(8,128)(2,1)S(1)} %get-tuple-element.18), channel_id=1, source_target_pairs={{0,1},{1,0},{2,3},{3,2},{4,5},{5,4},{6,7},{7,6},{8,9},{9,8},{10,11... | collective-permute-start | bytes 147464 | tf_op jit(solution)/shard_map/ppermute | solution.py:353
  33.8 20.0 %copy-start = (bf16[512,2048]{1,0:T(8,128)(2,1)S(1)}, bf16[512,2048]{1,0:T(8,128)(2,1)}, u32[]{:S(2)}) copy-start(bf16[512,2048]{1,0:T(8,128)(2,1)} %interp_ref.1) | copy-start | bytes 6291460

commit v7 on v6

--- a/solution.py
+++ b/solution.py
@@ -13,6 +13,8 @@
 CELLS = 128
 COLS = 16
 ENTRIES = 40
+NOPS = 128
+GROUP = 16
 DBLOCKS = 16
 HALO = 48
 WIDE = 4 * BAND
@@ -84,7 +86,7 @@
 
 
 def front_kernel(
-    child_hbm, order_hbm, phase_hbm, interp_hbm, send_ref, cos_ref, sin_ref, child_ref, order_ref, phase_ref, interp_ref, sems
+    child_hbm, order_hbm, phase_hbm, interp_hbm, send_hbm, cos_ref, sin_ref, child_ref, order_ref, phase_ref, interp_ref, send_ref, sems
 ):
     small = [(child_hbm, child_ref), (order_hbm, order_ref), (phase_hbm, phase_ref)]
     loads = [pltpu.make_async_copy(there, here, sems.at[k]) for k, (there, here) in enumerate(small)]
@@ -101,6 +103,7 @@
     c, s = cos_sin(phase_ref[...])
     cos_ref[...] = c
     sin_ref[...] = s
+    stores = []
     for t in range(TILES):
         at = slice(t * TILE, (t + 1) * TILE)
         loads[len(small) + t].wait()
@@ -110,6 +113,11 @@
             out = jnp.concatenate([blocks[k], blocks[k + 1], order], axis=1).astype(BF16)
             send_ref[at] = out
             send_ref[at + 1] = out
+        here = pl.ds(t * len(blocks), len(blocks))
+        stores.append(pltpu.make_async_copy(send_ref.at[here], send_hbm.at[here], sems.at[len(small) + TILES + t]))
+        stores[t].start()
+    for store in stores:
+        store.wait()
 
 
 def front(*args):
@@ -117,7 +125,7 @@
     return pl.pallas_call(
         front_kernel,
         in_specs=[outer()] * 4,
-        out_specs=[whole()] * 3,
+        out_specs=[outer(), whole(), whole()],
         out_shape=(
             jax.ShapeDtypeStruct((DBLOCKS, 8, WIDE + BAND), BF16),
             wave,
@@ -128,14 +136,15 @@
             pltpu.VMEM((1, CELLS), jnp.int32),
             pltpu.VMEM((CHILDREN, DP), F32),
             pltpu.VMEM((DC, DP), BF16),
-            pltpu.SemaphoreType.DMA((TILES + 3,)),
+            pltpu.VMEM((DBLOCKS, 8, WIDE + BAND), BF16),
+            pltpu.SemaphoreType.DMA((2 * TILES + 3,)),
         ],
         compiler_params=params(),
         cost_estimate=pl.CostEstimate(flops=2 * 128 * DC * DP, bytes_accessed=DC * DP * 2, transcendentals=0),
     )(*in_hbm(*args))
 
 
-def cells_kernel(recv_ref, order_ref, done_ref, sources_ref, edge_ref):
+def cells_kernel(recv_ref, order_ref, sources_ref, edge_ref):
     core, half, chip = lax.axis_index("core"), lax.axis_index("dir_1"), lax.axis_index("chip")
     turned = jnp.where(core == 0, chip % RUN == 0, chip % RUN == RUN - 1).astype(jnp.int32)
     own = order_ref[...]
@@ -153,84 +162,45 @@
     edge_ref[...] = jnp.where(core == 0, sources[CELLS - HALO : CELLS], sources[:HALO]).astype(BF16)
 
 
-def to_cells(received, order, done):
+def to_cells(received, order):
     return pl.pallas_call(
         cells_kernel,
-        in_specs=[whole()] * 3,
+        in_specs=[whole()] * 2,
         out_specs=[whole()] * 2,
         out_shape=(
             jax.ShapeDtypeStruct((2 * CELLS, WIDE), BF16),
             jax.ShapeDtypeStruct((HALO, WIDE), BF16),
         ),
         compiler_params=params(),
-    )(received, order, done)
-
-
-def choose(index, ops, out_ref):
+    )(received, order)
+
+
+def by_part_columns(ops):
     ops = ops.astype(F32)
-    ops = jnp.concatenate([ops[:, 0], ops[:, 1]], axis=1).astype(BF16)
-    lanes = lax.broadcasted_iota(jnp.int32, (CELLS, BAND), 1)
-    step = 8
-    for j0 in range(0, ENTRIES, step):
-        picks = [
-            jnp.where(index[:, j : j + 1] == lanes, 1.0, 0.0).astype(BF16)
-            for j in range(j0, j0 + step)
-        ]
-        chosen = jnp.dot(jnp.concatenate(picks, axis=0), ops, preferred_element_type=F32)
-        out_ref[j0 * CELLS : (j0 + step) * CELLS] = chosen.astype(BF16)
-
-
-def own_operators_kernel(index_hbm, ops_hbm, out_ref, done_ref, index_ref, ops_ref, sems):
-    loads = [
-        pltpu.make_async_copy(index_hbm, index_ref, sems.at[0]),
-        pltpu.make_async_copy(ops_hbm, ops_ref, sems.at[1]),
+    return jnp.concatenate([ops[:, 0], ops[:, 1]], axis=1).astype(BF16)
+
+
+def onehot_rows(positions, width, first, rows):
+    lanes = lax.broadcasted_iota(jnp.int32, (rows, width), 1)
+    picks = [
+        jnp.where(positions[first : first + rows, j : j + 1] == lanes, 1.0, 0.0).astype(BF16) for j in range(ENTRIES)
     ]
-    for load in loads:
-        load.start()
-    for load in loads:
-        load.wait()
-    choose(index_ref[...], ops_ref[...], out_ref)
-    done_ref[...] = jnp.zeros_like(done_ref)
-
-
-def other_operators_kernel(index_ref, ops_ref, out_ref):
-    choose(index_ref[...], ops_ref[...], out_ref)
-
-
-CHOICE = pl.CostEstimate(flops=2 * ENTRIES * CELLS * 128 * 256, bytes_accessed=ENTRIES * CELLS * 512, transcendentals=0)
-
-
-def own_operators(index, ops):
-    return pl.pallas_call(
-        own_operators_kernel,
-        in_specs=[outer()] * 2,
-        out_specs=[whole()] * 2,
-        out_shape=(
-            jax.ShapeDtypeStruct((ENTRIES * CELLS, 2 * BAND), BF16),
-            jax.ShapeDtypeStruct((8, BAND), F32),
-        ),
-        scratch_shapes=[
-            pltpu.VMEM((CELLS, ENTRIES), jnp.int32),
-            pltpu.VMEM((128, 2, BAND), BF16),
-            pltpu.SemaphoreType.DMA((2,)),
-        ],
-        compiler_params=params(),
-        cost_estimate=CHOICE,
-    )(*in_hbm(index, ops))
-
-
-def other_operators(index, ops):
-    return pl.pallas_call(
-        other_operators_kernel,
-        in_specs=[whole()] * 2,
-        out_specs=whole(),
-        out_shape=jax.ShapeDtypeStruct((ENTRIES * CELLS, 2 * BAND), BF16),
-        compiler_params=params(),
-        cost_estimate=CHOICE,
-    )(index, ops)
-
-
-def translate_kernel(sources_ref, edge_ref, code_ref, own_ref, other_ref, order_ref, out_ref):
+    return jnp.concatenate(picks, axis=0)
+
+
+def added_up(fields, ops):
+    re = jnp.zeros((GROUP, BAND), F32)
+    im = re
+    for j in range(ENTRIES):
+        at = slice(j * GROUP, (j + 1) * GROUP)
+        f, w = fields[at], ops[at]
+        fr, fi, wr, wi = f[:, :BAND], f[:, BAND:], w[:, :BAND], w[:, BAND:]
+        re = re + (wr * fr - wi * fi)
+        im = im + (wr * fi + wi * fr)
+    return jnp.concatenate([re, im], axis=1)
+
+
+def translate_kernel(sources_ref, edge_ref, code_ref, index_ref, own_ref, other_ref, order_ref, out_ref):
     core, half = lax.axis_index("core"), lax.axis_index("dir_1")
     edge = edge_ref[...].astype(F32)
     outside = sources_ref[CELLS:].astype(F32)
@@ -239,35 +209,29 @@
     edges = jnp.where(core == 0, first, second).astype(BF16)
     sources = jnp.concatenate([sources_ref[:CELLS], edges], axis=0)
     low, high = sources[:, : 2 * BAND], sources[:, 2 * BAND :]
-    sides = ((jnp.where(half == 0, low, high), own_ref), (jnp.where(half == 0, high, low), other_ref))
-
-    code = code_ref[...]
+    own_ops, other_ops = by_part_columns(own_ref[...]), by_part_columns(other_ref[...])
+    sides = (
+        (low, jnp.where(half == 0, own_ops, other_ops)),
+        (high, jnp.where(half == 0, other_ops, own_ops)),
+    )
+
+    code, index = code_ref[...], index_ref[...]
     cell = lax.broadcasted_iota(jnp.int32, code.shape, 0)
     up = (code * 37) >> 8
     u = (cell >> 4) + up - 3
     v = ((cell & 15) + code - 7 * up + (COLS - 3)) & 15
     source = (u & 7) * COLS + v + jnp.where((u < 0) | (u > 7), CELLS, 0)
-    lanes = lax.broadcasted_iota(jnp.int32, (CELLS, 2 * CELLS), 1)
-    totals = [jnp.zeros((CELLS, BAND), F32)] * 4
-    step = 8
-    for j0 in range(0, ENTRIES, step):
-        picks = [
-            jnp.where(source[:, j : j + 1] == lanes, 1.0, 0.0).astype(BF16)
-            for j in range(j0, j0 + step)
-        ]
-        picks = jnp.concatenate(picks, axis=0)
-        for h, (fields, chosen_ref) in enumerate(sides):
+    totals = []
+    for k in range(CELLS // GROUP):
+        picks = onehot_rows(source, 2 * CELLS, k * GROUP, GROUP)
+        choices = onehot_rows(index, NOPS, k * GROUP, GROUP)
+        both = []
+        for fields, ops in sides:
             got = jnp.dot(picks, fields, preferred_element_type=F32)
-            re, im = totals[2 * h : 2 * h + 2]
-            for k in range(step):
-                op = chosen_ref[(j0 + k) * CELLS : (j0 + k + 1) * CELLS].astype(F32)
-                g = got[k * CELLS : (k + 1) * CELLS]
-                gr, gi, wr, wi = g[:, :BAND], g[:, BAND:], op[:, :BAND], op[:, BAND:]
-                re = re + (wr * gr - wi * gi)
-                im = im + (wr * gi + wi * gr)
-            totals[2 * h : 2 * h + 2] = re, im
-    own, other = jnp.concatenate(totals[:2], axis=1), jnp.concatenate(totals[2:], axis=1)
-    translated = jnp.concatenate([jnp.where(half == 0, own, other), jnp.where(half == 0, other, own)], axis=1).astype(BF16)
+            chosen = jnp.dot(choices, ops, preferred_element_type=F32)
+            both.append(added_up(got, chosen))
+        totals.append(jnp.concatenate(both, axis=1))
+    translated = jnp.concatenate(totals, axis=0).astype(BF16)
     rows = lax.broadcasted_iota(jnp.int32, (CELLS, CELLS), 0)
     onehot = jnp.where(rows == order_ref[...], 1.0, 0.0).astype(BF16)
     out_ref[...] = jnp.dot(onehot, translated, preferred_element_type=F32).astype(BF16)
@@ -276,7 +240,7 @@
 def translate(*args):
     return pl.pallas_call(
         translate_kernel,
-        in_specs=[whole()] * 6,
+        in_specs=[whole()] * 7,
         out_specs=whole(),
         out_shape=jax.ShapeDtypeStruct((CELLS, WIDE), BF16),
         compiler_params=params(),
@@ -346,14 +310,9 @@
         send, DIR + ("chip", "core"), 0, 0, axis_index_groups=neighbour_groups(chips), tiled=True
     )
     index = operator_index.reshape(CELLS, ENTRIES)
-    chosen, done = own_operators(index, operators)
-    sources, edge = to_cells(received.reshape(CELLS, WIDE + BAND), patch_order, done)
-    edge, index = lax.optimization_barrier((edge, index))
-    chosen_other = other_operators(index, other)
+    sources, edge = to_cells(received.reshape(CELLS, WIDE + BAND), patch_order)
     edge = lax.ppermute(edge, "core", [(0, 1), (1, 0)])
-    returned = translate(
-        sources, edge, offset_code.reshape(CELLS, ENTRIES), chosen, chosen_other, patch_order
-    )
+    returned = translate(sources, edge, offset_code.reshape(CELLS, ENTRIES), index, operators, other, patch_order)
     back = lax.all_to_all(returned.reshape(DBLOCKS, 8, WIDE), DIR, 0, 0, tiled=True)
     fields = anterpolate(back.reshape(8 * DBLOCKS, WIDE), interp_matrix, c, s)
     return fields.reshape(8, CHILDREN, 2, DC)

time: 56.5 us -> 55.8 us (0.988); the launches traced: 55.4 us -> 55.5 us
  Pallas kernels: 10.9 us -> 8.4 us
  waiting for transfers between devices: 0.01 us -> 1.42 us
  starting transfers between devices: 27.3 us -> 28.6 us
    pallas_call x5 -> x3, Pallas kernels: 9.27 us -> 6.75 us  [the longest x1 3.41 us: translate(): pl.pallas_call(translate_kernel, in_specs=[whole()] * 7, out_specs=whole(...]
    ppermute x1, starting transfers between devices: 7.3 us -> 8.73 us  [per_device(): edge = lax.ppermute(edge, 'core', [(0, 1), (1, 0)])]
    ppermute x1, waiting for transfers between devices: 0.01 us -> 0.85 us  [per_device(): edge = lax.ppermute(edge, 'core', [(0, 1), (1, 0)])]
    all_to_all x1, waiting for transfers between devices: 0.01 us -> 0.57 us  [per_device(): lax.all_to_all(send, DIR + ('chip', 'core'), 0, 0, axis_index_groups=neig...]
  transfers between devices with their start and end apart: 3 -> 3, of which waited for: 0 -> 2; matrix products, arithmetic and copies ran while one was open for 0% -> 0% of each run, Pallas kernels for 6% -> 1%
where the time goes in v7:
time: 55.8 us; the launch traced here: 55.5 us
  starting transfers between devices  28.6 us (51%)
  blocking collectives  17 us (30%)
  Pallas kernels  8.4 us (15%)
  waiting for transfers between devices  1.42 us (3%)
    all_to_all x1, blocking collectives, per_device(): lax.all_to_all(returned.reshape(DBLOCKS, 8, WIDE), DIR, 0, 0, tiled=True)  17 us
    all_to_all x1, starting transfers between devices, per_device(): lax.all_to_all(send, DIR + ('chip', 'core'), 0, 0, axis_index_groups=neig...  10.1 us
    ppermute x1, starting transfers between devices, per_device(): lax.ppermute(operators, ('dir_1', 'chip', 'core'), other_half(chips))  9.76 us
    ppermute x1, starting transfers between devices, per_device(): edge = lax.ppermute(edge, 'core', [(0, 1), (1, 0)])  8.73 us
    pallas_call x1, Pallas kernels, translate(): pl.pallas_call(translate_kernel, in_specs=[whole()] * 7, out_specs=whole(...  3.41 us
    pallas_call x1, Pallas kernels, front(): pl.pallas_call(front_kernel, in_specs=[outer()] * 4, out_specs=[outer(),...  3.05 us
    pallas_call x1, Pallas kernels, anterpolate(): pl.pallas_call(anterpolate_kernel, in_specs=[whole()] * 4, out_specs=whol...  1.65 us
  transfers between devices with their start and end apart: 3, of which 2 were waited for; matrix products, arithmetic and copies ran while one was open for 0% of the time, Pallas kernels for 1%

profile of v7, /device:TPU:1, one launch (start us, length us, event | category | flops | bytes accessed | tf_op | source)
XLA Modules:
  0.0 55.5 jit_solution(11962125640626671003)
XLA Ops:
  0.0 0.0 copy-start.4
  0.0 0.0 copy-start
  0.0 0.0 copy-start.3
  0.0 0.0 copy-start.1
  0.0 0.0 copy-start.2
  0.0 3.1 %shard_map.73 = (bf16[16,8,640]{2,1,0:T(8,128)(2,1)}, f32[8,2048]{1,0:T(8,128)S(1)}, f32[8,2048]{1,0:T(8,128)S(1)}) custom-call(bf16[64,2,512]{2,1,0:T(2,128)(2,1)} %bitcast.12, s32[1,128]{1,0:T(1,128)} %order_ref.3, f32[8,2048]{1,0:T(8,128)} %phase_hbm.1, bf16[512,2048]{1,0:T(8,128)(2,1)} %interp_ref.1), custom_call_target="tpu_custom_call" | custom-call | flops 268435456 | bytes 2097152 | tf_op jit(solution)/shard_map/pallas_call | solution.py:125
  3.1 10.1 %all-to-all-start = ((bf16[16,8,640]{2,1,0:T(8,128)(2,1)}), bf16[16,8,640]{2,1,0:T(8,128)(2,1)S(1)}, u32[]{:S(2)}, u32[]{:S(2)}) async-start(bf16[16,8,640]{2,1,0:T(8,128)(2,1)} %get-tuple-element.10), calls=%async_computation | async-start | bytes 327680 | tf_op jit(solution)/shard_map/all_to_all | solution.py:309
  13.2 0.0 copy-done.3
  13.2 9.8 %collective-permute-start.1 = (bf16[128,2,128]{2,1,0:T(2,128)(2,1)S(1)}, bf16[128,2,128]{2,1,0:T(2,128)(2,1)S(1)}, u32[]{:S(2)}, u32[]{:S(2)}) collective-permute-start(bf16[128,2,128]{2,1,0:T(2,128)(2,1)S(1)} %copy-done.3), channel_id=1, source_target_pairs={{0,36},{1,37},{2,38},{3,39},{4,32},{5,33},{6,34},{7,35},{8,44},{9,... | collective-permute-start | bytes 196616 | tf_op jit(solution)/shard_map/ppermute | solution.py:307
  23.0 0.6 %all-to-all-done = bf16[16,8,640]{2,1,0:T(8,128)(2,1)S(1)} async-done(((bf16[16,8,640]{2,1,0:T(8,128)(2,1)}), bf16[16,8,640]{2,1,0:T(8,128)(2,1)S(1)}, u32[]{:S(2)}, u32[]{:S(2)}) %all-to-all-start) | async-done | bytes 163872 | tf_op jit(solution)/shard_map/all_to_all | solution.py:309
  23.6 0.0 copy-done.4
  23.6 0.3 shard_map.74
  23.9 8.7 %collective-permute-start = (bf16[48,512]{1,0:T(8,128)(2,1)S(1)}, bf16[48,512]{1,0:T(8,128)(2,1)S(1)}, u32[]{:S(2)}, u32[]{:S(2)}) collective-permute-start(bf16[48,512]{1,0:T(8,128)(2,1)S(1)} %get-tuple-element.12), channel_id=1, source_target_pairs={{0,1},{1,0},{2,3},{3,2},{4,5},{5,4},{6,7},{7,6},{8,9},{9,8},{10,11... | collective-permute-start | bytes 147464 | tf_op jit(solution)/shard_map/ppermute | solution.py:314
  32.6 0.0 collective-permute-done.1.other_ref
  32.6 0.8 %collective-permute-done.edge_ref = bf16[48,512]{1,0:T(8,128)(2,1)S(1)} collective-permute-done((bf16[48,512]{1,0:T(8,128)(2,1)S(1)}, bf16[48,512]{1,0:T(8,128)(2,1)S(1)}, u32[]{:S(2)}, u32[]{:S(2)}) %collective-permute-start) | collective-permute-done | bytes 49184 | tf_op jit(solution)/shard_map/ppermute | solution.py:314
  33.5 0.0 copy-done.1
  33.5 0.0 copy-done.2
  33.5 3.4 %shard_map.75 = bf16[128,512]{1,0:T(8,128)(2,1)S(1)} custom-call(bf16[256,512]{1,0:T(8,128)(2,1)S(1)} %get-tuple-element.11.sources_ref, bf16[48,512]{1,0:T(8,128)(2,1)S(1)} %collective-permute-done.edge_ref, s32[128,40]{1,0:T(8,128)S(1)} %bitcast.10, s32[128,40]{1,0:T(8,128)S(1)} %bitcast.11, bf16[128,2,128]{2,1,0:T(2,128)(2,1)S(1)} %copy-done.3, ...), custom_call_target="tpu_custom_call" | custom-call | tf_op jit(solution)/shard_map/pallas_call | solution.py:241
  36.9 17.0 %all_to_all.10 = bf16[16,8,512]{2,1,0:T(8,128)(2,1)S(1)} all-to-all(bf16[16,8,512]{2,1,0:T(8,128)(2,1)S(1)} %bitcast.9), channel_id=1, replica_groups=mesh['dir_0'=8,'dir_1'=2,'chip'=16,'core'=2] {'dir_0','dir_1'}, dimensions={0} | all-to-all | bytes 262144 | tf_op jit(solution)/shard_map/all_to_all | solution.py:316
  53.9 0.0 copy-done
  53.9 1.7 %shard_map.76 = bf16[64,2,512]{2,1,0:T(2,128)(2,1)} custom-call(bf16[128,512]{1,0:T(8,128)(2,1)S(1)} %bitcast.8, bf16[512,2048]{1,0:T(8,128)(2,1)S(1)} %copy-done, f32[8,2048]{1,0:T(8,128)S(1)} %get-tuple-element.13.cos_ref, f32[8,2048]{1,0:T(8,128)S(1)} %get-tuple-element.14.sin_ref), custom_call_target="tpu_custom_call" | custom-call | tf_op jit(solution)/shard_map/pallas_call | solution.py:277
Async XLA Ops:
  0.0 23.6 %copy-start.4 = (s32[1,128]{1,0:T(1,128)S(1)}, s32[1,128]{1,0:T(1,128)}, u32[]{:S(2)}) copy-start(s32[1,128]{1,0:T(1,128)} %order_ref.3) | copy-start | bytes 1540
  0.0 53.9 %copy-start = (bf16[512,2048]{1,0:T(8,128)(2,1)S(1)}, bf16[512,2048]{1,0:T(8,128)(2,1)}, u32[]{:S(2)}) copy-start(bf16[512,2048]{1,0:T(8,128)(2,1)} %interp_ref.1) | copy-start | bytes 6291460
  0.0 13.2 %copy-start.3 = (bf16[128,2,128]{2,1,0:T(2,128)(2,1)S(1)}, bf16[128,2,128]{2,1,0:T(2,128)(2,1)}, u32[]{:S(2)}) copy-start(bf16[128,2,128]{2,1,0:T(2,128)(2,1)} %own_ref.1) | copy-start | bytes 196612
  0.0 33.5 %copy-start.1 = (s32[8,16,40]{2,1,0:T(8,128)S(1)}, s32[8,16,40]{2,1,0:T(8,128)}, u32[]{:S(2)}) copy-start(s32[8,16,40]{2,1,0:T(8,128)} %param.11) | copy-start | bytes 61444
  0.0 33.5 %copy-start.2 = (s32[8,16,40]{2,1,0:T(8,128)S(1)}, s32[8,16,40]{2,1,0:T(8,128)}, u32[]{:S(2)}) copy-start(s32[8,16,40]{2,1,0:T(8,128)} %param.12) | copy-start | bytes 61444
  3.1 20.5 %all-to-all-start = ((bf16[16,8,640]{2,1,0:T(8,128)(2,1)}), bf16[16,8,640]{2,1,0:T(8,128)(2,1)S(1)}, u32[]{:S(2)}, u32[]{:S(2)}) async-start(bf16[16,8,640]{2,1,0:T(8,128)(2,1)} %get-tuple-element.10), calls=%async_computation | async-start | bytes 327680 | tf_op jit(solution)/shard_map/all_to_all | solution.py:309
  13.2 19.4 %collective-permute-start.1 = (bf16[128,2,128]{2,1,0:T(2,128)(2,1)S(1)}, bf16[128,2,128]{2,1,0:T(2,128)(2,1)S(1)}, u32[]{:S(2)}, u32[]{:S(2)}) collective-permute-start(bf16[128,2,128]{2,1,0:T(2,128)(2,1)S(1)} %copy-done.3), channel_id=1, source_target_pairs={{0,36},{1,37},{2,38},{3,39},{4,32},{5,33},{6,34},{7,35},{8,44},{9,... | collective-permute-start | bytes 196616 | tf_op jit(solution)/shard_map/ppermute | solution.py:307
  23.9 9.6 %collective-permute-start = (bf16[48,512]{1,0:T(8,128)(2,1)S(1)}, bf16[48,512]{1,0:T(8,128)(2,1)S(1)}, u32[]{:S(2)}, u32[]{:S(2)}) collective-permute-start(bf16[48,512]{1,0:T(8,128)(2,1)S(1)} %get-tuple-element.12), channel_id=1, source_target_pairs={{0,1},{1,0},{2,3},{3,2},{4,5},{5,4},{6,7},{7,6},{8,9},{9,8},{10,11... | collective-permute-start | bytes 147464 | tf_op jit(solution)/shard_map/ppermute | solution.py:314

commit v8 on v7

--- a/solution.py
+++ b/solution.py
@@ -21,6 +21,8 @@
 RUN = 4
 TILE = 512
 TILES = DP // TILE
+FRONT_TILE = 1024
+FRONT_TILES = DP // FRONT_TILE
 DIR = ("dir_0", "dir_1")
 F32 = jnp.float32
 BF16 = jnp.bfloat16
@@ -90,8 +92,8 @@
 ):
     small = [(child_hbm, child_ref), (order_hbm, order_ref), (phase_hbm, phase_ref)]
     loads = [pltpu.make_async_copy(there, here, sems.at[k]) for k, (there, here) in enumerate(small)]
-    for t in range(TILES):
-        at = pl.ds(t * TILE, TILE)
+    for t in range(FRONT_TILES):
+        at = pl.ds(t * FRONT_TILE, FRONT_TILE)
         loads.append(pltpu.make_async_copy(interp_hbm.at[:, at], interp_ref.at[:, at], sems.at[len(small) + t]))
     for load in loads:
         load.start()
@@ -104,8 +106,8 @@
     cos_ref[...] = c
     sin_ref[...] = s
     stores = []
-    for t in range(TILES):
-        at = slice(t * TILE, (t + 1) * TILE)
+    for t in range(FRONT_TILES):
+        at = slice(t * FRONT_TILE, (t + 1) * FRONT_TILE)
         loads[len(small) + t].wait()
         blocks = block_fields(child, interp_ref[:, at], c[:, at], s[:, at])
         for k in range(0, len(blocks), 2):
@@ -114,7 +116,7 @@
             send_ref[at] = out
             send_ref[at + 1] = out
         here = pl.ds(t * len(blocks), len(blocks))
-        stores.append(pltpu.make_async_copy(send_ref.at[here], send_hbm.at[here], sems.at[len(small) + TILES + t]))
+        stores.append(pltpu.make_async_copy(send_ref.at[here], send_hbm.at[here], sems.at[len(small) + FRONT_TILES + t]))
         stores[t].start()
     for store in stores:
         store.wait()
@@ -137,7 +139,7 @@
             pltpu.VMEM((CHILDREN, DP), F32),
             pltpu.VMEM((DC, DP), BF16),
             pltpu.VMEM((DBLOCKS, 8, WIDE + BAND), BF16),
-            pltpu.SemaphoreType.DMA((2 * TILES + 3,)),
+            pltpu.SemaphoreType.DMA((2 * FRONT_TILES + 3,)),
         ],
         compiler_params=params(),
         cost_estimate=pl.CostEstimate(flops=2 * 128 * DC * DP, bytes_accessed=DC * DP * 2, transcendentals=0),
@@ -233,7 +235,9 @@
         totals.append(jnp.concatenate(both, axis=1))
     translated = jnp.concatenate(totals, axis=0).astype(BF16)
     rows = lax.broadcasted_iota(jnp.int32, (CELLS, CELLS), 0)
-    onehot = jnp.where(rows == order_ref[...], 1.0, 0.0).astype(BF16)
+    place = order_ref[...]
+    place = ((place >> 3) & 1) * 64 + (place >> 4) * 8 + (place & 7)
+    onehot = jnp.where(rows == place, 1.0, 0.0).astype(BF16)
     out_ref[...] = jnp.dot(onehot, translated, preferred_element_type=F32).astype(BF16)
 
 
@@ -250,13 +254,15 @@
 def anterpolate_kernel(recv_ref, interp_ref, cos_ref, sin_ref, out_ref):
     total = jnp.zeros((128, DC), F32)
     per_tile = TILE // (2 * BAND)
+    halves = recv_ref[...].astype(F32).reshape(2, 64, WIDE)
     for t in range(TILES):
         at = slice(t * TILE, (t + 1) * TILE)
         c, s = cos_ref[:, at], sin_ref[:, at]
-        values = recv_ref[16 * per_tile * t : 16 * per_tile * (t + 1)].astype(F32)
+        rows = slice(8 * per_tile * t, 8 * per_tile * (t + 1))
+        values = halves[0, rows] + halves[1, rows]
         re, im = [], []
         for y in range(per_tile):
-            both = values[16 * y : 16 * y + 8] + values[16 * y + 8 : 16 * y + 16]
+            both = values[8 * y : 8 * y + 8]
             re += [both[:, :BAND], both[:, 2 * BAND : 3 * BAND]]
             im += [both[:, BAND : 2 * BAND], both[:, 3 * BAND :]]
         re, im = jnp.concatenate(re, axis=1), jnp.concatenate(im, axis=1)
@@ -293,6 +299,11 @@
     return groups
 
 
+def patch_groups(chips):
+    size = 2 * chips
+    return [[(2 * y + half) * size + box for half in range(2) for y in range(DBLOCKS // 2)] for box in range(size)]
+
+
 def other_half(chips):
     pairs = []
     for half in range(2):
@@ -313,7 +324,9 @@
     sources, edge = to_cells(received.reshape(CELLS, WIDE + BAND), patch_order)
     edge = lax.ppermute(edge, "core", [(0, 1), (1, 0)])
     returned = translate(sources, edge, offset_code.reshape(CELLS, ENTRIES), index, operators, other, patch_order)
-    back = lax.all_to_all(returned.reshape(DBLOCKS, 8, WIDE), DIR, 0, 0, tiled=True)
+    back = lax.all_to_all(
+        returned.reshape(DBLOCKS, 8, WIDE), DIR + ("chip", "core"), 0, 0, axis_index_groups=patch_groups(chips), tiled=True
+    )
     fields = anterpolate(back.reshape(8 * DBLOCKS, WIDE), interp_matrix, c, s)
     return fields.reshape(8, CHILDREN, 2, DC)
 

time: 55.8 us -> 55.3 us (level); the launches traced: 55.5 us -> 54.3 us
  blocking collectives: 17 us -> 16 us
    all_to_all x1, blocking collectives: 17 us -> 16 us  [per_device(): lax.all_to_all(returned.reshape(DBLOCKS, 8, WIDE), DIR + ('chip', 'core')...]
where the time goes in v8:
time: 55.3 us; the launch traced here: 54.3 us
  starting transfers between devices  28.6 us (52%)
  blocking collectives  16 us (29%)
  Pallas kernels  8.2 us (15%)
  waiting for transfers between devices  1.43 us (3%)
    all_to_all x1, blocking collectives, per_device(): lax.all_to_all(returned.reshape(DBLOCKS, 8, WIDE), DIR + ('chip', 'core')...  16 us
    all_to_all x1, starting transfers between devices, per_device(): lax.all_to_all(send, DIR + ('chip', 'core'), 0, 0, axis_index_groups=neig...  10.1 us
    ppermute x1, starting transfers between devices, per_device(): lax.ppermute(operators, ('dir_1', 'chip', 'core'), other_half(chips))  9.75 us
    ppermute x1, starting transfers between devices, per_device(): edge = lax.ppermute(edge, 'core', [(0, 1), (1, 0)])  8.73 us
    pallas_call x1, Pallas kernels, translate(): pl.pallas_call(translate_kernel, in_specs=[whole()] * 7, out_specs=whole(...  3.41 us
    pallas_call x1, Pallas kernels, front(): pl.pallas_call(front_kernel, in_specs=[outer()] * 4, out_specs=[outer(),...  2.85 us
    pallas_call x1, Pallas kernels, anterpolate(): pl.pallas_call(anterpolate_kernel, in_specs=[whole()] * 4, out_specs=whol...  1.65 us
  transfers between devices with their start and end apart: 3, of which 2 were waited for; matrix products, arithmetic and copies ran while one was open for 0% of the time, Pallas kernels for 1%

profile of v8, /device:TPU:1, one launch (start us, length us, event | category | flops | bytes accessed | tf_op | source)
XLA Modules:
  0.0 54.3 jit_solution(123311113120157160)
XLA Ops:
  0.0 0.0 copy-start.4
  0.0 0.0 copy-start
  0.0 0.0 copy-start.3
  0.0 0.0 copy-start.1
  0.0 0.0 copy-start.2
  0.0 2.9 %shard_map.73 = (bf16[16,8,640]{2,1,0:T(8,128)(2,1)}, f32[8,2048]{1,0:T(8,128)S(1)}, f32[8,2048]{1,0:T(8,128)S(1)}) custom-call(bf16[64,2,512]{2,1,0:T(2,128)(2,1)} %bitcast.12, s32[1,128]{1,0:T(1,128)} %order_ref.3, f32[8,2048]{1,0:T(8,128)} %phase_hbm.1, bf16[512,2048]{1,0:T(8,128)(2,1)} %interp_ref.1), custom_call_target="tpu_custom_call" | custom-call | flops 268435456 | bytes 2097152 | tf_op jit(solution)/shard_map/pallas_call | solution.py:127
  2.9 10.1 %all-to-all-start = ((bf16[16,8,640]{2,1,0:T(8,128)(2,1)}), bf16[16,8,640]{2,1,0:T(8,128)(2,1)S(1)}, u32[]{:S(2)}, u32[]{:S(2)}) async-start(bf16[16,8,640]{2,1,0:T(8,128)(2,1)} %get-tuple-element.10), calls=%async_computation | async-start | bytes 327680 | tf_op jit(solution)/shard_map/all_to_all | solution.py:320
  13.0 0.0 copy-done.3
  13.0 9.8 %collective-permute-start.1 = (bf16[128,2,128]{2,1,0:T(2,128)(2,1)S(1)}, bf16[128,2,128]{2,1,0:T(2,128)(2,1)S(1)}, u32[]{:S(2)}, u32[]{:S(2)}) collective-permute-start(bf16[128,2,128]{2,1,0:T(2,128)(2,1)S(1)} %copy-done.3), channel_id=1, source_target_pairs={{0,36},{1,37},{2,38},{3,39},{4,32},{5,33},{6,34},{7,35},{8,44},{9,... | collective-permute-start | bytes 196616 | tf_op jit(solution)/shard_map/ppermute | solution.py:318
  22.8 0.6 %all-to-all-done = bf16[16,8,640]{2,1,0:T(8,128)(2,1)S(1)} async-done(((bf16[16,8,640]{2,1,0:T(8,128)(2,1)}), bf16[16,8,640]{2,1,0:T(8,128)(2,1)S(1)}, u32[]{:S(2)}, u32[]{:S(2)}) %all-to-all-start) | async-done | bytes 163872 | tf_op jit(solution)/shard_map/all_to_all | solution.py:320
  23.4 0.0 copy-done.4
  23.4 0.3 shard_map.74
  23.7 8.7 %collective-permute-start = (bf16[48,512]{1,0:T(8,128)(2,1)S(1)}, bf16[48,512]{1,0:T(8,128)(2,1)S(1)}, u32[]{:S(2)}, u32[]{:S(2)}) collective-permute-start(bf16[48,512]{1,0:T(8,128)(2,1)S(1)} %get-tuple-element.12), channel_id=1, source_target_pairs={{0,1},{1,0},{2,3},{3,2},{4,5},{5,4},{6,7},{7,6},{8,9},{9,8},{10,11... | collective-permute-start | bytes 147464 | tf_op jit(solution)/shard_map/ppermute | solution.py:325
  32.4 0.0 collective-permute-done.1.other_ref
  32.4 0.8 %collective-permute-done.edge_ref = bf16[48,512]{1,0:T(8,128)(2,1)S(1)} collective-permute-done((bf16[48,512]{1,0:T(8,128)(2,1)S(1)}, bf16[48,512]{1,0:T(8,128)(2,1)S(1)}, u32[]{:S(2)}, u32[]{:S(2)}) %collective-permute-start) | collective-permute-done | bytes 49184 | tf_op jit(solution)/shard_map/ppermute | solution.py:325
  33.3 0.0 copy-done.1
  33.3 0.0 copy-done.2
  33.3 3.4 %shard_map.75 = bf16[128,512]{1,0:T(8,128)(2,1)S(1)} custom-call(bf16[256,512]{1,0:T(8,128)(2,1)S(1)} %get-tuple-element.11.sources_ref, bf16[48,512]{1,0:T(8,128)(2,1)S(1)} %collective-permute-done.edge_ref, s32[128,40]{1,0:T(8,128)S(1)} %bitcast.10, s32[128,40]{1,0:T(8,128)S(1)} %bitcast.11, bf16[128,2,128]{2,1,0:T(2,128)(2,1)S(1)} %copy-done.3, ...), custom_call_target="tpu_custom_call" | custom-call | tf_op jit(solution)/shard_map/pallas_call | solution.py:245
  36.7 16.0 %all_to_all.10 = bf16[16,8,512]{2,1,0:T(8,128)(2,1)S(1)} all-to-all(bf16[16,8,512]{2,1,0:T(8,128)(2,1)S(1)} %bitcast.9), channel_id=1, replica_groups={{0,64,128,192,256,320,384,448,32,96,160,224,288,352,416,480},{1,65,129,..., dimensions={0} | all-to-all | bytes 262144 | tf_op jit(solution)/shard_map/all_to_all | solution.py:327
  52.7 0.0 copy-done
  52.7 1.7 %shard_map.76 = bf16[64,2,512]{2,1,0:T(2,128)(2,1)} custom-call(bf16[128,512]{1,0:T(8,128)(2,1)S(1)} %bitcast.8, bf16[512,2048]{1,0:T(8,128)(2,1)S(1)} %copy-done, f32[8,2048]{1,0:T(8,128)S(1)} %get-tuple-element.13.cos_ref, f32[8,2048]{1,0:T(8,128)S(1)} %get-tuple-element.14.sin_ref), custom_call_target="tpu_custom_call" | custom-call | tf_op jit(solution)/shard_map/pallas_call | solution.py:283
Async XLA Ops:
  0.0 23.4 %copy-start.4 = (s32[1,128]{1,0:T(1,128)S(1)}, s32[1,128]{1,0:T(1,128)}, u32[]{:S(2)}) copy-start(s32[1,128]{1,0:T(1,128)} %order_ref.3) | copy-start | bytes 1540
  0.0 52.7 %copy-start = (bf16[512,2048]{1,0:T(8,128)(2,1)S(1)}, bf16[512,2048]{1,0:T(8,128)(2,1)}, u32[]{:S(2)}) copy-start(bf16[512,2048]{1,0:T(8,128)(2,1)} %interp_ref.1) | copy-start | bytes 6291460
  0.0 13.0 %copy-start.3 = (bf16[128,2,128]{2,1,0:T(2,128)(2,1)S(1)}, bf16[128,2,128]{2,1,0:T(2,128)(2,1)}, u32[]{:S(2)}) copy-start(bf16[128,2,128]{2,1,0:T(2,128)(2,1)} %own_ref.1) | copy-start | bytes 196612
  0.0 33.3 %copy-start.1 = (s32[8,16,40]{2,1,0:T(8,128)S(1)}, s32[8,16,40]{2,1,0:T(8,128)}, u32[]{:S(2)}) copy-start(s32[8,16,40]{2,1,0:T(8,128)} %param.11) | copy-start | bytes 61444
  0.0 33.3 %copy-start.2 = (s32[8,16,40]{2,1,0:T(8,128)S(1)}, s32[8,16,40]{2,1,0:T(8,128)}, u32[]{:S(2)}) copy-start(s32[8,16,40]{2,1,0:T(8,128)} %param.12) | copy-start | bytes 61444
  2.9 20.5 %all-to-all-start = ((bf16[16,8,640]{2,1,0:T(8,128)(2,1)}), bf16[16,8,640]{2,1,0:T(8,128)(2,1)S(1)}, u32[]{:S(2)}, u32[]{:S(2)}) async-start(bf16[16,8,640]{2,1,0:T(8,128)(2,1)} %get-tuple-element.10), calls=%async_computation | async-start | bytes 327680 | tf_op jit(solution)/shard_map/all_to_all | solution.py:320
  13.0 19.4 %collective-permute-start.1 = (bf16[128,2,128]{2,1,0:T(2,128)(2,1)S(1)}, bf16[128,2,128]{2,1,0:T(2,128)(2,1)S(1)}, u32[]{:S(2)}, u32[]{:S(2)}) collective-permute-start(bf16[128,2,128]{2,1,0:T(2,128)(2,1)S(1)} %copy-done.3), channel_id=1, source_target_pairs={{0,36},{1,37},{2,38},{3,39},{4,32},{5,33},{6,34},{7,35},{8,44},{9,... | collective-permute-start | bytes 196616 | tf_op jit(solution)/shard_map/ppermute | solution.py:318
  23.7 9.6 %collective-permute-start = (bf16[48,512]{1,0:T(8,128)(2,1)S(1)}, bf16[48,512]{1,0:T(8,128)(2,1)S(1)}, u32[]{:S(2)}, u32[]{:S(2)}) collective-permute-start(bf16[48,512]{1,0:T(8,128)(2,1)S(1)} %get-tuple-element.12), channel_id=1, source_target_pairs={{0,1},{1,0},{2,3},{3,2},{4,5},{5,4},{6,7},{7,6},{8,9},{9,8},{10,11... | collective-permute-start | bytes 147464 | tf_op jit(solution)/shard_map/ppermute | solution.py:325

commit v9 on v8

--- a/solution.py
+++ b/solution.py
@@ -251,8 +251,8 @@
     )(*args)
 
 
-def anterpolate_kernel(recv_ref, interp_ref, cos_ref, sin_ref, out_ref):
-    total = jnp.zeros((128, DC), F32)
+def anterpolate_kernel(recv_ref, interp_ref, cos_ref, sin_ref, out_hbm, out_ref, sems):
+    shifted = []
     per_tile = TILE // (2 * BAND)
     halves = recv_ref[...].astype(F32).reshape(2, 64, WIDE)
     for t in range(TILES):
@@ -271,20 +271,27 @@
             ck, sk = c[k : k + 1], s[k : k + 1]
             real.append(ck * re + sk * im)
             imag.append(ck * im - sk * re)
-        shifted = jnp.concatenate(real + imag, axis=0).astype(BF16)
-        total += lax.dot_general(
-            shifted, interp_ref[:, at], (((1,), (1,)), ((), ())), preferred_element_type=F32
-        )
-    rows = by_box((total * (DC / DP)).astype(BF16))
-    out_ref[...] = rows.reshape(64, 2, DC)
+        shifted.append(jnp.concatenate(real + imag, axis=0).astype(BF16))
+    shifted = jnp.concatenate(shifted, axis=1)
+    stores = []
+    for n in range(2):
+        at = slice(n * DC // 2, (n + 1) * DC // 2)
+        total = lax.dot_general(shifted, interp_ref[at], (((1,), (1,)), ((), ())), preferred_element_type=F32)
+        out_ref[n] = by_box((total * (DC / DP)).astype(BF16)).reshape(64, 2, DC // 2)
+        there = out_hbm.at[:, :, pl.ds(n * DC // 2, DC // 2)]
+        stores.append(pltpu.make_async_copy(out_ref.at[n], there, sems.at[n]))
+        stores[n].start()
+    for store in stores:
+        store.wait()
 
 
 def anterpolate(received, interp, c, s):
     return pl.pallas_call(
         anterpolate_kernel,
         in_specs=[whole()] * 4,
-        out_specs=whole(),
+        out_specs=outer(),
         out_shape=jax.ShapeDtypeStruct((64, 2, DC), BF16),
+        scratch_shapes=[pltpu.VMEM((2, 64, 2, DC // 2), BF16), pltpu.SemaphoreType.DMA((2,))],
         compiler_params=params(),
     )(received, interp, c, s)
 

time: 55.3 us -> 55.9 us (1.011)
  Pallas kernels: 8.2 us -> 8.77 us
    pallas_call x1, Pallas kernels: 1.65 us -> 2.23 us  [anterpolate(): pl.pallas_call(anterpolate_kernel, in_specs=[whole()] * 4, out_specs=oute...]
where the time goes in v9:
time: 55.9 us; the launch traced here: 54.9 us
  starting transfers between devices  28.6 us (51%)
  blocking collectives  16 us (29%)
  Pallas kernels  8.77 us (16%)
  waiting for transfers between devices  1.43 us (3%)
    all_to_all x1, blocking collectives, per_device(): lax.all_to_all(returned.reshape(DBLOCKS, 8, WIDE), DIR + ('chip', 'core')...  16 us
    all_to_all x1, starting transfers between devices, per_device(): lax.all_to_all(send, DIR + ('chip', 'core'), 0, 0, axis_index_groups=neig...  10.1 us
    ppermute x1, starting transfers between devices, per_device(): lax.ppermute(operators, ('dir_1', 'chip', 'core'), other_half(chips))  9.75 us
    ppermute x1, starting transfers between devices, per_device(): edge = lax.ppermute(edge, 'core', [(0, 1), (1, 0)])  8.73 us
    pallas_call x1, Pallas kernels, translate(): pl.pallas_call(translate_kernel, in_specs=[whole()] * 7, out_specs=whole(...  3.41 us
    pallas_call x1, Pallas kernels, front(): pl.pallas_call(front_kernel, in_specs=[outer()] * 4, out_specs=[outer(),...  2.85 us
    pallas_call x1, Pallas kernels, anterpolate(): pl.pallas_call(anterpolate_kernel, in_specs=[whole()] * 4, out_specs=oute...  2.23 us
  transfers between devices with their start and end apart: 3, of which 2 were waited for; matrix products, arithmetic and copies ran while one was open for 0% of the time, Pallas kernels for 1%

profile of v9, /device:TPU:1, one launch (start us, length us, event | category | flops | bytes accessed | tf_op | source)
XLA Modules:
  0.0 54.9 jit_solution(12127845685569275233)
XLA Ops:
  0.0 0.0 copy-start.4
  0.0 0.0 copy-start
  0.0 0.0 copy-start.3
  0.0 0.0 copy-start.1
  0.0 0.0 copy-start.2
  0.0 2.9 %shard_map.73 = (bf16[16,8,640]{2,1,0:T(8,128)(2,1)}, f32[8,2048]{1,0:T(8,128)S(1)}, f32[8,2048]{1,0:T(8,128)S(1)}) custom-call(bf16[64,2,512]{2,1,0:T(2,128)(2,1)} %bitcast.12, s32[1,128]{1,0:T(1,128)} %order_ref.3, f32[8,2048]{1,0:T(8,128)} %phase_hbm.1, bf16[512,2048]{1,0:T(8,128)(2,1)} %interp_ref.1), custom_call_target="tpu_custom_call" | custom-call | flops 268435456 | bytes 2097152 | tf_op jit(solution)/shard_map/pallas_call | solution.py:127
  2.9 10.1 %all-to-all-start = ((bf16[16,8,640]{2,1,0:T(8,128)(2,1)}), bf16[16,8,640]{2,1,0:T(8,128)(2,1)S(1)}, u32[]{:S(2)}, u32[]{:S(2)}) async-start(bf16[16,8,640]{2,1,0:T(8,128)(2,1)} %get-tuple-element.10), calls=%async_computation | async-start | bytes 327680 | tf_op jit(solution)/shard_map/all_to_all | solution.py:327
  13.0 0.0 copy-done.3
  13.0 9.8 %collective-permute-start.1 = (bf16[128,2,128]{2,1,0:T(2,128)(2,1)S(1)}, bf16[128,2,128]{2,1,0:T(2,128)(2,1)S(1)}, u32[]{:S(2)}, u32[]{:S(2)}) collective-permute-start(bf16[128,2,128]{2,1,0:T(2,128)(2,1)S(1)} %copy-done.3), channel_id=1, source_target_pairs={{0,36},{1,37},{2,38},{3,39},{4,32},{5,33},{6,34},{7,35},{8,44},{9,... | collective-permute-start | bytes 196616 | tf_op jit(solution)/shard_map/ppermute | solution.py:325
  22.8 0.6 %all-to-all-done = bf16[16,8,640]{2,1,0:T(8,128)(2,1)S(1)} async-done(((bf16[16,8,640]{2,1,0:T(8,128)(2,1)}), bf16[16,8,640]{2,1,0:T(8,128)(2,1)S(1)}, u32[]{:S(2)}, u32[]{:S(2)}) %all-to-all-start) | async-done | bytes 163872 | tf_op jit(solution)/shard_map/all_to_all | solution.py:327
  23.4 0.0 copy-done.4
  23.4 0.3 shard_map.74
  23.7 8.7 %collective-permute-start = (bf16[48,512]{1,0:T(8,128)(2,1)S(1)}, bf16[48,512]{1,0:T(8,128)(2,1)S(1)}, u32[]{:S(2)}, u32[]{:S(2)}) collective-permute-start(bf16[48,512]{1,0:T(8,128)(2,1)S(1)} %get-tuple-element.12), channel_id=1, source_target_pairs={{0,1},{1,0},{2,3},{3,2},{4,5},{5,4},{6,7},{7,6},{8,9},{9,8},{10,11... | collective-permute-start | bytes 147464 | tf_op jit(solution)/shard_map/ppermute | solution.py:332
  32.4 0.0 collective-permute-done.1.other_ref
  32.4 0.8 %collective-permute-done.edge_ref = bf16[48,512]{1,0:T(8,128)(2,1)S(1)} collective-permute-done((bf16[48,512]{1,0:T(8,128)(2,1)S(1)}, bf16[48,512]{1,0:T(8,128)(2,1)S(1)}, u32[]{:S(2)}, u32[]{:S(2)}) %collective-permute-start) | collective-permute-done | bytes 49184 | tf_op jit(solution)/shard_map/ppermute | solution.py:332
  33.3 0.0 copy-done.1
  33.3 0.0 copy-done.2
  33.3 3.4 %shard_map.75 = bf16[128,512]{1,0:T(8,128)(2,1)S(1)} custom-call(bf16[256,512]{1,0:T(8,128)(2,1)S(1)} %get-tuple-element.11.sources_ref, bf16[48,512]{1,0:T(8,128)(2,1)S(1)} %collective-permute-done.edge_ref, s32[128,40]{1,0:T(8,128)S(1)} %bitcast.10, s32[128,40]{1,0:T(8,128)S(1)} %bitcast.11, bf16[128,2,128]{2,1,0:T(2,128)(2,1)S(1)} %copy-done.3, ...), custom_call_target="tpu_custom_call" | custom-call | tf_op jit(solution)/shard_map/pallas_call | solution.py:245
  36.7 16.0 %all_to_all.10 = bf16[16,8,512]{2,1,0:T(8,128)(2,1)S(1)} all-to-all(bf16[16,8,512]{2,1,0:T(8,128)(2,1)S(1)} %bitcast.9), channel_id=1, replica_groups={{0,64,128,192,256,320,384,448,32,96,160,224,288,352,416,480},{1,65,129,..., dimensions={0} | all-to-all | bytes 262144 | tf_op jit(solution)/shard_map/all_to_all | solution.py:334
  52.7 0.0 copy-done
  52.7 2.2 %shard_map.76 = bf16[64,2,512]{2,1,0:T(2,128)(2,1)} custom-call(bf16[128,512]{1,0:T(8,128)(2,1)S(1)} %bitcast.8, bf16[512,2048]{1,0:T(8,128)(2,1)S(1)} %copy-done, f32[8,2048]{1,0:T(8,128)S(1)} %get-tuple-element.13.cos_ref, f32[8,2048]{1,0:T(8,128)S(1)} %get-tuple-element.14.sin_ref), custom_call_target="tpu_custom_call" | custom-call | tf_op jit(solution)/shard_map/pallas_call | solution.py:289
Async XLA Ops:
  0.0 23.4 %copy-start.4 = (s32[1,128]{1,0:T(1,128)S(1)}, s32[1,128]{1,0:T(1,128)}, u32[]{:S(2)}) copy-start(s32[1,128]{1,0:T(1,128)} %order_ref.3) | copy-start | bytes 1540
  0.0 52.7 %copy-start = (bf16[512,2048]{1,0:T(8,128)(2,1)S(1)}, bf16[512,2048]{1,0:T(8,128)(2,1)}, u32[]{:S(2)}) copy-start(bf16[512,2048]{1,0:T(8,128)(2,1)} %interp_ref.1) | copy-start | bytes 6291460
  0.0 13.0 %copy-start.3 = (bf16[128,2,128]{2,1,0:T(2,128)(2,1)S(1)}, bf16[128,2,128]{2,1,0:T(2,128)(2,1)}, u32[]{:S(2)}) copy-start(bf16[128,2,128]{2,1,0:T(2,128)(2,1)} %own_ref.1) | copy-start | bytes 196612
  0.0 33.3 %copy-start.1 = (s32[8,16,40]{2,1,0:T(8,128)S(1)}, s32[8,16,40]{2,1,0:T(8,128)}, u32[]{:S(2)}) copy-start(s32[8,16,40]{2,1,0:T(8,128)} %param.11) | copy-start | bytes 61444
  0.0 33.3 %copy-start.2 = (s32[8,16,40]{2,1,0:T(8,128)S(1)}, s32[8,16,40]{2,1,0:T(8,128)}, u32[]{:S(2)}) copy-start(s32[8,16,40]{2,1,0:T(8,128)} %param.12) | copy-start | bytes 61444
  2.9 20.5 %all-to-all-start = ((bf16[16,8,640]{2,1,0:T(8,128)(2,1)}), bf16[16,8,640]{2,1,0:T(8,128)(2,1)S(1)}, u32[]{:S(2)}, u32[]{:S(2)}) async-start(bf16[16,8,640]{2,1,0:T(8,128)(2,1)} %get-tuple-element.10), calls=%async_computation | async-start | bytes 327680 | tf_op jit(solution)/shard_map/all_to_all | solution.py:327
  13.0 19.4 %collective-permute-start.1 = (bf16[128,2,128]{2,1,0:T(2,128)(2,1)S(1)}, bf16[128,2,128]{2,1,0:T(2,128)(2,1)S(1)}, u32[]{:S(2)}, u32[]{:S(2)}) collective-permute-start(bf16[128,2,128]{2,1,0:T(2,128)(2,1)S(1)} %copy-done.3), channel_id=1, source_target_pairs={{0,36},{1,37},{2,38},{3,39},{4,32},{5,33},{6,34},{7,35},{8,44},{9,... | collective-permute-start | bytes 196616 | tf_op jit(solution)/shard_map/ppermute | solution.py:325
  23.7 9.6 %collective-permute-start = (bf16[48,512]{1,0:T(8,128)(2,1)S(1)}, bf16[48,512]{1,0:T(8,128)(2,1)S(1)}, u32[]{:S(2)}, u32[]{:S(2)}) collective-permute-start(bf16[48,512]{1,0:T(8,128)(2,1)S(1)} %get-tuple-element.12), channel_id=1, source_target_pairs={{0,1},{1,0},{2,3},{3,2},{4,5},{5,4},{6,7},{7,6},{8,9},{9,8},{10,11... | collective-permute-start | bytes 147464 | tf_op jit(solution)/shard_map/ppermute | solution.py:332

commit v10 on v8

--- a/solution.py
+++ b/solution.py
@@ -19,7 +19,7 @@
 HALO = 48
 WIDE = 4 * BAND
 RUN = 4
-TILE = 512
+TILE = 1024
 TILES = DP // TILE
 FRONT_TILE = 1024
 FRONT_TILES = DP // FRONT_TILE

time: 55.3 us -> 55.3 us (level)
  no operation moved by 1% of the time
where the time goes in v10:
time: 55.3 us; the launch traced here: 54.3 us
  starting transfers between devices  28.6 us (52%)
  blocking collectives  16 us (29%)
  Pallas kernels  8.2 us (15%)
  waiting for transfers between devices  1.43 us (3%)
    all_to_all x1, blocking collectives, per_device(): lax.all_to_all(returned.reshape(DBLOCKS, 8, WIDE), DIR + ('chip', 'core')...  16 us
    all_to_all x1, starting transfers between devices, per_device(): lax.all_to_all(send, DIR + ('chip', 'core'), 0, 0, axis_index_groups=neig...  10.1 us
    ppermute x1, starting transfers between devices, per_device(): lax.ppermute(operators, ('dir_1', 'chip', 'core'), other_half(chips))  9.75 us
    ppermute x1, starting transfers between devices, per_device(): edge = lax.ppermute(edge, 'core', [(0, 1), (1, 0)])  8.73 us
    pallas_call x1, Pallas kernels, translate(): pl.pallas_call(translate_kernel, in_specs=[whole()] * 7, out_specs=whole(...  3.41 us
    pallas_call x1, Pallas kernels, front(): pl.pallas_call(front_kernel, in_specs=[outer()] * 4, out_specs=[outer(),...  2.85 us
    pallas_call x1, Pallas kernels, anterpolate(): pl.pallas_call(anterpolate_kernel, in_specs=[whole()] * 4, out_specs=whol...  1.65 us
  transfers between devices with their start and end apart: 3, of which 2 were waited for; matrix products, arithmetic and copies ran while one was open for 0% of the time, Pallas kernels for 1%

profile of v10, /device:TPU:1, one launch (start us, length us, event | category | flops | bytes accessed | tf_op | source)
XLA Modules:
  0.0 54.3 jit_solution(8865630784426526581)
XLA Ops:
  0.0 0.0 copy-start.4
  0.0 0.0 copy-start
  0.0 0.0 copy-start.3
  0.0 0.0 copy-start.1
  0.0 0.0 copy-start.2
  0.0 2.9 %shard_map.73 = (bf16[16,8,640]{2,1,0:T(8,128)(2,1)}, f32[8,2048]{1,0:T(8,128)S(1)}, f32[8,2048]{1,0:T(8,128)S(1)}) custom-call(bf16[64,2,512]{2,1,0:T(2,128)(2,1)} %bitcast.12, s32[1,128]{1,0:T(1,128)} %order_ref.3, f32[8,2048]{1,0:T(8,128)} %phase_hbm.1, bf16[512,2048]{1,0:T(8,128)(2,1)} %interp_ref.1), custom_call_target="tpu_custom_call" | custom-call | flops 268435456 | bytes 2097152 | tf_op jit(solution)/shard_map/pallas_call | solution.py:127
  2.9 10.1 %all-to-all-start = ((bf16[16,8,640]{2,1,0:T(8,128)(2,1)}), bf16[16,8,640]{2,1,0:T(8,128)(2,1)S(1)}, u32[]{:S(2)}, u32[]{:S(2)}) async-start(bf16[16,8,640]{2,1,0:T(8,128)(2,1)} %get-tuple-element.10), calls=%async_computation | async-start | bytes 327680 | tf_op jit(solution)/shard_map/all_to_all | solution.py:320
  13.0 0.0 copy-done.3
  13.0 9.8 %collective-permute-start.1 = (bf16[128,2,128]{2,1,0:T(2,128)(2,1)S(1)}, bf16[128,2,128]{2,1,0:T(2,128)(2,1)S(1)}, u32[]{:S(2)}, u32[]{:S(2)}) collective-permute-start(bf16[128,2,128]{2,1,0:T(2,128)(2,1)S(1)} %copy-done.3), channel_id=1, source_target_pairs={{0,36},{1,37},{2,38},{3,39},{4,32},{5,33},{6,34},{7,35},{8,44},{9,... | collective-permute-start | bytes 196616 | tf_op jit(solution)/shard_map/ppermute | solution.py:318
  22.8 0.6 %all-to-all-done = bf16[16,8,640]{2,1,0:T(8,128)(2,1)S(1)} async-done(((bf16[16,8,640]{2,1,0:T(8,128)(2,1)}), bf16[16,8,640]{2,1,0:T(8,128)(2,1)S(1)}, u32[]{:S(2)}, u32[]{:S(2)}) %all-to-all-start) | async-done | bytes 163872 | tf_op jit(solution)/shard_map/all_to_all | solution.py:320
  23.4 0.0 copy-done.4
  23.4 0.3 shard_map.74
  23.7 8.7 %collective-permute-start = (bf16[48,512]{1,0:T(8,128)(2,1)S(1)}, bf16[48,512]{1,0:T(8,128)(2,1)S(1)}, u32[]{:S(2)}, u32[]{:S(2)}) collective-permute-start(bf16[48,512]{1,0:T(8,128)(2,1)S(1)} %get-tuple-element.12), channel_id=1, source_target_pairs={{0,1},{1,0},{2,3},{3,2},{4,5},{5,4},{6,7},{7,6},{8,9},{9,8},{10,11... | collective-permute-start | bytes 147464 | tf_op jit(solution)/shard_map/ppermute | solution.py:325
  32.4 0.0 collective-permute-done.1.other_ref
  32.4 0.8 %collective-permute-done.edge_ref = bf16[48,512]{1,0:T(8,128)(2,1)S(1)} collective-permute-done((bf16[48,512]{1,0:T(8,128)(2,1)S(1)}, bf16[48,512]{1,0:T(8,128)(2,1)S(1)}, u32[]{:S(2)}, u32[]{:S(2)}) %collective-permute-start) | collective-permute-done | bytes 49184 | tf_op jit(solution)/shard_map/ppermute | solution.py:325
  33.3 0.0 copy-done.1
  33.3 0.0 copy-done.2
  33.3 3.4 %shard_map.75 = bf16[128,512]{1,0:T(8,128)(2,1)S(1)} custom-call(bf16[256,512]{1,0:T(8,128)(2,1)S(1)} %get-tuple-element.11.sources_ref, bf16[48,512]{1,0:T(8,128)(2,1)S(1)} %collective-permute-done.edge_ref, s32[128,40]{1,0:T(8,128)S(1)} %bitcast.10, s32[128,40]{1,0:T(8,128)S(1)} %bitcast.11, bf16[128,2,128]{2,1,0:T(2,128)(2,1)S(1)} %copy-done.3, ...), custom_call_target="tpu_custom_call" | custom-call | tf_op jit(solution)/shard_map/pallas_call | solution.py:245
  36.7 16.0 %all_to_all.10 = bf16[16,8,512]{2,1,0:T(8,128)(2,1)S(1)} all-to-all(bf16[16,8,512]{2,1,0:T(8,128)(2,1)S(1)} %bitcast.9), channel_id=1, replica_groups={{0,64,128,192,256,320,384,448,32,96,160,224,288,352,416,480},{1,65,129,..., dimensions={0} | all-to-all | bytes 262144 | tf_op jit(solution)/shard_map/all_to_all | solution.py:327
  52.7 0.0 copy-done
  52.7 1.7 %shard_map.76 = bf16[64,2,512]{2,1,0:T(2,128)(2,1)} custom-call(bf16[128,512]{1,0:T(8,128)(2,1)S(1)} %bitcast.8, bf16[512,2048]{1,0:T(8,128)(2,1)S(1)} %copy-done, f32[8,2048]{1,0:T(8,128)S(1)} %get-tuple-element.13.cos_ref, f32[8,2048]{1,0:T(8,128)S(1)} %get-tuple-element.14.sin_ref), custom_call_target="tpu_custom_call" | custom-call | tf_op jit(solution)/shard_map/pallas_call | solution.py:283
Async XLA Ops:
  0.0 23.4 %copy-start.4 = (s32[1,128]{1,0:T(1,128)S(1)}, s32[1,128]{1,0:T(1,128)}, u32[]{:S(2)}) copy-start(s32[1,128]{1,0:T(1,128)} %order_ref.3) | copy-start | bytes 1540
  0.0 52.7 %copy-start = (bf16[512,2048]{1,0:T(8,128)(2,1)S(1)}, bf16[512,2048]{1,0:T(8,128)(2,1)}, u32[]{:S(2)}) copy-start(bf16[512,2048]{1,0:T(8,128)(2,1)} %interp_ref.1) | copy-start | bytes 6291460
  0.0 13.0 %copy-start.3 = (bf16[128,2,128]{2,1,0:T(2,128)(2,1)S(1)}, bf16[128,2,128]{2,1,0:T(2,128)(2,1)}, u32[]{:S(2)}) copy-start(bf16[128,2,128]{2,1,0:T(2,128)(2,1)} %own_ref.1) | copy-start | bytes 196612
  0.0 33.3 %copy-start.1 = (s32[8,16,40]{2,1,0:T(8,128)S(1)}, s32[8,16,40]{2,1,0:T(8,128)}, u32[]{:S(2)}) copy-start(s32[8,16,40]{2,1,0:T(8,128)} %param.11) | copy-start | bytes 61444
  0.0 33.3 %copy-start.2 = (s32[8,16,40]{2,1,0:T(8,128)S(1)}, s32[8,16,40]{2,1,0:T(8,128)}, u32[]{:S(2)}) copy-start(s32[8,16,40]{2,1,0:T(8,128)} %param.12) | copy-start | bytes 61444
  2.9 20.5 %all-to-all-start = ((bf16[16,8,640]{2,1,0:T(8,128)(2,1)}), bf16[16,8,640]{2,1,0:T(8,128)(2,1)S(1)}, u32[]{:S(2)}, u32[]{:S(2)}) async-start(bf16[16,8,640]{2,1,0:T(8,128)(2,1)} %get-tuple-element.10), calls=%async_computation | async-start | bytes 327680 | tf_op jit(solution)/shard_map/all_to_all | solution.py:320
  13.0 19.4 %collective-permute-start.1 = (bf16[128,2,128]{2,1,0:T(2,128)(2,1)S(1)}, bf16[128,2,128]{2,1,0:T(2,128)(2,1)S(1)}, u32[]{:S(2)}, u32[]{:S(2)}) collective-permute-start(bf16[128,2,128]{2,1,0:T(2,128)(2,1)S(1)} %copy-done.3), channel_id=1, source_target_pairs={{0,36},{1,37},{2,38},{3,39},{4,32},{5,33},{6,34},{7,35},{8,44},{9,... | collective-permute-start | bytes 196616 | tf_op jit(solution)/shard_map/ppermute | solution.py:318
  23.7 9.6 %collective-permute-start = (bf16[48,512]{1,0:T(8,128)(2,1)S(1)}, bf16[48,512]{1,0:T(8,128)(2,1)S(1)}, u32[]{:S(2)}, u32[]{:S(2)}) collective-permute-start(bf16[48,512]{1,0:T(8,128)(2,1)S(1)} %get-tuple-element.12), channel_id=1, source_target_pairs={{0,1},{1,0},{2,3},{3,2},{4,5},{5,4},{6,7},{7,6},{8,9},{9,8},{10,11... | collective-permute-start | bytes 147464 | tf_op jit(solution)/shard_map/ppermute | solution.py:325
